TPU v7x, 128 devices: a whole 4x4x4 slice. The times are simulated.
128 devices in a mesh: dp: 16 (over z_lo, y, core), seq: 8 (over x, z_hi).
Axes of the slice: x: 4, y: 4, z: 4 (z_hi: 2, z_lo: 2; z = z_hi * 2 + z_lo), core: 2. Of those that a mesh axis runs over, the one named last changes fastest.
Arguments:
- x_in: bfloat16 [32, 1024, 1024], P('dp', 'seq'), may hold values from -6 to 6
- scale_ids: int32 [32, 1024], P('dp', 'seq'), may hold values from 0 to 8, as said below
- pad_mask: int32 [32, 1024], P('dp', 'seq'), may hold values from 0 to 1, as said below
- loss_weights: int32 [32, 1024], P('dp', 'seq'), may hold values from 1 to 3
- targets: int32 [32, 1024], P('dp', 'seq'), may hold values from 0 to 4095
- labels: int32 [32], P('dp'), may hold values from 0 to 999
- cond_w: float32 [1024, 8192], P(None, 'dp'), may hold values from -0.1875 to 0.1875
- attn_w: float32 [1024, 4096], P(None, 'dp')
- mlp_w: float32 [2, 1024, 4096], P(None, None, 'dp'), may hold values from -0.1875 to 0.1875
- head_w: float32 [1024, 4096], P(None, 'dp')
- class_table: float32 [1000, 1024], P(None, 'dp'), may hold values from -6 to 6
- biases: float32 [20480], P('dp'), may hold values from -0.3 to 0.3
- first_cond: float32 [1024, 8192], P(None, 'dp'), may hold values from -1.1444092e-05 to 1.1444092e-05
- first_attn: float32 [1024, 4096], P(None, 'dp'), may hold values from -1.1444092e-05 to 1.1444092e-05
- first_mlp: float32 [2, 1024, 4096], P(None, None, 'dp'), may hold values from -1.1444092e-05 to 1.1444092e-05
- first_head: float32 [1024, 4096], P(None, 'dp'), may hold values from -1.1444092e-05 to 1.1444092e-05
- first_table: float32 [1000, 1024], P(None, 'dp'), may hold values from -1.1444092e-05 to 1.1444092e-05
- first_bias: float32 [20480], P('dp'), may hold values from -3.0517578e-05 to 3.0517578e-05
- second_cond: float32 [1024, 8192], P(None, 'dp'), may hold values from 3.818277e-12 to 1.5273107e-11
- second_attn: float32 [1024, 4096], P(None, 'dp'), may hold values from 3.818277e-12 to 1.5273107e-11
- second_mlp: float32 [2, 1024, 4096], P(None, None, 'dp'), may hold values from 3.818277e-12 to 1.5273107e-11
- second_head: float32 [1024, 4096], P(None, 'dp'), may hold values from 3.818277e-12 to 1.5273107e-11
- second_table: float32 [1000, 1024], P(None, 'dp'), may hold values from 3.818277e-12 to 1.5273107e-11
- second_bias: float32 [20480], P('dp'), may hold values from 3.436449e-11 to 1.3745796e-10
Outputs:
- updated_cond: float32 [1024, 8192], P(None, 'dp')
- updated_attn: float32 [1024, 4096], P(None, 'dp')
- updated_mlp: float32 [2, 1024, 4096], P(None, None, 'dp')
- updated_head: float32 [1024, 4096], P(None, 'dp')
- updated_table: float32 [1000, 1024], P(None, 'dp')
- updated_bias: float32 [20480], P('dp')
- moment_cond: float32 [1024, 8192], P(None, 'dp')
- moment_attn: float32 [1024, 4096], P(None, 'dp')
- moment_mlp: float32 [2, 1024, 4096], P(None, None, 'dp')
- moment_head: float32 [1024, 4096], P(None, 'dp')
- moment_table: float32 [1000, 1024], P(None, 'dp')
- moment_bias: float32 [20480], P('dp')
- square_cond: float32 [1024, 8192], P(None, 'dp')
- square_attn: float32 [1024, 4096], P(None, 'dp')
- square_mlp: float32 [2, 1024, 4096], P(None, None, 'dp')
- square_head: float32 [1024, 4096], P(None, 'dp')
- square_table: float32 [1000, 1024], P(None, 'dp')
- square_bias: float32 [20480], P('dp')
- copy_cond: bfloat16 [1024, 8192], P(None, 'dp')
- copy_attn: bfloat16 [1024, 4096], P(None, 'dp')
- copy_mlp: bfloat16 [2, 1024, 4096], P(None, None, 'dp')
- copy_head: bfloat16 [1024, 4096], P(None, 'dp')
- copy_table: bfloat16 [1000, 1024], P(None, 'dp')
- copy_bias: bfloat16 [20480], P('dp')
- grad_norm: float32 [], replicated
- loss_sum: float32 [], replicated
- true_count: float32 [], replicated
Inputs may be any that keep to these rules, and one draw needn't show every extreme that they name: `scale_ids`: along each image the ids never fall; slot 0 of each image is real and has id 0. `pad_mask`: in each aligned block of 128 slots of an image the real slots come first, 64 of them or more; the last block of each image is full.
All inputs are finite; a program needn't handle non-finite values.
Results may differ from a plain program's by a relative error of at most 0.002.
The roundings to bfloat16 on the way count: a program that leaves them out, or rounds other values in their place, can miss the bound.
Values may be sent and summed in bfloat16 or wider, within the bound.
A program may use at most 320 MiB of HBM per device.

v0:
```python
from functools import partial

import jax
import jax.numpy as jnp
from jax import lax
from jax.sharding import PartitionSpec as P

HEAD_DIM = 64
STEP = 5


HIGH = lax.Precision.HIGHEST
NORM_EPS = 1e-06
CLIP = 0.01
LEARN = 0.02
DECAY = 0.1
BETA_ONE = 0.5
BETA_TWO = 0.5
ADAM_EPS = 1e-08
SCORE_SCALE = 0.125


def layer_norm(values):
    center = values - jnp.mean(values, -1, keepdims=True)
    spread = jnp.mean(center * center, -1, keepdims=True)
    return center * lax.rsqrt(spread + NORM_EPS)


def modulate(values, scale_row, shift_row):
    return layer_norm(values) * (1.0 + scale_row) + shift_row


def modulate_back(values, scale_row, shift_row, grad_out):
    _, pull_back = jax.vjp(modulate, values, scale_row, shift_row)
    return pull_back(grad_out)


def bias_parts(bias_all, model_width, hidden):
    offsets = [
        8 * model_width,
        9 * model_width,
        10 * model_width,
        11 * model_width,
        11 * model_width + hidden,
        12 * model_width + hidden,
    ]
    return jnp.split(bias_all, offsets)


def outer_sum(left, right):
    return lax.dot_general(
        left, right, (((0,), (0,)), ((), ())), preferred_element_type=jnp.float32
    )


def right_transposed(left, matrix):
    return lax.dot_general(
        left, matrix, (((2,), (1,)), ((), ())), preferred_element_type=jnp.float32
    )


def attend(queries, key_rows, key_level, scale_query):
    scores = (
        jnp.einsum("ishe,ikhe->ihsk", queries, key_rows, preferred_element_type=jnp.float32)
        * SCORE_SCALE
    )
    visible = key_level.astype(jnp.float32)[:, None, None, :] <= scale_query[:, None, :, None]
    return jax.nn.softmax(jnp.where(visible, scores, -1e30), axis=-1)


def forward_layer(
    tokens, scale_query, level_own, ada_parts, attn_full, mlp_full, head_full, bias_set
):
    images, slots, model_width = tokens.shape
    head_count = model_width // HEAD_DIM
    gate_attn, gate_mlp, scale_attn, scale_mlp, shift_attn, shift_mlp, scale_head, shift_head = (
        ada_parts
    )
    bias_q, bias_v, bias_proj, bias_fc1, bias_fc2, bias_head = bias_set
    normed = modulate(tokens, scale_attn, shift_attn).astype(jnp.bfloat16)
    bias_qkv = jnp.concatenate([bias_q, jnp.zeros_like(bias_q), bias_v])
    qkv_all = (
        jnp.dot(normed, attn_full[:, : 3 * model_width], preferred_element_type=jnp.float32)
        + bias_qkv
    ).astype(jnp.bfloat16)
    queries, key_own, value_own = jnp.split(qkv_all, 3, axis=2)
    key_all, value_all, level_all = (
        lax.all_gather(key_own, "seq", axis=1, tiled=True),
        lax.all_gather(value_own, "seq", axis=1, tiled=True),
        lax.all_gather(level_own, "seq", axis=1, tiled=True),
    )
    probs = attend(
        queries.reshape(images, slots, head_count, HEAD_DIM),
        key_all.reshape(images, -1, head_count, HEAD_DIM),
        level_all,
        scale_query,
    )
    mixed_out = jnp.einsum(
        "ihsk,ikhe->ishe",
        probs.astype(jnp.bfloat16),
        value_all.reshape(images, -1, head_count, HEAD_DIM),
        preferred_element_type=jnp.float32,
    )
    mixed_out = mixed_out.reshape(images, slots, model_width).astype(jnp.bfloat16)
    branch = (
        jnp.dot(mixed_out, attn_full[:, 3 * model_width :], preferred_element_type=jnp.float32)
        + bias_proj
    )
    after_attn = tokens + gate_attn * branch
    normed_two = modulate(after_attn, scale_mlp, shift_mlp).astype(jnp.bfloat16)
    pre_act = jnp.dot(normed_two, mlp_full[0], preferred_element_type=jnp.float32) + bias_fc1
    activated = jax.nn.gelu(pre_act, approximate=True).astype(jnp.bfloat16)
    mlp_out = right_transposed(activated, mlp_full[1]) + bias_fc2
    after_mlp = after_attn + gate_mlp * mlp_out
    normed_head = modulate(after_mlp, scale_head, shift_head).astype(jnp.bfloat16)
    logits = jnp.dot(normed_head, head_full, preferred_element_type=jnp.float32) + bias_head
    return (
        tokens,
        scale_query,
        normed,
        queries,
        key_all,
        value_all,
        level_all,
        mixed_out,
        branch,
        after_attn,
        normed_two,
        pre_act,
        activated,
        mlp_out,
        after_mlp,
        normed_head,
        logits,
    )


def backward_layer(saved, grad_logits, ada_parts, attn_full, mlp_full, head_full):
    (
        tokens,
        scale_query,
        normed,
        queries,
        key_all,
        value_all,
        level_all,
        mixed_out,
        branch,
        after_attn,
        normed_two,
        pre_act,
        activated,
        mlp_out,
        after_mlp,
        normed_head,
    ) = saved
    gate_attn, gate_mlp, scale_attn, scale_mlp, shift_attn, shift_mlp, scale_head, shift_head = (
        ada_parts
    )
    images, slots, model_width = tokens.shape
    head_count = model_width // HEAD_DIM
    rows = images * slots
    grad_head = outer_sum(normed_head.reshape(rows, model_width), grad_logits.reshape(rows, -1))
    grad_bias_head = jnp.sum(grad_logits.astype(jnp.float32), axis=(0, 1))
    grad_normed_head = right_transposed(grad_logits, head_full)
    grad_mlp_res, grad_scale_head, grad_shift_head = modulate_back(
        after_mlp, scale_head, shift_head, grad_normed_head
    )
    grad_gate_mlp = jnp.sum(grad_mlp_res * mlp_out, axis=1, keepdims=True)
    grad_mlp_out = (gate_mlp * grad_mlp_res).astype(jnp.bfloat16)
    grad_second = outer_sum(grad_mlp_out.reshape(rows, model_width), activated.reshape(rows, -1))
    grad_bias_fc2 = jnp.sum(grad_mlp_out.astype(jnp.float32), axis=(0, 1))
    grad_activated = jnp.dot(grad_mlp_out, mlp_full[1], preferred_element_type=jnp.float32)
    _, gelu_back = jax.vjp(partial(jax.nn.gelu, approximate=True), pre_act)
    grad_pre = gelu_back(grad_activated)[0].astype(jnp.bfloat16)
    grad_first = outer_sum(normed_two.reshape(rows, model_width), grad_pre.reshape(rows, -1))
    grad_bias_fc1 = jnp.sum(grad_pre.astype(jnp.float32), axis=(0, 1))
    grad_normed_two = right_transposed(grad_pre, mlp_full[0])
    grad_attn_res, grad_scale_mlp, grad_shift_mlp = modulate_back(
        after_attn, scale_mlp, shift_mlp, grad_normed_two
    )
    grad_attn_res = grad_attn_res + grad_mlp_res
    grad_gate_attn = jnp.sum(grad_attn_res * branch, axis=1, keepdims=True)
    grad_branch = (gate_attn * grad_attn_res).astype(jnp.bfloat16)
    grad_proj = outer_sum(
        mixed_out.reshape(rows, model_width), grad_branch.reshape(rows, model_width)
    )
    grad_bias_proj = jnp.sum(grad_branch.astype(jnp.float32), axis=(0, 1))
    grad_mixed = right_transposed(grad_branch, attn_full[:, 3 * model_width :]).astype(jnp.bfloat16)
    query_four = queries.reshape(images, slots, head_count, HEAD_DIM)
    key_four = key_all.reshape(images, -1, head_count, HEAD_DIM)
    value_four = value_all.reshape(images, -1, head_count, HEAD_DIM)
    grad_four = grad_mixed.reshape(images, slots, head_count, HEAD_DIM)
    probs = attend(query_four, key_four, level_all, scale_query)
    grad_probs = jnp.einsum(
        "ishe,ikhe->ihsk", grad_four, value_four, preferred_element_type=jnp.float32
    )
    inner = jnp.sum(probs * grad_probs, axis=-1, keepdims=True)
    grad_scores = (probs * (grad_probs - inner)).astype(jnp.bfloat16)
    grad_query = (
        jnp.einsum("ihsk,ikhe->ishe", grad_scores, key_four, preferred_element_type=jnp.float32)
        * SCORE_SCALE
    )
    key_term = (
        jnp.einsum("ihsk,ishe->ikhe", grad_scores, query_four, preferred_element_type=jnp.float32)
        * SCORE_SCALE
    )
    value_term = jnp.einsum(
        "ihsk,ishe->ikhe", probs.astype(jnp.bfloat16), grad_four, preferred_element_type=jnp.float32
    )
    grad_key, grad_value = (
        lax.psum_scatter(
            key_term.reshape(images, -1, model_width), "seq", scatter_dimension=1, tiled=True
        ),
        lax.psum_scatter(
            value_term.reshape(images, -1, model_width), "seq", scatter_dimension=1, tiled=True
        ),
    )
    grad_qkv = jnp.concatenate(
        [grad_query.reshape(images, slots, model_width), grad_key, grad_value], axis=2
    ).astype(jnp.bfloat16)
    grad_qkv_w = outer_sum(normed.reshape(rows, model_width), grad_qkv.reshape(rows, -1))
    grad_bias_q = jnp.sum(grad_qkv[:, :, :model_width].astype(jnp.float32), axis=(0, 1))
    grad_bias_v = jnp.sum(grad_qkv[:, :, 2 * model_width :].astype(jnp.float32), axis=(0, 1))
    grad_normed = right_transposed(grad_qkv, attn_full[:, : 3 * model_width])
    _, grad_scale_attn, grad_shift_attn = modulate_back(tokens, scale_attn, shift_attn, grad_normed)
    grad_ada = jnp.concatenate(
        [
            piece[:, 0, :]
            for piece in (
                grad_gate_attn,
                grad_gate_mlp,
                grad_scale_attn,
                grad_scale_mlp,
                grad_shift_attn,
                grad_shift_mlp,
                grad_scale_head,
                grad_shift_head,
            )
        ],
        axis=1,
    )
    grad_attn = jnp.concatenate([grad_qkv_w, grad_proj], axis=1)
    grad_mlp = jnp.stack([grad_first, grad_second])
    bias_grads = (
        grad_bias_q,
        grad_bias_v,
        grad_bias_proj,
        grad_bias_fc1,
        grad_bias_fc2,
        grad_bias_head,
    )
    return (grad_ada, grad_attn, grad_mlp, grad_head, bias_grads)


def square_total(members):
    return sum((jnp.sum(member * member) for member in members))


def adamw(weight, first, second, grad, factor):
    clipped = grad * factor
    first_new = BETA_ONE * first + (1.0 - BETA_ONE) * clipped
    second_new = BETA_TWO * second + (1.0 - BETA_TWO) * clipped * clipped
    first_hat = first_new / (1.0 - BETA_ONE**STEP)
    second_hat = second_new / (1.0 - BETA_TWO**STEP)
    weight_new = weight - LEARN * (first_hat / (jnp.sqrt(second_hat) + ADAM_EPS) + DECAY * weight)
    return (weight_new, first_new, second_new)


def local(
    x_in,
    scale_ids,
    pad_mask,
    loss_weights,
    targets,
    labels,
    cond_w,
    attn_w,
    mlp_w,
    head_w,
    class_table,
    biases,
    first_cond,
    first_attn,
    first_mlp,
    first_head,
    first_table,
    first_bias,
    second_cond,
    second_attn,
    second_mlp,
    second_head,
    second_table,
    second_bias,
):
    cond_full, attn_full, mlp_full, head_full, table_full, bias_full = (
        lax.all_gather(cond_w.astype(jnp.bfloat16), "dp", axis=1, tiled=True),
        lax.all_gather(attn_w.astype(jnp.bfloat16), "dp", axis=1, tiled=True),
        lax.all_gather(mlp_w.astype(jnp.bfloat16), "dp", axis=2, tiled=True),
        lax.all_gather(head_w.astype(jnp.bfloat16), "dp", axis=1, tiled=True),
        lax.all_gather(class_table.astype(jnp.bfloat16), "dp", axis=1, tiled=True),
        lax.all_gather(biases.astype(jnp.bfloat16), "dp", axis=0, tiled=True),
    )
    model_width = x_in.shape[2]
    hidden = mlp_full.shape[2]
    is_real = pad_mask.astype(jnp.float32)
    weight_tok = (loss_weights * pad_mask).astype(jnp.float32)
    true_count = lax.psum(jnp.sum(is_real), ("dp", "seq"))
    bias_set = bias_parts(bias_full.astype(jnp.float32), model_width, hidden)
    class_hit = labels[:, None] == jnp.arange(table_full.shape[0])[None, :]
    embedded = jnp.dot(
        class_hit.astype(jnp.bfloat16), table_full, preferred_element_type=jnp.float32
    )
    condition = jax.nn.silu(embedded).astype(jnp.bfloat16)
    ada_rows = jnp.dot(condition, cond_full, preferred_element_type=jnp.float32) + bias_set[0]
    ada_parts = tuple((piece[:, None, :] for piece in jnp.split(ada_rows, 8, axis=1)))
    level_own = jnp.where(pad_mask > 0, scale_ids, 1000).astype(jnp.bfloat16)
    saved = forward_layer(
        x_in.astype(jnp.float32),
        scale_ids.astype(jnp.float32),
        level_own,
        ada_parts,
        attn_full,
        mlp_full,
        head_full,
        bias_set[1:],
    )
    logits = saved[-1]
    log_total = jax.nn.logsumexp(logits, axis=2)
    target_hit = targets[:, :, None] == jnp.arange(logits.shape[2])[None, None, :]
    picked = jnp.sum(jnp.where(target_hit, logits, 0.0), axis=2)
    loss_local = jnp.sum(weight_tok * (log_total - picked))
    grad_logits = (
        (weight_tok / true_count)[:, :, None]
        * (jnp.exp(logits - log_total[:, :, None]) - target_hit.astype(jnp.float32))
    ).astype(jnp.bfloat16)
    grad_ada, grad_attn, grad_mlp, grad_head, bias_grads = backward_layer(
        saved[:-1], grad_logits, ada_parts, attn_full, mlp_full, head_full
    )
    grad_cond = lax.dot_general(
        condition.astype(jnp.float32), grad_ada, (((0,), (0,)), ((), ())), precision=HIGH
    )
    grad_condition = lax.dot_general(
        grad_ada, cond_full.astype(jnp.float32), (((1,), (1,)), ((), ())), precision=HIGH
    )
    _, silu_back = jax.vjp(jax.nn.silu, embedded)
    grad_embedded = silu_back(grad_condition)[0]
    grad_table = lax.dot_general(
        class_hit.astype(jnp.float32), grad_embedded, (((0,), (0,)), ((), ())), precision=HIGH
    )
    grad_bias = jnp.concatenate([jnp.sum(grad_ada, axis=0)] + list(bias_grads))
    sum_cond, sum_attn, sum_mlp, sum_head, sum_table, sum_bias = lax.psum(
        (grad_cond, grad_attn, grad_mlp, grad_head, grad_table, grad_bias), "seq"
    )
    shards = (
        lax.psum_scatter(sum_cond, "dp", scatter_dimension=1, tiled=True),
        lax.psum_scatter(sum_attn, "dp", scatter_dimension=1, tiled=True),
        lax.psum_scatter(sum_mlp, "dp", scatter_dimension=2, tiled=True),
        lax.psum_scatter(sum_head, "dp", scatter_dimension=1, tiled=True),
        lax.psum_scatter(sum_table, "dp", scatter_dimension=1, tiled=True),
        lax.psum_scatter(sum_bias, "dp", scatter_dimension=0, tiled=True),
    )
    local_squares = square_total(shards) / lax.axis_size("seq")
    loss_total, square_sum = lax.psum((loss_local, local_squares), ("dp", "seq"))
    grad_norm = jnp.sqrt(square_sum)
    factor = jnp.minimum(1.0, CLIP / grad_norm)
    params = (cond_w, attn_w, mlp_w, head_w, class_table, biases)
    firsts = (first_cond, first_attn, first_mlp, first_head, first_table, first_bias)
    seconds = (second_cond, second_attn, second_mlp, second_head, second_table, second_bias)
    results = [
        adamw(param, first, second, grad, factor)
        for param, first, second, grad in zip(params, firsts, seconds, shards)
    ]
    new_weights = [entry[0] for entry in results]
    new_first = [entry[1] for entry in results]
    new_second = [entry[2] for entry in results]
    copies = [weight.astype(jnp.bfloat16) for weight in new_weights]
    return tuple(
        new_weights + new_first + new_second + copies + [grad_norm, loss_total, true_count]
    )


def solution(mesh):
    in_specs = (
        P("dp", "seq", None),
        P("dp", "seq"),
        P("dp", "seq"),
        P("dp", "seq"),
        P("dp", "seq"),
        P("dp"),
        P(None, "dp"),
        P(None, "dp"),
        P(None, None, "dp"),
        P(None, "dp"),
        P(None, "dp"),
        P("dp"),
        P(None, "dp"),
        P(None, "dp"),
        P(None, None, "dp"),
        P(None, "dp"),
        P(None, "dp"),
        P("dp"),
        P(None, "dp"),
        P(None, "dp"),
        P(None, None, "dp"),
        P(None, "dp"),
        P(None, "dp"),
        P("dp"),
    )
    out_specs = (
        P(None, "dp"),
        P(None, "dp"),
        P(None, None, "dp"),
        P(None, "dp"),
        P(None, "dp"),
        P("dp"),
        P(None, "dp"),
        P(None, "dp"),
        P(None, None, "dp"),
        P(None, "dp"),
        P(None, "dp"),
        P("dp"),
        P(None, "dp"),
        P(None, "dp"),
        P(None, None, "dp"),
        P(None, "dp"),
        P(None, "dp"),
        P("dp"),
        P(None, "dp"),
        P(None, "dp"),
        P(None, None, "dp"),
        P(None, "dp"),
        P(None, "dp"),
        P("dp"),
        P(),
        P(),
        P(),
    )
    return jax.shard_map(local, mesh=mesh, in_specs=in_specs, out_specs=out_specs, check_vma=False)
```

profile of v0, /device:TPU:1, one launch (start us, length us, event | category | flops | bytes accessed | tf_op | source)
XLA Modules:
  0.0 2057.3 jit_solution(12116388626094345383)
XLA Ops:
  9.1 2.7 convert_element_type.135
  12.8 22.0 %all-gather = bf16[16,1,1280]{2,1,0:T(2,128)(2,1)S(1)} all-gather(bf16[1,1,1280]{2,1,0:T(2,128)(2,1)S(1)} %reshape.200), channel_id=1, replica_groups=mesh['dp'=16,'seq'=8] {'dp'}, dimensions={0}, use_global_device_ids=true | all-gather | bytes 43520 | tf_op jit(solution)/shard_map/all_gather | solution.py:302
  35.5 12.5 all-gather.9.cloned.1.call-done
  48.0 2.2 fusion.65
  50.2 91.7 %all-gather.11.cloned.1.call-done = bf16[1024,8192]{1,0:T(8,128)(2,1)} async-done(((bf16[1024,512]{1,0:T(8,128)(2,1)}), bf16[1024,8192]{1,0:T(8,128)(2,1)}) %all-gather.11.cloned.1.call-update) | async-done | bytes 16777232 | tf_op jit(solution)/shard_map/all_gather | solution.py:297
  142.0 8.0 convolution_add_fusion
  150.1 55.5 %all-gather.13.cloned.1.call-done = bf16[1024,4096]{1,0:T(8,128)(2,1)} async-done(((bf16[1024,256]{1,0:T(8,128)(2,1)}), bf16[1024,4096]{1,0:T(8,128)(2,1)}) %all-gather.13.cloned.1.call-update) | async-done | bytes 8388624 | tf_op jit(solution)/shard_map/all_gather | solution.py:298
  205.6 4.7 fusion.31
  213.6 2.1 convert_element_type.155
  215.8 18.9 all_gather.32
  236.3 46.1 %all-gather.17.cloned.1.call-done = bf16[2,1024,1024]{2,1,0:T(8,128)(2,1)} async-done(((bf16[2,128,1024]{2,1,0:T(8,128)(2,1)}), bf16[2,1024,1024]{2,1,0:T(8,128)(2,1)}) %all-gather.17.cloned.1.call-update) | async-done | bytes 4194320 | tf_op jit(solution)/shard_map/all_gather | solution.py:88
  282.4 6.2 copy.102
  288.6 65.9 %all-gather.15.cloned.1.call-done = bf16[2,1024,1024]{2,1,0:T(8,128)(2,1)} async-done(((bf16[2,128,1024]{2,1,0:T(8,128)(2,1)}), bf16[2,1024,1024]{2,1,0:T(8,128)(2,1)}) %all-gather.15.cloned.1.call-update) | async-done | bytes 4194320 | tf_op jit(solution)/shard_map/all_gather | solution.py:89
  354.5 6.2 copy.100
  360.7 11.3 fusion.98
  372.0 10.6 fusion.40
  382.6 3.6 fusion.94
  386.4 67.9 %all-gather.19.cloned.1.call-done = bf16[2,1024,4096]{2,1,0:T(8,128)(2,1)} async-done(((bf16[2,1024,256]{2,1,0:T(8,128)(2,1)}), bf16[2,1024,4096]{2,1,0:T(8,128)(2,1)}) %all-gather.19.cloned.1.call-update) | async-done | bytes 16777232 | tf_op jit(solution)/shard_map/all_gather | solution.py:299
  454.3 5.8 fusion.13
  460.2 8.7 fusion.93
  469.1 48.6 %all-gather.21.cloned.1.call-done = bf16[1024,4096]{1,0:T(8,128)(2,1)} async-done(((bf16[1024,256]{1,0:T(8,128)(2,1)}), bf16[1024,4096]{1,0:T(8,128)(2,1)}) %all-gather.21.cloned.1.call-update) | async-done | bytes 8388624 | tf_op jit(solution)/shard_map/all_gather | solution.py:300
  517.8 5.9 fusion.99
  527.7 64.3 %psum.63 = f32[]{:T(128)} all-reduce(f32[]{:T(128)} %get-tuple-element.40), channel_id=1, replica_groups=mesh['dp'=16,'seq'=8] {'dp','seq'}, use_global_device_ids=true, to_apply=%region_1.0 | all-reduce | flops 1 | bytes 8 | tf_op jit(solution)/shard_map/psum | solution.py:308
  592.6 4.4 convert_reduce_fusion
  597.1 6.8 multiply_reduce_fusion.5
  606.1 7.6 convert_reduce_fusion.1
  613.7 6.3 multiply_reduce_fusion.6
  622.3 3.1 fusion.43
  625.5 2.0 copy.104
  627.5 15.9 multiply_reduce_fusion
  643.4 11.5 multiply_convert_fusion
  654.9 5.0 broadcast_multiply_fusion
  660.6 8.7 copy.105
  670.3 10.0 fusion.26
  680.4 8.7 copy.106
  689.3 7.9 fusion.44
  698.2 82.8 %reduce-scatter.8.cloned.1.call-done = f32[2,128,1024]{2,1,0:T(8,128)} async-done(((f32[2,1024,1024]{2,1,0:T(8,128)}), f32[2,128,1024]{2,1,0:T(8,128)}) %reduce-scatter.8.cloned.1.call-update) | async-done | bytes 1048592 | tf_op jit(solution)/shard_map/reduce_scatter | solution.py:212
  781.1 2.1 convert.10
  783.2 114.5 %reduce-scatter.10.cloned.1.call-done = f32[2,128,1024]{2,1,0:T(8,128)} async-done(((f32[2,1024,1024]{2,1,0:T(8,128)}), f32[2,128,1024]{2,1,0:T(8,128)}) %reduce-scatter.10.cloned.1.call-update) | async-done | bytes 1048592 | tf_op jit(solution)/shard_map/reduce_scatter | solution.py:215
  899.1 5.2 fusion.78
  904.4 16.6 fusion.100
  921.0 3.9 fusion.61
  925.2 9.9 convolution_bitcast_fusion
  938.1 2.0 convolution_bitcast_fusion.3
  940.0 6.1 pad_maximum_fusion.1
  947.8 2.5 convolution_bitcast_fusion.2
  950.3 4.9 convolution_bitcast_fusion.1
  955.2 11.2 pad_maximum_fusion
  966.8 17.2 fusion.77
  986.4 101.7 %reduce-scatter.18.cloned.1.call-done = f32[1024,256]{1,0:T(8,128)} async-done(((f32[1024,4096]{1,0:T(8,128)}), f32[1024,256]{1,0:T(8,128)}) %reduce-scatter.18.cloned.1.call-update) | async-done | bytes 1048592 | tf_op jit(solution)/shard_map/reduce_scatter | solution.py:359
  1088.1 99.3 %reduce-scatter.14.cloned.1.call-done = f32[1024,256]{1,0:T(8,128)} async-done(((f32[1024,4096]{1,0:T(8,128)}), f32[1024,256]{1,0:T(8,128)}) %reduce-scatter.14.cloned.1.call-update) | async-done | bytes 1048592 | tf_op jit(solution)/shard_map/reduce_scatter | solution.py:357
  1187.4 183.8 %reduce-scatter.16.cloned.1.call-done = f32[2,1024,256]{2,1,0:T(8,128)} async-done(((f32[2,1024,4096]{2,1,0:T(8,128)}), f32[2,1024,256]{2,1,0:T(8,128)}) %reduce-scatter.16.cloned.1.call-update) | async-done | bytes 2097168 | tf_op jit(solution)/shard_map/reduce_scatter | solution.py:358
  1371.2 183.8 %reduce-scatter.12.cloned.1.call-done = f32[1024,512]{1,0:T(8,128)} async-done(((f32[1024,8192]{1,0:T(8,128)}), f32[1024,512]{1,0:T(8,128)}) %reduce-scatter.12.cloned.1.call-update) | async-done | bytes 2097168 | tf_op jit(solution)/shard_map/reduce_scatter | solution.py:356
  1556.4 109.5 %all-reduce.6.cloned.1.call-done = f32[20480]{0:T(1024)} async-done(((f32[20480]{0:T(1024)}), f32[20480]{0:T(1024)}) %all-reduce.6.cloned.1.call-update) | async-done | bytes 81936
  1666.6 21.8 %psum.77 = f32[1280]{0:T(1024)S(1)} all-reduce(f32[1280]{0:T(1024)S(1)} %dynamic-slice.1), channel_id=1, replica_groups=mesh['dp'=16,'seq'=8] {'seq'}, use_global_device_ids=true, to_apply=%region_49.50 | all-reduce | flops 1280 | bytes 10240 | tf_op jit(solution)/shard_map/psum | solution.py:352
  1689.1 258.1 %all-reduce.8.cloned.1.call-done = (f32[1024,512]{1,0:T(8,128)}, f32[1024,256]{1,0:T(8,128)}, f32[2,1024,256]{2,1,0:T(8,128)}, f32[1024,256]{1,0:T(8,128)}, f32[1000,64]{0,1:T(8,128)}) async-done(((f32[1024,512]{1,0:T(8,128)}, f32[1024,256]{1,0:T(8,128)}, f32[2,1024,256]{2,1,0:T(8,128)}, f32[1024,256]{1,0:T(8,128)}, f32[1000,64]{0,1:T(8,128)}), (f32[1024,512]{1,0:T(8,128)}, f32[1024,256]{1,0:T(8,128)}, ...) | async-done | bytes 6547472 | tf_op jit(solution)/shard_map/psum | solution.py:352
  1947.2 2.9 multiply_reduce_fusion.2
  1950.1 2.7 multiply_reduce_fusion.1
  1958.2 70.3 %all-reduce.1 = (f32[]{:T(128)}, f32[]{:T(128)}) all-reduce(f32[]{:T(128)S(6)} %div.149, f32[]{:T(128)} %get-tuple-element.39), channel_id=1, replica_groups=mesh['dp'=16,'seq'=8] {'dp','seq'}, use_global_device_ids=true, to_apply=%region_52.53 | all-reduce | flops 2 | bytes 16 | tf_op jit(solution)/shard_map/psum | solution.py:364
  2029.9 2.3 fusion.81
  2032.3 4.1 fusion.83
  2036.6 4.2 fusion.85
  2040.9 2.4 fusion.87
  2045.0 4.2 fusion.89
  (232 shorter events, 35.8 us)
Async XLA Ops:
  7.2 4.7 copy-start.13
  7.2 5.6 copy-start.51
  7.2 27.8 %copy-start.7 = (bf16[2,128,1024]{2,1,0:T(8,128)(2,1)S(1)}, bf16[2,128,1024]{2,1,0:T(8,128)(2,1)}, u32[]{:S(2)}) copy-start(bf16[2,128,1024]{2,1,0:T(8,128)(2,1)} %param.24) | copy-start | bytes 1572868
  7.2 40.7 %copy-start.63 = (s32[2]{0:T(128)S(1)}, s32[2]{0:T(128)}, u32[]{:S(2)}) copy-start(s32[2]{0:T(128)} %param.29) | copy-start | bytes 28
  7.2 40.7 %all-gather.9.cloned.1.call-start = ((), (), s32[]{:S(2)}) async-start(), calls=%async_computation.7 | async-start | bytes 2228224 | tf_op jit(solution)/shard_map/all_gather | solution.py:301
  9.0 132.9 %all-gather.11.cloned.1.call-start = ((), (), s32[]{:S(2)}) async-start(), calls=%async_computation.8 | async-start | bytes 17825792 | tf_op jit(solution)/shard_map/all_gather | solution.py:297
  11.8 193.8 %all-gather.13.cloned.1.call-start = ((), (), s32[]{:S(2)}) async-start(), calls=%async_computation.9 | async-start | bytes 8912896 | tf_op jit(solution)/shard_map/all_gather | solution.py:298
  12.7 269.7 %all-gather.17.cloned.1.call-start = ((), (), s32[]{:S(2)}) async-start(), calls=%async_computation.11 | async-start | bytes 4718592 | tf_op jit(solution)/shard_map/all_gather | solution.py:88
  35.2 170.4 %copy-start.45 = (f32[2,128]{1,0:T(2,128)}, f32[2,128]{1,0:T(2,128)S(1)}, u32[]{:S(2)}) copy-start(f32[2,128]{1,0:T(2,128)S(1)} %broadcast_multiply_fusion.3) | copy-start | bytes 3076
  35.5 170.1 %copy-start.53 = (f32[2,128]{1,0:T(2,128)}, f32[2,128]{1,0:T(2,128)S(1)}, u32[]{:S(2)}) copy-start(f32[2,128]{1,0:T(2,128)S(1)} %add_rsqrt_fusion) | copy-start | bytes 3076
  50.2 99.8 %copy-start.40 = (f32[2,1024]{1,0:T(2,128)}, f32[2,1024]{1,0:T(2,128)S(1)}, u32[]{:S(2)}) copy-start(f32[2,1024]{1,0:T(2,128)S(1)} %fusion.65) | copy-start | bytes 24580
  150.0 60.3 %copy-start.47 = (f32[2,1024]{1,0:T(2,128)}, f32[2,1024]{1,0:T(2,128)S(1)}, u32[]{:S(2)}) copy-start(f32[2,1024]{1,0:T(2,128)S(1)} %get-tuple-element.104) | copy-start | bytes 24580
  150.0 60.3 %copy-start.49 = (f32[2,1024]{1,0:T(2,128)}, f32[2,1024]{1,0:T(2,128)S(1)}, u32[]{:S(2)}) copy-start(f32[2,1024]{1,0:T(2,128)S(1)} %get-tuple-element.105) | copy-start | bytes 24580
  150.1 304.2 %copy-start.43 = (f32[2,1024]{1,0:T(2,128)}, f32[2,1024]{1,0:T(2,128)S(1)}, u32[]{:S(2)}) copy-start(f32[2,1024]{1,0:T(2,128)S(1)} %get-tuple-element.102) | copy-start | bytes 24580
  211.5 4.3 copy-start.58
  211.5 4.3 copy-start.65
  211.5 143.0 %all-gather.15.cloned.1.call-start = ((), (), s32[]{:S(2)}) async-start(), calls=%async_computation.10 | async-start | bytes 4718592 | tf_op jit(solution)/shard_map/all_gather | solution.py:89
  212.1 242.2 %all-gather.19.cloned.1.call-start = ((), (), s32[]{:S(2)}) async-start(), calls=%async_computation.12 | async-start | bytes 17825792 | tf_op jit(solution)/shard_map/all_gather | solution.py:299
  213.6 304.2 %all-gather.21.cloned.1.call-start = ((), (), s32[]{:S(2)}) async-start(), calls=%async_computation.13 | async-start | bytes 8912896 | tf_op jit(solution)/shard_map/all_gather | solution.py:300
  215.7 565.4 %reduce-scatter.8.cloned.1.call-start = ((), (), s32[]{:S(2)}) async-start(), calls=%async_computation.14 | async-start | bytes 9437184 | tf_op jit(solution)/shard_map/reduce_scatter | solution.py:212
  382.6 77.5 %copy-start.19 = (bf16[2,16,64,128]{3,2,1,0:T(8,128)(2,1)}, bf16[2,16,64,128]{3,2,1,0:T(8,128)(2,1)S(1)}, u32[]{:S(2)}) copy-start(bf16[2,16,64,128]{3,2,1,0:T(8,128)(2,1)S(1)} %fusion.40) | copy-start | bytes 1572868
  460.1 8.7 copy-start.17
  517.8 7.9 copy-start.61
  523.7 3.3 copy-start.62
  597.1 6.8 copy-start.8
  605.1 8.6 copy-start.32
  613.7 6.3 copy-start.25
  613.7 6.7 copy-start.11
  613.7 6.7 copy-start.35
  654.9 5.7 copy-start
  669.3 228.4 %reduce-scatter.10.cloned.1.call-start = ((), (), s32[]{:S(2)}) async-start(), calls=%async_computation.15 | async-start | bytes 9437184 | tf_op jit(solution)/shard_map/reduce_scatter | solution.py:215
  689.1 297.3 %reduce-scatter.20.cloned.1.call-start = ((), (), s32[]{:S(2)}) async-start(), calls=%async_computation.20 | async-start | bytes 4456448 | tf_op jit(solution)/shard_map/reduce_scatter | solution.py:360
  697.2 207.1 %copy-start.9 = (bf16[2,16,64,128]{3,2,1,0:T(8,128)(2,1)}, bf16[2,16,64,128]{3,2,1,0:T(8,128)(2,1)S(1)}, u32[]{:S(2)}) copy-start(bf16[2,16,64,128]{3,2,1,0:T(8,128)(2,1)S(1)} %fusion.44) | copy-start | bytes 1572868
  697.2 201.9 %copy-start.46 = (f32[2,128]{1,0:T(2,128)S(1)}, f32[2,128]{1,0:T(2,128)}, u32[]{:S(2)}) copy-start(f32[2,128]{1,0:T(2,128)} %copy-done.45) | copy-start | bytes 3076
  697.2 201.9 %copy-start.54 = (f32[2,128]{1,0:T(2,128)S(1)}, f32[2,128]{1,0:T(2,128)}, u32[]{:S(2)}) copy-start(f32[2,128]{1,0:T(2,128)} %copy-done.53) | copy-start | bytes 3076
  899.0 5.3 copy-start.28
  904.4 16.6 copy-start.41
  904.4 16.6 copy-start.64
  925.0 163.2 %reduce-scatter.18.cloned.1.call-start = ((), (), s32[]{:S(2)}) async-start(), calls=%async_computation.19 | async-start | bytes 17825792 | tf_op jit(solution)/shard_map/reduce_scatter | solution.py:359
  935.2 2.8 copy-start.27
  935.2 252.2 %reduce-scatter.14.cloned.1.call-start = ((), (), s32[]{:S(2)}) async-start(), calls=%async_computation.17 | async-start | bytes 17825792 | tf_op jit(solution)/shard_map/reduce_scatter | solution.py:357
  946.2 425.1 %reduce-scatter.16.cloned.1.call-start = ((), (), s32[]{:S(2)}) async-start(), calls=%async_computation.18 | async-start | bytes 35651584 | tf_op jit(solution)/shard_map/reduce_scatter | solution.py:358
  966.5 588.6 %reduce-scatter.12.cloned.1.call-start = ((), (), s32[]{:S(2)}) async-start(), calls=%async_computation.16 | async-start | bytes 35651584 | tf_op jit(solution)/shard_map/reduce_scatter | solution.py:356
  984.0 571.1 %copy-start.66 = (u32[128]{0:T(128)S(1)}, u32[128]{0:T(128)}, u32[]{:S(2)}) copy-start(u32[128]{0:T(128)} %constant.105) | copy-start | bytes 1540
  984.0 681.8 %all-reduce.6.cloned.1.call-start = ((), (), s32[]{:S(2)}) async-start(), calls=%async_computation.21 | async-start | bytes 163840
  986.1 961.1 %all-reduce.8.cloned.1.call-start = ((), (), s32[]{:S(2)}) async-start(), calls=%async_computation.22 | async-start | bytes 13107200 | tf_op jit(solution)/shard_map/psum | solution.py:352
  1555.1 474.2 %copy-start.52 = (f32[1280]{0:T(1024)S(1)}, f32[1280]{0:T(1024)}, u32[]{:S(2)}) copy-start(f32[1280]{0:T(1024)} %param.35) | copy-start | bytes 15364
  1555.1 474.2 %copy-start.59 = (f32[1280]{0:T(1024)S(1)}, f32[1280]{0:T(1024)}, u32[]{:S(2)}) copy-start(f32[1280]{0:T(1024)} %param.41) | copy-start | bytes 15364
  1555.1 474.2 %copy-start.60 = (f32[1280]{0:T(1024)S(1)}, f32[1280]{0:T(1024)}, u32[]{:S(2)}) copy-start(f32[1280]{0:T(1024)} %param.47) | copy-start | bytes 15364
  1555.1 474.8 %copy-start.36 = (f32[1000,64]{0,1:T(8,128)S(1)}, f32[1000,64]{0,1:T(8,128)}, u32[]{:S(2)}) copy-start(f32[1000,64]{0,1:T(8,128)} %param.34) | copy-start | bytes 768004
  1947.2 5.6 copy-start.37
  1947.2 6.3 copy-start.15
  1947.2 6.3 copy-start.16
  1947.2 85.1 %copy-start.12 = (f32[1024,256]{1,0:T(8,128)S(1)}, f32[1024,256]{1,0:T(8,128)}, u32[]{:S(2)}) copy-start(f32[1024,256]{1,0:T(8,128)} %param.33) | copy-start | bytes 3145732
  2029.9 6.5 copy-start.22
  2032.2 4.1 copy-start.3
  2032.2 4.1 copy-start.6
  2032.2 4.4 copy-start.21
  2036.6 4.2 copy-start.14
  2036.6 4.2 copy-start.33
  2036.6 4.2 copy-start.34
  2036.6 6.7 copy-start.24
  2040.8 3.6 copy-start.5
  2040.8 4.1 copy-start.23
  (19 other events, 32.7 us)
Sparse Core Ops, SparseCore 0:
  10.4 37.5 all-gather.8
  50.2 91.7 all-gather.10
  144.2 61.3 all-gather.12
  211.6 70.7 all-gather.16
  285.2 69.2 all-gather.14
  356.5 97.7 all-gather.18
  456.5 61.2 all-gather.20
  669.4 111.5 reduce-scatter.7
  785.0 112.6 reduce-scatter.9
  925.1 61.2 reduce-scatter.19
  988.8 99.2 reduce-scatter.17
  1090.4 97.0 reduce-scatter.13
  1189.9 181.2 reduce-scatter.15
  1373.6 181.4 reduce-scatter.11
  1557.9 107.8 all-reduce.5
  1668.9 278.2 all-reduce.7
where the time goes:
time: 2070 us; the launch traced here: 2060 us
  waiting for transfers between devices  1520 us (73%)
  blocking collectives  197 us (10%)
  matrix products  187 us (9%)
  other arithmetic  77.7 us (4%)
  local copies, waits for them, and re-layouts  48.8 us (2%)
  between operations  21.8 us (1%)
    psum x1, waiting for transfers between devices, local(): lax.psum((grad_cond, grad_attn, grad_mlp, grad_head, grad_table, grad_bia...  258 us
    reduce_scatter x1, waiting for transfers between devices, local(): lax.psum_scatter(sum_cond, 'dp', scatter_dimension=1, tiled=True)  184 us
    reduce_scatter x1, waiting for transfers between devices, local(): lax.psum_scatter(sum_mlp, 'dp', scatter_dimension=2, tiled=True)  184 us
    reduce_scatter x1, waiting for transfers between devices, backward_layer(): lax.psum_scatter(value_term.reshape(images, -1, model_width), 'seq', scat...  115 us
    unnamed x17, waiting for transfers between devices  110 us
    reduce_scatter x1, waiting for transfers between devices, local(): lax.psum_scatter(sum_head, 'dp', scatter_dimension=1, tiled=True)  102 us
    reduce_scatter x1, waiting for transfers between devices, local(): lax.psum_scatter(sum_attn, 'dp', scatter_dimension=1, tiled=True)  99.3 us
    all_gather x1, waiting for transfers between devices, local(): lax.all_gather(cond_w.astype(jnp.bfloat16), 'dp', axis=1, tiled=True)  91.7 us
  transfers between devices with their start and end apart: 16, of which 16 were waited for; matrix products, arithmetic and copies ran while one was open for 8% of the time, Pallas kernels for 0%

commit v1 on v0

v1 whole, which is shorter than its diff:
```python
import functools

import jax
import jax.numpy as jnp
from jax import lax
from jax.experimental import pallas as pl
from jax.experimental.pallas import tpu as pltpu
from jax.sharding import PartitionSpec as P

STEP = 5
HIGH = lax.Precision.HIGHEST
NORM_EPS = 1e-06
CLIP = 0.01
LEARN = 0.02
DECAY = 0.1
BETA_ONE = 0.5
BETA_TWO = 0.5
ADAM_EPS = 1e-08
SCORE_SCALE = 0.125
MESH = pl.DeviceIdType.MESH
F32 = jnp.float32
BF16 = jnp.bfloat16
ANY = pl.BlockSpec(memory_space=pl.ANY)
VM = pl.BlockSpec(memory_space=pltpu.VMEM)

ROWS_YZ = 576
HALF_YZ = 288
QUARTER = 112
PART_ROWS = (32, 56, 40)
PART_BASE = (0, 256, 704)
ORDERS = ("xyz", "yzx", "zxy")


def place():
    dp = lax.axis_index("dp")
    sq = lax.axis_index("seq")
    core = lax.rem(dp, 2)
    y = lax.rem(dp // 2, 4)
    z = lax.rem(sq, 2) * 2 + dp // 8
    return sq // 2, y, z, core


def at(x, y, z, core):
    x, y, z = lax.rem(x + 4, 4), lax.rem(y + 4, 4), lax.rem(z + 4, 4)
    return (lax.rem(z, 2) * 8 + y * 2 + core, x * 2 + z // 2)


def greet(devices):
    bar = pltpu.get_barrier_semaphore()
    for device in devices:
        pl.semaphore_signal(bar, inc=1, device_id=device, device_id_type=MESH)
    pl.semaphore_wait(bar, len(devices))


def remote(src, dst, send, recv, device):
    return pltpu.make_async_remote_copy(
        src_ref=src, dst_ref=dst, send_sem=send, recv_sem=recv, device_id=device, device_id_type=MESH
    )


def params(collective_id, vmem=None):
    return pltpu.CompilerParams(
        collective_id=collective_id, has_side_effects=True, vmem_limit_bytes=vmem
    )


def gather_kernel(s, w, wo, ss, rs, loc, os, orr):
    x, y, z, c = place()
    zl = lax.rem(z, 2)
    up, down = lax.rem(y + 1, 4), lax.rem(y + 3, 4)
    side = 1 - 2 * c
    yp, ym = at(x, y + 1, z, c), at(x, y - 1, z, c)
    zp, zm = at(x, y, z + 1, c), at(x, y, z - 1, c)
    xp, xm = at(x + 1, y, z, c), at(x - 1, y, z, c)
    zs = at(x, y, z + side, c)
    mate = at(x, y, z, 1 - c)
    greet([yp, ym, zp, zm, xp, xm, mate])

    def quarter(pos):
        return pl.ds(pl.multiple_of(ROWS_YZ + QUARTER * lax.rem(pos + 4, 4), 16), QUARTER)

    mine = quarter(x)
    full, first, second = pl.ds(0, ROWS_YZ), pl.ds(0, HALF_YZ), pl.ds(HALF_YZ, HALF_YZ)
    order = (0, 1, 2, 3)
    sent = []

    def go(j, k, src, dst, device):
        cp = remote(src, dst, ss.at[j, k], rs.at[j, k], device)
        cp.start()
        sent.append(cp)

    def got(j, k, ref):
        remote(ref, ref, ss.at[j, k], rs.at[j, k], mate).wait_recv()

    locals_ = []
    for j in order:
        go(j, 0, s.at[j, full], w.at[zl, y, j, full], yp)
        go(j, 1, s.at[j, full], w.at[zl, y, j, full], ym)
        go(j, 6, s.at[j, mine], w.at[zl, y, j, mine], zs)
        for i, rows in enumerate((full, mine)):
            cp = pltpu.make_async_copy(s.at[j, rows], w.at[zl, y, j, rows], loc.at[j, i])
            cp.start()
            locals_.append(cp)
    for cp in locals_:
        cp.wait()
    for j in order:
        got(j, 6, w.at[1 - zl, y, j, mine])
        go(j, 7, w.at[:, y, j, mine], w.at[:, y, j, mine], yp)
        go(j, 8, w.at[:, y, j, mine], w.at[:, y, j, mine], ym)
        got(j, 0, w.at[zl, down, j, full])
        got(j, 1, w.at[zl, up, j, full])
        go(j, 2, w.at[zl, down, j, first], w.at[zl, down, j, first], yp)
        go(j, 3, w.at[zl, up, j, second], w.at[zl, up, j, second], ym)
    for j in order:
        got(j, 7, w.at[:, down, j, mine])
        got(j, 8, w.at[:, up, j, mine])
        go(j, 9, w.at[0, down, j, mine], w.at[0, down, j, mine], yp)
        go(j, 10, w.at[1, up, j, mine], w.at[1, up, j, mine], ym)
        far = lax.rem(y + 2, 4)
        got(j, 2, w.at[zl, far, j, first])
        got(j, 3, w.at[zl, far, j, second])
        go(j, 4, w.at[zl, :, j, first], w.at[zl, :, j, first], zp)
        go(j, 5, w.at[zl, :, j, second], w.at[zl, :, j, second], zm)
    for j in order:
        far = lax.rem(y + 2, 4)
        got(j, 9, w.at[0, far, j, mine])
        got(j, 10, w.at[1, far, j, mine])
        go(j, 11, w.at[:, :, j, mine], w.at[:, :, j, mine], xp)
        go(j, 12, w.at[:, :, j, mine], w.at[:, :, j, mine], xm)
    for j in order:
        left, right = quarter(x - 1), quarter(x + 1)
        got(j, 11, w.at[:, :, j, left])
        got(j, 12, w.at[:, :, j, right])
        go(j, 13, w.at[0, :, j, left], w.at[0, :, j, left], xp)
        go(j, 14, w.at[1, :, j, right], w.at[1, :, j, right], xm)
    last = []
    for j in order:
        across = quarter(x + 2)
        got(j, 4, w.at[1 - zl, :, j, first])
        got(j, 5, w.at[1 - zl, :, j, second])
        got(j, 13, w.at[0, :, j, across])
        got(j, 14, w.at[1, :, j, across])
        if j == 0:
            for i in range(2):
                src = w.at[1, 2 + i, 0]
                dst = wo.at[2 * i + c]
                cp = remote(src, dst, os.at[i], orr.at[i], mate)
                cp.start()
                lc = pltpu.make_async_copy(src, dst, loc.at[i, 2])
                lc.start()
                last += [cp, lc]
    for cp in last:
        cp.wait()
    for cp in sent:
        cp.wait_send()


def gather_weights(shard):
    return pl.pallas_call(
        gather_kernel,
        out_shape=(
            jax.ShapeDtypeStruct((2, 4, 4, 1024, 256), BF16),
            jax.ShapeDtypeStruct((4, 1024, 256), BF16),
        ),
        in_specs=[ANY],
        out_specs=(ANY, ANY),
        scratch_shapes=[
            pltpu.SemaphoreType.DMA((4, 15)),
            pltpu.SemaphoreType.DMA((4, 15)),
            pltpu.SemaphoreType.DMA((4, 3)),
            pltpu.SemaphoreType.DMA((2,)),
            pltpu.SemaphoreType.DMA((2,)),
        ],
        compiler_params=params(0),
    )(shard)


def pair_kernel(n, *refs):
    ins, outs = refs[:n], refs[n : 2 * n]
    ss, rs, loc = refs[2 * n :]
    x, y, z, c = place()
    mate = at(x, y, z, 1 - c)
    greet([mate])
    cps = []
    for i in range(n):
        cps.append(remote(ins[i], outs[i].at[c], ss.at[i], rs.at[i], mate))
        cps.append(pltpu.make_async_copy(ins[i], outs[i].at[c], loc.at[i]))
    for cp in cps:
        cp.start()
    for cp in cps:
        cp.wait()


def pair_gather(cid, *arrays):
    n = len(arrays)
    return pl.pallas_call(
        functools.partial(pair_kernel, n),
        out_shape=tuple(jax.ShapeDtypeStruct((2,) + a.shape, a.dtype) for a in arrays),
        in_specs=[ANY] * n,
        out_specs=(ANY,) * n,
        scratch_shapes=[pltpu.SemaphoreType.DMA((n,))] * 3,
        compiler_params=params(cid),
    )(*arrays)


def swap_kernel(a, o, got, ss, rs):
    x, y, z, c = place()
    mate = at(x, y, z, 1 - c)
    greet([mate])
    cp = remote(a.at[1 - c], got, ss, rs, mate)
    cp.start()
    cp.wait()
    o[...] = a[c] + got[...]


def swap_add(cid, a):
    return pl.pallas_call(
        swap_kernel,
        out_shape=jax.ShapeDtypeStruct(a.shape[1:], a.dtype),
        in_specs=[VM],
        out_specs=VM,
        scratch_shapes=[
            pltpu.VMEM(a.shape[1:], a.dtype),
            pltpu.SemaphoreType.DMA,
            pltpu.SemaphoreType.DMA,
        ],
        compiler_params=params(cid, 32 * 2**20),
    )(a)


def group_peers():
    dp = lax.axis_index("dp")
    sq = lax.axis_index("seq")
    core = lax.rem(dp, 2)
    out = [(dp + 1 - 2 * core, sq)]
    for i in range(1, 8):
        for flip in range(2):
            out.append((dp + flip * (1 - 2 * core), lax.rem(sq + i, 8)))
    return out


def a2a_kernel(a, o, ss, rs, loc):
    dp = lax.axis_index("dp")
    sq = lax.axis_index("seq")
    peers = [(dp, lax.rem(sq + i, 8)) for i in range(1, 8)]
    greet(peers)
    own = pltpu.make_async_copy(a.at[sq], o.at[sq], loc)
    own.start()
    cps = []
    for i in range(1, 8):
        to = lax.rem(sq + i, 8)
        cp = remote(a.at[to], o.at[sq], ss.at[i], rs.at[i], (dp, to))
        cp.start()
        cps.append(cp)
    own.wait()
    for cp in cps:
        cp.wait()


def all_to_all(cid, a):
    return pl.pallas_call(
        a2a_kernel,
        out_shape=jax.ShapeDtypeStruct(a.shape, a.dtype),
        in_specs=[ANY],
        out_specs=ANY,
        scratch_shapes=[
            pltpu.SemaphoreType.DMA((8,)),
            pltpu.SemaphoreType.DMA((8,)),
            pltpu.SemaphoreType.DMA,
        ],
        compiler_params=params(cid),
    )(a)


def head_lanes(pair, core):
    return pl.ds(pl.multiple_of(((pair // 2 * 2 + core) * 2 + lax.rem(pair, 2)) * 128, 128), 128)


def to_tokens_kernel(a, o, ss, rs, loc):
    dp = lax.axis_index("dp")
    sq = lax.axis_index("seq")
    core = lax.rem(dp, 2)
    base = dp - core
    pair, owner = sq // 2, lax.rem(sq, 2)
    greet(group_peers())
    lanes = head_lanes(pair, core)

    def copy(i):
        to = lax.rem(sq + i, 8)
        return remote(
            a.at[to], o.at[:, lanes], ss.at[i], rs.at[pair, core], (base + owner, to)
        )

    for i in range(1, 8):
        copy(i).start()
    own = pltpu.make_async_copy(a.at[sq], o.at[:, lanes], loc)

    @pl.when(owner == core)
    def _():
        own.start()

    @pl.when(owner != core)
    def _():
        copy(0).start()

    for p in range(4):
        for q in range(2):
            view = o.at[:, pl.ds(((p // 2 * 2 + q) * 2 + p % 2) * 128, 128)]

            @pl.when(jnp.logical_or(sq != p * 2 + core, core != q))
            def _():
                remote(view, view, ss.at[0], rs.at[p, q], (base + owner, sq)).wait_recv()

    for i in range(1, 8):
        copy(i).wait_send()

    @pl.when(owner == core)
    def _():
        own.wait()

    @pl.when(owner != core)
    def _():
        copy(0).wait_send()


def to_tokens(cid, a):
    return pl.pallas_call(
        to_tokens_kernel,
        out_shape=jax.ShapeDtypeStruct((256, 1024), a.dtype),
        in_specs=[ANY],
        out_specs=ANY,
        scratch_shapes=[
            pltpu.SemaphoreType.DMA((8,)),
            pltpu.SemaphoreType.DMA((4, 2)),
            pltpu.SemaphoreType.DMA,
        ],
        compiler_params=params(cid),
    )(a)


def to_heads_kernel(a, o, ss, rs, loc):
    dp = lax.axis_index("dp")
    sq = lax.axis_index("seq")
    core = lax.rem(dp, 2)
    base = dp - core
    pair, owner = sq // 2, lax.rem(sq, 2)
    greet(group_peers())
    own = pltpu.make_async_copy(a.at[:, head_lanes(pair, core)], o.at[sq], loc)

    def each(fn):
        for p in range(4):
            for q in range(2):
                view = a.at[:, pl.ds(((p // 2 * 2 + q) * 2 + p % 2) * 128, 128)]
                to = (base + q, p * 2 + core)
                cp = remote(view, o.at[sq], ss.at[p, q], rs.at[sq], to)
                here = jnp.logical_and(sq == p * 2 + core, core == q)
                fn(cp, here)

    def start(cp, here):
        @pl.when(jnp.logical_not(here))
        def _():
            cp.start()

    def finish(cp, here):
        @pl.when(jnp.logical_not(here))
        def _():
            cp.wait_send()

    each(start)

    @pl.when(owner == core)
    def _():
        own.start()

    for i in range(8):
        view = o.at[i]

        @pl.when(jnp.logical_or(sq != i, owner != core))
        def _():
            remote(view, view, ss.at[0, 0], rs.at[i], (base, sq)).wait_recv()

    each(finish)

    @pl.when(owner == core)
    def _():
        own.wait()


def to_heads(cid, a):
    return pl.pallas_call(
        to_heads_kernel,
        out_shape=jax.ShapeDtypeStruct((8, 256, 128), a.dtype),
        in_specs=[ANY],
        out_specs=ANY,
        scratch_shapes=[
            pltpu.SemaphoreType.DMA((4, 2)),
            pltpu.SemaphoreType.DMA((8,)),
            pltpu.SemaphoreType.DMA,
        ],
        compiler_params=params(cid),
    )(a)


def cond_kernel(
    msg, slots, table, cond_w, msg_all, slots_all, cond_all, emb_out, ada,
    cond_own, ada_own, s1, r1, s2, r2, s3, r3, s4, r4,
):
    dp = lax.axis_index("dp")
    sq = lax.axis_index("seq")
    core = lax.rem(dp, 2)
    row = [(lax.rem(dp + i, 16), sq) for i in range(1, 16)]
    group = group_peers()
    greet(row + group[1:])
    first = []
    for i, to in enumerate(row):
        cp = remote(msg, msg_all.at[dp], s1.at[i], r1.at[i], to)
        cp.start()
        first.append(cp)
    msg_all[dp] = msg[...]
    for cp in first:
        cp.wait()
    seen = msg_all[...]
    count = jnp.sum(seen[:, 10, 2:3], axis=0, keepdims=True)
    slots[7:8, :] = jnp.broadcast_to(count, (1, 128))
    second = []
    for i, to in enumerate(group):
        cp = remote(slots, slots_all.at[sq * 2 + core], s2.at[i], r2.at[i], to)
        cp.start()
        second.append(cp)
    slots_all[sq * 2 + core] = slots[...]
    classes = table.shape[0]
    lane = lax.broadcasted_iota(jnp.int32, (32, classes), 1)
    labels = jnp.concatenate([seen[d, 10:11, i : i + 1] for d in range(16) for i in range(2)], axis=0)
    hit = jnp.where(lane == labels.astype(jnp.int32), 1.0, 0.0).astype(BF16)
    emb = jnp.dot(hit, table[...], preferred_element_type=F32)
    emb_out[...] = emb
    cond_own[...] = (emb / (1.0 + jnp.exp(-emb))).astype(BF16)
    cond_all[dp] = cond_own[...]
    third = []
    for i, to in enumerate(row):
        cp = remote(cond_own, cond_all.at[dp], s3.at[i], r3.at[i], to)
        cp.start()
        third.append(cp)
    for cp in third:
        cp.wait()
    acc = jnp.zeros((32, 512), F32)
    for d in range(16):
        acc += jnp.dot(cond_all[d], cond_w[pl.ds(64 * d, 64), :], preferred_element_type=F32)
    bias = []
    for i in range(4):
        at_row = dp * 4 + i
        bias.append(msg_all[at_row // 10, pl.ds(lax.rem(at_row, 10), 1), :])
    acc += jnp.concatenate(bias, axis=1)
    for d in range(16):
        ada_own[d] = acc[2 * d : 2 * d + 2]
    fourth = []
    for i in range(15):
        to = lax.rem(dp + 1 + i, 16)
        cp = remote(ada_own.at[to], ada.at[dp], s4.at[i], r4.at[i], (to, sq))
        cp.start()
        fourth.append(cp)
    ada[dp] = ada_own[dp]
    for cp in fourth:
        cp.wait()
    for cp in second:
        cp.wait()


def condition(msg, slots, table, cond_w):
    dma = pltpu.SemaphoreType.DMA
    return pl.pallas_call(
        cond_kernel,
        out_shape=(
            jax.ShapeDtypeStruct((16, 16, 128), F32),
            jax.ShapeDtypeStruct((16, 8, 128), F32),
            jax.ShapeDtypeStruct((16, 32, 64), BF16),
            jax.ShapeDtypeStruct((32, 64), F32),
            jax.ShapeDtypeStruct((16, 2, 512), F32),
        ),
        in_specs=[VM] * 4,
        out_specs=(VM,) * 5,
        scratch_shapes=[pltpu.VMEM((32, 64), BF16), pltpu.VMEM((16, 2, 512), F32)]
        + [dma((15,))] * 8,
        input_output_aliases={},
        compiler_params=params(1),
    )(msg, slots, table, cond_w)


def small_kernel(
    msg, cond_w, ada_all, bias_sum, dcond,
    got, mine, all_seq, part, back, s1, r1, s2, r2, s3, r3,
):
    dp = lax.axis_index("dp")
    sq = lax.axis_index("seq")
    row = [lax.rem(dp + i, 16) for i in range(1, 16)]
    line = [lax.rem(sq + i, 8) for i in range(1, 8)]
    greet([(d, sq) for d in row] + [(dp, s) for s in line])
    cps = []
    for i, d in enumerate(row):
        cp = remote(msg.at[d], got.at[dp], s1.at[i], r1.at[i], (d, sq))
        cp.start()
        cps.append(cp)
    got[dp] = msg[dp]
    for cp in cps:
        cp.wait()
    seen = got[...]
    for d in range(16):
        mine[d] = seen[d, :8, :]
    rest = jnp.sum(seen[:, 8:24, :], axis=0)
    mine[16] = rest[:8]
    mine[17] = rest[8:]
    cps = []
    for i, s in enumerate(line):
        cp = remote(mine, all_seq.at[sq], s2.at[i], r2.at[i], (dp, s))
        cp.start()
        cps.append(cp)
    all_seq[sq] = mine[...]
    for cp in cps:
        cp.wait()
    total = jnp.sum(all_seq[...], axis=0)
    bias_sum[0] = total[16]
    bias_sum[1] = total[17]
    rows = []
    for d in range(16):
        for i in range(2):
            rows.append(
                jnp.concatenate([total[d, 4 * i + k : 4 * i + k + 1, :] for k in range(4)], axis=1)
            )
    dada = jnp.concatenate(rows, axis=0)
    ada_all[...] = dada
    for d in range(16):
        part[d] = lax.dot_general(
            dada, cond_w[pl.ds(64 * d, 64), :].astype(F32), (((1,), (1,)), ((), ())),
            precision=HIGH, preferred_element_type=F32,
        )
    cps = []
    for i, d in enumerate(row):
        cp = remote(part.at[d], back.at[dp], s3.at[i], r3.at[i], (d, sq))
        cp.start()
        cps.append(cp)
    back[dp] = part[dp]
    for cp in cps:
        cp.wait()
    dcond[...] = jnp.sum(back[...], axis=0)


def small_reduce(msg, cond_w):
    dma = pltpu.SemaphoreType.DMA
    return pl.pallas_call(
        small_kernel,
        out_shape=(
            jax.ShapeDtypeStruct((32, 512), F32),
            jax.ShapeDtypeStruct((2, 8, 128), F32),
            jax.ShapeDtypeStruct((32, 64), F32),
        ),
        in_specs=[VM] * 2,
        out_specs=(VM,) * 3,
        scratch_shapes=[
            pltpu.VMEM((16, 24, 128), F32),
            pltpu.VMEM((18, 8, 128), F32),
            pltpu.VMEM((8, 18, 8, 128), F32),
            pltpu.VMEM((16, 32, 64), F32),
            pltpu.VMEM((16, 32, 64), F32),
        ]
        + [dma((15,))] * 6,
        compiler_params=params(2),
    )(msg, cond_w)


def pick(ref, x, y, z, extra=()):
    everything = slice(None)
    zl = everything if z is None else lax.rem(z, 2)
    zh = everything if z is None else z // 2
    return (
        zl,
        everything if y is None else y,
        everything if x is None else x,
        zh,
    )


def halves(order, phase, rows):
    axis = order[phase]
    later = order[phase + 1 :]
    if axis != "z" and "z" in later:
        return ("zl", slice(0, 1), slice(1, 2))
    if "y" in later:
        return ("y", slice(0, 2), slice(2, 4))
    if "x" in later:
        return ("x", slice(0, 2), slice(2, 4))
    cut = (rows // 16) * 8 if (rows // 16) * 16 == rows else (rows // 16) * 8 + 8
    return ("r", slice(0, cut), slice(cut, rows))


def cut_size(part, phase):
    order, rows = ORDERS[part], PART_ROWS[part]
    axis, later = order[phase], order[phase + 1 :]
    dims = {
        "zl": 2 if "z" in later else 1,
        "y": 4 if "y" in later else 1,
        "x": 4 if "x" in later else 1,
        "zh": 2 if "z" in later else 1,
        "r": rows,
    }
    return dims


def reduce_kernel(*refs):
    gs = refs[0:4]
    extra, out, norm = refs[4:7]
    pos = 7
    parts = [refs[pos + 3 * slot : pos + 3 * slot + 3] for slot in range(2)]
    pos += 6
    recv = {}
    for p in range(3):
        for ph in range(3):
            recv[p, ph] = refs[pos : pos + 4]
            pos += 4
    ss, rs, loc, gss, grs, oloc, tile, tiles, nss, nrs = refs[pos:]

    x, y, z, c = place()
    zl, zh = lax.rem(z, 2), z // 2
    here = {"x": x, "y": y, "z": z}

    def step(axis, by):
        q = dict(here)
        q[axis] = q[axis] + by
        return at(q["x"], q["y"], q["z"], c)

    mate = at(x, y, z, 1 - c)
    greet([step(a, b) for a in "xyz" for b in (1, 2, 3)] + [mate])

    def view(ref, p, ph, index, half=None):
        order = ORDERS[p]
        sel = {}
        for i, a in enumerate(order):
            if i < ph:
                sel[a] = here[a]
            elif i == ph:
                sel[a] = lax.rem(index + 4, 4)
            else:
                sel[a] = None
        idx = {
            "zl": slice(0, 2) if sel["z"] is None else pl.ds(lax.rem(sel["z"], 2), 1),
            "y": slice(0, 4) if sel["y"] is None else pl.ds(sel["y"], 1),
            "x": slice(0, 4) if sel["x"] is None else pl.ds(sel["x"], 1),
            "zh": slice(0, 2) if sel["z"] is None else pl.ds(sel["z"] // 2, 1),
            "r": slice(0, PART_ROWS[p]),
        }
        if half is not None:
            name, one, two = halves(order, ph, PART_ROWS[p])
            idx[name] = (one, two)[half]
        return ref.at[idx["zl"], idx["y"], idx["x"], idx["zh"], idx["r"]]

    def add(dst, srcs):
        dims = dst.shape[:4]
        total = dims[0] * dims[1] * dims[2] * dims[3]

        def body(i, carry):
            d = lax.rem(i, dims[3])
            i2 = i // dims[3]
            cc = lax.rem(i2, dims[2])
            i3 = i2 // dims[2]
            b = lax.rem(i3, dims[1])
            a = i3 // dims[1]
            acc = dst[a, b, cc, d]
            for s in srcs:
                acc = acc + s[a, b, cc, d]
            dst[a, b, cc, d] = acc
            return carry

        lax.fori_loop(0, total, body, 0)

    sent = []

    def job(j):
        slot = j % 2
        loads = []
        for p in range(3):
            r = PART_ROWS[p]
            for xi in range(4):
                for zi in range(2):
                    src = gs[j].at[:, :, pl.ds(PART_BASE[p] + (xi * 2 + zi) * r, r)]
                    cp = pltpu.make_async_copy(src, parts[slot][p].at[:, :, xi, zi], loc.at[slot, p, xi * 2 + zi])
                    cp.start()
                    loads.append(cp)
        yield
        for cp in loads:
            cp.wait()
        mine = []

        def go(p, ph, k, src, dst, device):
            cp = remote(src, dst, ss.at[j, p * 3 + ph, k], rs.at[j, p * 3 + ph, k], device)
            cp.start()
            mine.append(cp)

        def got(p, ph, k, ref):
            remote(ref, ref, ss.at[j, p * 3 + ph, k], rs.at[j, p * 3 + ph, k], mate).wait_recv()

        for ph in range(3):
            for p in range(3):
                a = ORDERS[p][ph]
                i = here[a]
                g = parts[slot][p]
                bufs = [b.at[j] for b in recv[p, ph]]
                go(p, ph, 0, view(g, p, ph, i + 2, 0), bufs[0], step(a, 1))
                go(p, ph, 1, view(g, p, ph, i + 2, 1), bufs[1], step(a, -1))
            yield
            for p in range(3):
                a = ORDERS[p][ph]
                i = here[a]
                g = parts[slot][p]
                bufs = [b.at[j] for b in recv[p, ph]]
                got(p, ph, 0, bufs[0])
                add(view(g, p, ph, i + 1, 0), [bufs[0]])
                got(p, ph, 1, bufs[1])
                add(view(g, p, ph, i - 1, 1), [bufs[1]])
                go(p, ph, 2, view(g, p, ph, i + 1), bufs[2], step(a, 1))
                go(p, ph, 3, view(g, p, ph, i - 1), bufs[3], step(a, -1))
            yield
            for p in range(3):
                a = ORDERS[p][ph]
                i = here[a]
                g = parts[slot][p]
                bufs = [b.at[j] for b in recv[p, ph]]
                got(p, ph, 2, bufs[2])
                got(p, ph, 3, bufs[3])
                add(view(g, p, ph, i), [bufs[2], bufs[3]])
        outs = []
        for p in range(3):
            r = PART_ROWS[p]
            piece = parts[slot][p].at[zl, y, x, zh]
            val = piece[...]
            sq = val * val
            acc = tile[...]
            for t in range(r // 8):
                for u in range(2):
                    acc = acc + sq[8 * t : 8 * t + 8, 128 * u : 128 * u + 128]
            tile[...] = acc
            rows = pl.ds(pl.multiple_of(PART_BASE[p] + (x * 2 + zh) * r, 8), r)
            cp = pltpu.make_async_copy(piece, out.at[j, rows], oloc.at[j, p])
            cp.start()
            outs.append(cp)
            cp = remote(piece, out.at[j, rows], gss.at[j, p, 0], grs.at[j, p, 0], step("z", 2))
            cp.start()
            mine.append(cp)
        yield
        for cp in outs:
            cp.wait()

        def rows_of(p, xi, zi, n):
            r = PART_ROWS[p]
            return pl.ds(pl.multiple_of(PART_BASE[p] + (lax.rem(xi + 4, 4) * 2 + zi) * r, 8), n * r)

        def ago(p, k, rows, device):
            cp = remote(out.at[j, rows], out.at[j, rows], gss.at[j, p, k], grs.at[j, p, k], device)
            cp.start()
            mine.append(cp)

        def agot(p, k, rows):
            ref = out.at[j, rows]
            remote(ref, ref, gss.at[j, p, k], grs.at[j, p, k], mate).wait_recv()

        for p in range(3):
            agot(p, 0, rows_of(p, x, 1 - zh, 1))
            ago(p, 1, rows_of(p, x, 0, 2), step("x", 1))
            ago(p, 2, rows_of(p, x, 0, 2), step("x", -1))
        yield
        for p in range(3):
            agot(p, 1, rows_of(p, x - 1, 0, 2))
            agot(p, 2, rows_of(p, x + 1, 0, 2))
            ago(p, 3, rows_of(p, x - 1, 0, 1), step("x", 1))
            ago(p, 4, rows_of(p, x + 1, 1, 1), step("x", -1))
        yield
        for p in range(3):
            agot(p, 3, rows_of(p, x + 2, 0, 1))
            agot(p, 4, rows_of(p, x + 2, 1, 1))
        for cp in mine:
            cp.wait_send()

    tile[...] = extra[...]
    jobs = [job(j) for j in range(4)]
    waiting = {0: [0, 2], 1: [1, 3]}
    active = []
    for slot in (0, 1):
        active.append([slot, waiting[slot].pop(0)])
    while active:
        for entry in list(active):
            try:
                next(jobs[entry[1]])
            except StopIteration:
                if waiting[entry[0]]:
                    entry[1] = waiting[entry[0]].pop(0)
                    next(jobs[entry[1]])
                else:
                    active.remove(entry)
    k = 0
    for a in ("x", "y", "z"):
        cps = []
        for by in (1, 2, 3):
            cp = remote(tile, tiles.at[k], nss.at[k], nrs.at[k], step(a, by))
            cp.start()
            cps.append((cp, k))
            k += 1
        for cp, _ in cps:
            cp.wait()
        acc = tile[...]
        for _, i in cps:
            acc = acc + tiles[i]
        tile[...] = acc
    cp = remote(tile, tiles.at[k], nss.at[k], nrs.at[k], mate)
    cp.start()
    cp.wait()
    norm[...] = tile[...] + tiles[k]


def reduce_grads(grads, extra):
    dma = pltpu.SemaphoreType.DMA
    scratch = []
    for slot in range(2):
        for p in range(3):
            scratch.append(pltpu.VMEM((2, 4, 4, 2, PART_ROWS[p], 256), F32))
    for p in range(3):
        for ph in range(3):
            dims = cut_size(p, ph)
            name, one, two = halves(ORDERS[p], ph, PART_ROWS[p])
            for k in range(4):
                d = dict(dims)
                if k < 2:
                    sl = (one, two)[k]
                    d[name] = sl.stop - sl.start
                scratch.append(pltpu.VMEM((4, d["zl"], d["y"], d["x"], d["zh"], d["r"], 256), F32))
    scratch += [
        dma((4, 9, 4)),
        dma((4, 9, 4)),
        dma((2, 3, 8)),
        dma((4, 3, 5)),
        dma((4, 3, 5)),
        dma((4, 3)),
        pltpu.VMEM((8, 128), F32),
        pltpu.VMEM((10, 8, 128), F32),
        dma((10,)),
        dma((10,)),
    ]
    return pl.pallas_call(
        reduce_kernel,
        out_shape=(
            jax.ShapeDtypeStruct((4, 1024, 256), F32),
            jax.ShapeDtypeStruct((8, 128), F32),
        ),
        in_specs=[ANY] * 4 + [VM],
        out_specs=(ANY, VM),
        scratch_shapes=scratch,
        compiler_params=params(3, 62 * 2**20),
    )(*grads, extra)


def layer_norm(values):
    center = values - jnp.mean(values, -1, keepdims=True)
    spread = jnp.mean(center * center, -1, keepdims=True)
    return center * lax.rsqrt(spread + NORM_EPS)


def modulate(values, scale_row, shift_row):
    return layer_norm(values) * (1.0 + scale_row) + shift_row


def modulate_back(values, scale_row, shift_row, grad_out):
    _, pull_back = jax.vjp(modulate, values, scale_row, shift_row)
    return pull_back(grad_out)


def columns(h, w):
    return jnp.einsum("td,jdk->jtk", h, w, preferred_element_type=F32)


def rows_back(g, w):
    return jnp.einsum("jtk,jdk->td", g, w, preferred_element_type=F32)


def weight_grad(h, g):
    return jnp.einsum("td,jtk->jdk", h, g, preferred_element_type=F32)


def adamw(weight, first, second, grad, factor):
    clipped = grad * factor
    first_new = BETA_ONE * first + (1.0 - BETA_ONE) * clipped
    second_new = BETA_TWO * second + (1.0 - BETA_TWO) * clipped * clipped
    first_hat = first_new / (1.0 - BETA_ONE**STEP)
    second_hat = second_new / (1.0 - BETA_TWO**STEP)
    weight_new = weight - LEARN * (first_hat / (jnp.sqrt(second_hat) + ADAM_EPS) + DECAY * weight)
    return (weight_new, first_new, second_new)


def local(
    x_in, scale_ids, pad_mask, loss_weights, targets, labels,
    cond_w, attn_w, mlp_w, head_w, class_table, biases,
    first_cond, first_attn, first_mlp, first_head, first_table, first_bias,
    second_cond, second_attn, second_mlp, second_head, second_table, second_bias,
):
    dp = lax.axis_index("dp")
    core = dp % 2
    wb_cond = cond_w.astype(BF16)
    shard = jnp.stack([attn_w, mlp_w[0], mlp_w[1], head_w]).astype(BF16)

    count_part = jnp.sum(pad_mask.astype(F32))
    row = jnp.concatenate([labels.astype(F32), count_part[None], jnp.zeros((125,), F32)])
    msg = jnp.concatenate(
        [biases.astype(BF16).astype(F32).reshape(10, 128), row[None], jnp.zeros((5, 128), F32)]
    )
    level = jnp.where(pad_mask > 0, scale_ids, 1000).astype(F32)
    weight_own = (loss_weights * pad_mask).astype(F32)
    slots = jnp.concatenate(
        [level * 16.0 + scale_ids.astype(F32), targets.astype(F32), weight_own, jnp.zeros((2, 128), F32)]
    )
    msg_all, slots_all, cond_all, embedded, ada = condition(
        msg, slots, class_table.astype(BF16), wb_cond
    )
    w, wo = gather_weights(shard)
    w = w.reshape(8, 4, 1024, 256)

    bias_all = msg_all[:, :10].reshape(20480)
    b_q, b_v, b_proj, b_fc1, b_fc2, b_head = jnp.split(
        bias_all[8192:], [1024, 2048, 3072, 7168, 8192]
    )

    def own_columns(b):
        return lax.dynamic_index_in_dim(b.reshape(-1, 2, 256), core, 1, keepdims=False)

    slots_all = slots_all.reshape(8, 2, 8, 128)
    true_count = jnp.sum(slots_all[:, 0, 7, 0])
    ada_rows = jnp.transpose(ada, (1, 0, 2)).reshape(2, 1, 8192)
    g_a, g_m, s_a, s_m, t_a, t_m, s_h, t_h = jnp.split(ada_rows, 8, axis=2)
    sq_index = lax.axis_index("seq")
    pair_slots = lax.dynamic_index_in_dim(slots_all, sq_index, 0, keepdims=False)
    target_pair = pair_slots[:, 2:4].reshape(512).astype(jnp.int32)
    weight_pair = pair_slots[:, 4:6].reshape(512)
    owner = sq_index % 2
    levels = lax.dynamic_index_in_dim(slots_all, owner, 1, keepdims=False)[:, 0:2]
    levels = jnp.transpose(levels, (1, 0, 2)).reshape(2, 1024)
    key_level = jnp.floor(levels / 16.0)
    query_level = levels - key_level * 16.0

    x = x_in.astype(F32)
    h1 = modulate(x, s_a, t_a).astype(BF16).reshape(256, 1024)
    (h1,) = pair_gather(4, h1)
    h1 = h1.reshape(512, 1024)
    bias_qkv = jnp.concatenate([own_columns(b_q), jnp.zeros((2, 256), F32), own_columns(b_v)])
    qkv = (columns(h1, w[:6, 0]) + bias_qkv[:, None, :]).astype(BF16)
    blocks = qkv.reshape(3, 2, 2, 256, 2, 128).transpose(1, 4, 2, 0, 3, 5).reshape(8, 3, 256, 128)
    heads = all_to_all(5, blocks)

    def by_head(block):
        return block.reshape(8, 2, 128, 2, 64).transpose(1, 3, 0, 2, 4).reshape(2, 2, 1024, 64)

    def from_head(block):
        return block.reshape(2, 2, 8, 128, 64).transpose(2, 0, 3, 1, 4).reshape(8, 256, 128)

    q, k, v = (by_head(heads[:, i]) for i in range(3))
    visible = (key_level[:, None, None, :] <= query_level[:, None, :, None])
    scores = jnp.einsum("ihqd,ihkd->ihqk", q, k, preferred_element_type=F32) * SCORE_SCALE
    probs = jax.nn.softmax(jnp.where(visible, scores, -1e30), axis=-1)
    probs_low = probs.astype(BF16)
    o = jnp.einsum("ihqk,ihkd->ihqd", probs_low, v, preferred_element_type=F32).astype(BF16)
    o = to_tokens(6, from_head(o))
    att = jnp.einsum("td,jdk->tjk", o, wo, preferred_element_type=F32).reshape(256, 1024) + b_proj
    att = att.reshape(2, 128, 1024)
    x1 = x + g_a * att
    h2 = modulate(x1, s_m, t_m).astype(BF16).reshape(256, 1024)
    (h2,) = pair_gather(7, h2)
    h2 = h2.reshape(512, 1024)
    f = columns(h2, w[:, 1]) + own_columns(b_fc1)[:, None, :]
    u = jax.nn.gelu(f, approximate=True).astype(BF16)
    mlp = swap_add(8, rows_back(u, w[:, 2]).reshape(2, 256, 1024)) + b_fc2
    mlp = mlp.reshape(2, 128, 1024)
    x2 = x1 + g_m * mlp
    h3 = modulate(x2, s_h, t_h).astype(BF16).reshape(256, 1024)
    (h3,) = pair_gather(9, h3)
    h3 = h3.reshape(512, 1024)
    logits = columns(h3, w[:, 3]) + own_columns(b_head)[:, None, :]
    top = jnp.max(logits, axis=(0, 2))
    mass = jnp.sum(jnp.exp(logits - top[None, :, None]), axis=(0, 2))
    column = (
        (2 * jnp.arange(8)[:, None] + core) * 256 + jnp.arange(256)[None, :]
    )
    target_hit = target_pair[None, :, None] == column[:, None, :]
    picked = jnp.sum(jnp.where(target_hit, logits, 0.0), axis=(0, 2))
    stats = jnp.stack([top, mass, picked]).reshape(3, 4, 128)
    (stats,) = pair_gather(10, stats)
    stats = stats.reshape(2, 3, 512)
    top_all = jnp.max(stats[:, 0], axis=0)
    mass_all = jnp.sum(stats[:, 1] * jnp.exp(stats[:, 0] - top_all[None]), axis=0)
    log_total = top_all + jnp.log(mass_all)
    picked_all = jnp.sum(stats[:, 2], axis=0)
    loss_part = 0.5 * jnp.sum(weight_pair * (log_total - picked_all))
    dlogits = (
        (weight_pair / true_count)[None, :, None]
        * (jnp.exp(logits - log_total[None, :, None]) - target_hit.astype(F32))
    ).astype(BF16)

    grad_head = weight_grad(h3, dlogits)
    db_head = jnp.sum(dlogits.astype(F32), axis=1)
    dh3 = swap_add(11, rows_back(dlogits, w[:, 3]).reshape(2, 256, 1024)).reshape(2, 128, 1024)
    dx2, ds_h, dt_h = modulate_back(x2, s_h, t_h, dh3)
    dg_m = jnp.sum(dx2 * mlp, axis=1, keepdims=True)
    dmlp = (g_m * dx2).astype(BF16).reshape(256, 1024)
    db_fc2 = jnp.sum(dmlp.astype(F32), axis=0)
    (dmlp,) = pair_gather(12, dmlp)
    dmlp = dmlp.reshape(512, 1024)
    grad_two = weight_grad(dmlp, u)
    du = columns(dmlp, w[:, 2])
    _, gelu_back = jax.vjp(functools.partial(jax.nn.gelu, approximate=True), f)
    df = gelu_back(du)[0].astype(BF16)
    grad_one = weight_grad(h2, df)
    db_fc1 = jnp.sum(df.astype(F32), axis=1)
    dh2 = swap_add(13, rows_back(df, w[:, 1]).reshape(2, 256, 1024)).reshape(2, 128, 1024)
    dx1, ds_m, dt_m = modulate_back(x1, s_m, t_m, dh2)
    dx1 = dx1 + dx2
    dg_a = jnp.sum(dx1 * att, axis=1, keepdims=True)
    datt = (g_a * dx1).astype(BF16).reshape(256, 1024)
    db_proj = jnp.sum(datt.astype(F32), axis=0)
    do = jnp.einsum(
        "tjk,jdk->td", datt.reshape(256, 4, 256), wo, preferred_element_type=F32
    ).astype(BF16)
    do_heads = by_head(to_heads(14, do))
    o_pair, datt_pair = pair_gather(15, o, datt)
    datt_own = lax.dynamic_index_in_dim(
        datt_pair.reshape(512, 2, 2, 256), core, 2, keepdims=False
    )
    grad_o = jnp.einsum(
        "td,tjk->jdk", o_pair.reshape(512, 1024), datt_own, preferred_element_type=F32
    )
    dprobs = jnp.einsum("ihqd,ihkd->ihqk", do_heads, v, preferred_element_type=F32)
    inner = jnp.sum(probs * dprobs, axis=-1, keepdims=True)
    dscores = (probs * (dprobs - inner)).astype(BF16)
    dq = jnp.einsum("ihqk,ihkd->ihqd", dscores, k, preferred_element_type=F32) * SCORE_SCALE
    dk = jnp.einsum("ihqk,ihqd->ihkd", dscores, q, preferred_element_type=F32) * SCORE_SCALE
    dv = jnp.einsum("ihqk,ihqd->ihkd", probs_low, do_heads, preferred_element_type=F32)
    dqkv = jnp.stack([from_head(t.astype(BF16)) for t in (dq, dk, dv)], axis=1)
    dqkv = all_to_all(16, dqkv)
    dqkv = dqkv.reshape(2, 2, 2, 3, 256, 128).transpose(3, 0, 2, 4, 1, 5).reshape(6, 512, 256)
    grad_qkv = weight_grad(h1, dqkv)
    db_qkv = jnp.sum(dqkv.astype(F32), axis=1)
    dh1 = swap_add(17, rows_back(dqkv, w[:6, 0]).reshape(2, 256, 1024)).reshape(2, 128, 1024)
    _, ds_a, dt_a = modulate_back(x, s_a, t_a, dh1)
    dada = jnp.concatenate([dg_a, dg_m, ds_a, ds_m, dt_a, dt_m, ds_h, dt_h], axis=2)[:, 0]

    def spread_columns(b):
        mine = jnp.arange(2)[None, :, None] == core
        return jnp.where(mine, b[:, None, :], 0.0).reshape(-1)

    bias_part = jnp.concatenate(
        [
            jnp.sum(dada, axis=0),
            spread_columns(db_qkv[0:2]),
            spread_columns(db_qkv[4:6]),
            db_proj,
            spread_columns(db_fc1),
            db_fc2,
            spread_columns(db_head),
        ]
    ).reshape(16, 10, 128)
    ada_msg = dada.reshape(2, 16, 512).transpose(1, 0, 2).reshape(16, 8, 128)
    tail = jnp.concatenate([jnp.full((16, 1, 128), loss_part), jnp.zeros((16, 5, 128), F32)], axis=1)
    dada_all, bias_sum, dcond = small_reduce(
        jnp.concatenate([ada_msg, bias_part, tail], axis=1), wb_cond
    )
    bias_sum = bias_sum.reshape(16, 128)
    loss_total = bias_sum[10, 0]
    grad_bias = bias_sum[:10].reshape(1280)
    cond_full = jnp.transpose(cond_all, (1, 0, 2)).reshape(32, 1024).astype(F32)
    grad_cond = lax.dot_general(
        cond_full, dada_all, (((0,), (0,)), ((), ())), precision=HIGH, preferred_element_type=F32
    )
    _, silu_back = jax.vjp(jax.nn.silu, embedded)
    demb = silu_back(dcond)[0]
    labels_all = msg_all[:, 10, 0:2].reshape(32).astype(jnp.int32)
    class_hit = (labels_all[:, None] == jnp.arange(class_table.shape[0])[None, :]).astype(F32)
    grad_table = lax.dot_general(
        class_hit, demb, (((0,), (0,)), ((), ())), precision=HIGH, preferred_element_type=F32
    )
    own_squares = (
        jnp.sum(grad_cond * grad_cond) + jnp.sum(grad_table * grad_table) + jnp.sum(grad_bias * grad_bias)
    ) / 8.0
    extra = jnp.zeros((8, 128), F32).at[0, 0].set(own_squares)
    grad_attn = jnp.concatenate([grad_qkv, grad_o])
    shape = (2, 4, 1024, 256)
    summed, squares = reduce_grads(
        [g.reshape(shape) for g in (grad_attn, grad_one, grad_two, grad_head)], extra
    )
    grad_norm = jnp.sqrt(jnp.sum(squares))
    factor = jnp.minimum(1.0, CLIP / grad_norm)
    grads = (grad_cond, summed[0], summed[1:3], summed[3], grad_table, grad_bias)
    weights = (cond_w, attn_w, mlp_w, head_w, class_table, biases)
    firsts = (first_cond, first_attn, first_mlp, first_head, first_table, first_bias)
    seconds = (second_cond, second_attn, second_mlp, second_head, second_table, second_bias)
    results = [
        adamw(weight, first, second, grad, factor)
        for weight, first, second, grad in zip(weights, firsts, seconds, grads)
    ]
    new_weights = [entry[0] for entry in results]
    new_first = [entry[1] for entry in results]
    new_second = [entry[2] for entry in results]
    copies = [weight.astype(BF16) for weight in new_weights]
    return tuple(new_weights + new_first + new_second + copies + [grad_norm, loss_total, true_count])


def solution(mesh):
    split = (P(None, "dp"), P(None, "dp"), P(None, None, "dp"), P(None, "dp"), P(None, "dp"), P("dp"))
    in_specs = (P("dp", "seq", None),) + (P("dp", "seq"),) * 4 + (P("dp"),) + split * 3
    out_specs = split * 4 + (P(), P(), P())
    return jax.shard_map(local, mesh=mesh, in_specs=in_specs, out_specs=out_specs, check_vma=False)
```

time: 2070 us -> 913 us (0.44)
  waiting for transfers between devices: 1520 us -> 0 us
  Pallas kernels: 0 us -> 621 us
  blocking collectives: 197 us -> 0 us
  matrix products: 187 us -> 127 us
  local copies, waits for them, and re-layouts: 48.8 us -> 74.9 us
    reduce_scatter x7 -> x0, waiting for transfers between devices: 766 us -> none  [the longest x1 184 us: local(): lax.psum_scatter(sum_cond, 'dp', scatter_dimension=1, tiled=True)]
    pallas_call x0 -> x18, Pallas kernels: none -> 621 us  [the longest x1 224 us: reduce_grads(): pl.pallas_call(reduce_kernel, out_shape=(jax.ShapeDtypeStruct((4, 1024, 2...]
    all_gather x7 -> x0, waiting for transfers between devices: 388 us -> none  [the longest x1 91.7 us: local(): lax.all_gather(cond_w.astype(jnp.bfloat16), 'dp', axis=1, tiled=True)]
    psum x1 -> x0, waiting for transfers between devices: 258 us -> none  [local(): lax.psum((grad_cond, grad_attn, grad_mlp, grad_head, grad_table, grad_bia...]
    psum x3 -> x0, blocking collectives: 156 us -> none  [the longest x1 70.3 us: local(): lax.psum((loss_local, local_squares), ('dp', 'seq'))]
    unnamed x17 -> x0, waiting for transfers between devices: 110 us -> none
    dot_general x25 -> x22, matrix products: 176 us -> 115 us  [the longest x4 28.3 us: columns(): return jnp.einsum('td,jdk->jtk', h, w, preferred_element_type=F32)]
    all_gather x2 -> x0, blocking collectives: 41 us -> none  [the longest x1 22 us: local(): lax.all_gather(biases.astype(jnp.bfloat16), 'dp', axis=0, tiled=True)]
  transfers between devices with their start and end apart: 16 -> 0, of which waited for: 16 -> 0; matrix products, arithmetic and copies ran while one was open for 8% -> 0% of each run, Pallas kernels for 0% -> 0%
where the time goes in v1:
time: 913 us; the launch traced here: 907 us
  Pallas kernels  621 us (68%)
  matrix products  127 us (14%)
  other arithmetic  76.9 us (8%)
  local copies, waits for them, and re-layouts  74.9 us (8%)
    pallas_call x1, Pallas kernels, reduce_grads(): pl.pallas_call(reduce_kernel, out_shape=(jax.ShapeDtypeStruct((4, 1024, 2...  224 us
    pallas_call x1, Pallas kernels, gather_weights(): pl.pallas_call(gather_kernel, out_shape=(jax.ShapeDtypeStruct((2, 4, 4, 1...  151 us
    pallas_call x6, Pallas kernels, pair_gather(): pl.pallas_call(functools.partial(pair_kernel, n), out_shape=tuple((jax.Sh...  104 us
    pallas_call x2, Pallas kernels, all_to_all(): pl.pallas_call(a2a_kernel, out_shape=jax.ShapeDtypeStruct(a.shape, a.dtyp...  45.9 us
    pallas_call x1, Pallas kernels, small_reduce(): pl.pallas_call(small_kernel, out_shape=(jax.ShapeDtypeStruct((32, 512), F...  30.1 us
    dot_general x4, matrix products, columns(): return jnp.einsum('td,jdk->jtk', h, w, preferred_element_type=F32)  28.3 us
    transpose x3, local copies, waits for them, and re-layouts, weight_grad(): return jnp.einsum('td,jtk->jdk', h, g, preferred_element_type=F32)  27.8 us
    dot_general x4, matrix products, weight_grad(): return jnp.einsum('td,jtk->jdk', h, g, preferred_element_type=F32)  25.6 us

profile of v1, /device:TPU:1, one launch (start us, length us, event | category | flops | bytes accessed | tf_op | source)
XLA Modules:
  0.0 906.8 jit_solution(12750485642293975048)
XLA Ops:
  7.5 2.8 convert_element_type.164.cond_w
  12.2 25.5 %shard_map.439 = (f32[16,16,128]{2,1,0:T(8,128)}, f32[16,8,128]{2,1,0:T(8,128)}, bf16[16,32,64]{2,1,0:T(8,128)(2,1)}, f32[32,64]{1,0:T(8,128)}, f32[16,2,512]{2,1,0:T(2,128)}) custom-call(f32[16,128]{1,0:T(8,128)} %maximum_maximum_fusion.1.msg, f32[8,128]{1,0:T(8,128)} %maximum_maximum_fusion.2.slots, bf16[1000,64]{1,0:T(8,128)(2,1)} %copy.307.table, ...), custom_call_target="tpu_custom_call" | custom-call | tf_op jit(solution)/shard_map/pallas_call | solution.py:471
  41.3 17.4 %shard_map.441 = bf16[2,256,1024]{2,1,0:T(8,128)(2,1)} custom-call(bf16[256,1024]{1,0:T(8,128)(2,1)} %bitcast.492), custom_call_target="tpu_custom_call" | custom-call | tf_op jit(solution)/shard_map/pallas_call | solution.py:196
  58.9 1.8 convert.13
  60.7 1.6 pad_maximum_fusion.1.s
  62.3 150.5 %shard_map.440 = (bf16[2,4,4,1024,256]{4,3,2,1,0:T(8,128)(2,1)}, bf16[4,1024,256]{2,1,0:T(8,128)(2,1)}) custom-call(bf16[4,1024,256]{2,1,0:T(8,128)(2,1)} %pad_maximum_fusion.1.s), custom_call_target="tpu_custom_call" | custom-call | tf_op jit(solution)/shard_map/pallas_call | solution.py:159
  212.8 5.0 fusion.98
  217.8 2.5 reshape.476
  220.3 2.8 copy.312
  223.1 19.9 %shard_map.442 = bf16[8,3,256,128]{3,2,1,0:T(8,128)(2,1)} custom-call(bf16[8,3,256,128]{3,2,1,0:T(8,128)(2,1)} %bitcast.488), custom_call_target="tpu_custom_call" | custom-call | tf_op jit(solution)/shard_map/pallas_call | solution.py:261
  243.0 1.5 fusion.175
  246.5 2.3 broadcast_compare_fusion
  248.8 11.3 %fusion.180 = (f32[2,2,1024]{2,1,0:T(2,128)S(1)}, f32[2,2,1024,1024]{2,3,1,0:T(8,128)}) fusion(pred[2,1024,1024]{1,2,0:T(8,128)(4,1)} %broadcast_compare_fusion, bf16[2,2,1024,64]{2,3,1,0:T(8,128)(2,1)S(1)} %reshape.478, bf16[2,2,1024,64]{2,3,1,0:T(8,128)(2,1)S(1)} %reshape.479), kind=kOutput, calls=%fused_computation.320 | convolution fusion | flops 553649152 | bytes 19939328 | tf_op jit(solution)/shard_map/sub | solution.py:962
  261.0 7.5 fusion.101
  270.6 16.5 %shard_map.443.refs_0_ = bf16[256,1024]{1,0:T(8,128)(2,1)} custom-call(bf16[8,256,128]{2,1,0:T(8,128)(2,1)} %copy.321.a), custom_call_target="tpu_custom_call" | custom-call | tf_op jit(solution)/shard_map/pallas_call | solution.py:327
  287.1 2.5 fusion.121
  292.5 17.4 %shard_map.444 = bf16[2,256,1024]{2,1,0:T(8,128)(2,1)} custom-call(bf16[256,1024]{1,0:T(8,128)(2,1)} %bitcast.494), custom_call_target="tpu_custom_call" | custom-call | tf_op jit(solution)/shard_map/pallas_call | solution.py:196
  309.9 8.0 fusion.47
  318.0 5.1 fusion.80.a
  323.0 2.9 shard_map.445
  327.6 17.1 %shard_map.446 = bf16[2,256,1024]{2,1,0:T(8,128)(2,1)} custom-call(bf16[256,1024]{1,0:T(8,128)(2,1)} %bitcast.495), custom_call_target="tpu_custom_call" | custom-call | tf_op jit(solution)/shard_map/pallas_call | solution.py:196
  344.8 7.1 add_reduce_fusion
  351.9 2.9 fusion.45
  355.4 1.7 shard_map.447
  359.8 2.9 fusion.43
  362.7 4.6 fusion.85.a
  367.3 2.9 shard_map.448
  373.0 17.2 %shard_map.449 = bf16[2,256,1024]{2,1,0:T(8,128)(2,1)} custom-call(bf16[256,1024]{1,0:T(8,128)(2,1)} %bitcast.497), custom_call_target="tpu_custom_call" | custom-call | tf_op jit(solution)/shard_map/pallas_call | solution.py:196
  390.2 8.2 fusion.15
  398.5 4.7 convert_reduce_fusion.1
  403.2 1.7 convert_reduce_fusion
  405.0 4.6 fusion.90.a
  409.7 2.9 shard_map.450
  414.4 3.2 fusion.107.a
  417.6 13.3 %shard_map.451 = bf16[8,256,128]{2,1,0:T(8,128)(2,1)} custom-call(bf16[256,1024]{1,0:T(8,128)(2,1)} %fusion.107.a), custom_call_target="tpu_custom_call" | custom-call | tf_op jit(solution)/shard_map/pallas_call | solution.py:390
  432.9 7.5 multiply_reduce_fusion
  440.4 8.2 multiply_convert_fusion
  448.7 1.6 fusion.109
  450.3 1.6 copy-done
  453.1 6.0 fusion.108
  460.5 8.4 fusion.104
  471.5 26.0 %shard_map.452 = bf16[8,3,256,128]{3,2,1,0:T(8,128)(2,1)} custom-call(bf16[8,3,256,128]{3,2,1,0:T(8,128)(2,1)} %pad_maximum_fusion.2.a), custom_call_target="tpu_custom_call" | custom-call | tf_op jit(solution)/shard_map/pallas_call | solution.py:261
  497.5 1.6 convert_reduce_fusion.2
  499.2 3.0 copy.344
  503.5 4.3 fusion.95.a
  507.9 2.9 shard_map.453
  513.0 30.1 %shard_map.454 = (f32[32,512]{1,0:T(8,128)}, f32[2,8,128]{2,1,0:T(8,128)}, f32[32,64]{1,0:T(8,128)}) custom-call(f32[16,24,128]{2,1,0:T(8,128)} %maximum_maximum_fusion.msg, bf16[1024,512]{1,0:T(8,128)(2,1)} %convert_element_type.164.cond_w), custom_call_target="tpu_custom_call" | custom-call | tf_op jit(solution)/shard_map/pallas_call | solution.py:549
  543.3 1.7 multiply_reduce_fusion.10
  545.2 3.8 multiply_reduce_fusion.1
  552.9 8.2 convolution_bitcast_fusion
  561.0 9.3 %copy.353 = f32[8,1024,256]{2,1,0:T(8,128)} copy(f32[8,1024,256]{1,2,0:T(8,128)} %convolution_bitcast_fusion) | data formatting | bytes 16777216 | tf_op jit(solution)/shard_map/td,jtk->jdk/transpose | solution.py:882
  570.3 5.6 convolution_bitcast_fusion.2
  575.9 9.4 %copy.351 = f32[8,1024,256]{2,1,0:T(8,128)} copy(f32[8,1024,256]{1,2,0:T(8,128)} %convolution_bitcast_fusion.2) | data formatting | bytes 16777216 | tf_op jit(solution)/shard_map/td,jtk->jdk/transpose | solution.py:882
  585.3 8.4 convolution_bitcast_fusion.1
  593.7 9.1 %copy.352 = f32[8,1024,256]{2,1,0:T(8,128)} copy(f32[8,1024,256]{1,2,0:T(8,128)} %convolution_bitcast_fusion.1) | data formatting | bytes 16777216 | tf_op jit(solution)/shard_map/td,jtk->jdk/transpose | solution.py:882
  602.8 33.3 %shard_map.455 = (bf16[2,256,1024]{2,1,0:T(8,128)(2,1)}, bf16[2,256,1024]{2,1,0:T(8,128)(2,1)}) custom-call(bf16[256,1024]{1,0:T(8,128)(2,1)} %shard_map.443.refs_0_, bf16[256,1024]{1,0:T(8,128)(2,1)} %bitcast.489), custom_call_target="tpu_custom_call" | custom-call | tf_op jit(solution)/shard_map/pallas_call | solution.py:196
  636.1 1.9 reshape.512
  641.2 3.5 convolution_bitcast_fusion.3
  644.7 4.3 pad_maximum_fusion
  649.0 9.1 %copy.350 = f32[8,1024,256]{2,1,0:T(8,128)} copy(f32[8,1024,256]{1,2,0:T(8,128)} %pad_maximum_fusion) | data formatting | bytes 16777216 | tf_op jit(solution)/shard_map/concatenate | solution.py:1086
  658.2 223.6 %shard_map.456 = (f32[4,1024,256]{2,1,0:T(8,128)}, f32[8,128]{1,0:T(8,128)}) custom-call(f32[2,4,1024,256]{3,2,1,0:T(8,128)} %bitcast.485, f32[2,4,1024,256]{3,2,1,0:T(8,128)} %bitcast.483, f32[2,4,1024,256]{3,2,1,0:T(8,128)} %bitcast.484, f32[2,4,1024,256]{3,2,1,0:T(8,128)} %bitcast.482, f32[8,128]{1,0:T(8,128)} %scatter.4.refs_4_), custom_call_target="tpu_custom_call" | custom-call | tf_op jit(solution)/shard_map/pallas_call | solution.py:845
  885.6 8.0 fusion.163
  894.4 4.1 fusion.161
  900.5 4.2 fusion.167
  (261 shorter events, 51.0 us)
Async XLA Ops:
  0.7 39.1 %copy-start.2 = (bf16[2,128,1024]{2,1,0:T(8,128)(2,1)S(1)}, bf16[2,128,1024]{2,1,0:T(8,128)(2,1)}, u32[]{:S(2)}) copy-start(bf16[2,128,1024]{2,1,0:T(8,128)(2,1)} %param.26) | copy-start | bytes 1572868
  3.5 0.5 copy-start.53
  7.5 51.2 %copy-start.13 = (f32[1024,256]{1,0:T(8,128)S(1)}, f32[1024,256]{1,0:T(8,128)}, u32[]{:S(2)}) copy-start(f32[1024,256]{1,0:T(8,128)} %param.35) | copy-start | bytes 3145732
  7.5 51.2 %copy-start.15 = (f32[1024,256]{1,0:T(8,128)S(1)}, f32[1024,256]{1,0:T(8,128)}, u32[]{:S(2)}) copy-start(f32[1024,256]{1,0:T(8,128)} %param.33) | copy-start | bytes 3145732
  39.9 20.7 %copy-start.47 = (f32[2,128]{1,0:T(2,128)}, f32[2,128]{1,0:T(2,128)S(1)}, u32[]{:S(2)}) copy-start(f32[2,128]{1,0:T(2,128)S(1)} %broadcast_multiply_fusion.2) | copy-start | bytes 3076
  40.2 20.4 %copy-start.49 = (f32[2,128]{1,0:T(2,128)}, f32[2,128]{1,0:T(2,128)S(1)}, u32[]{:S(2)}) copy-start(f32[2,128]{1,0:T(2,128)S(1)} %add_rsqrt_fusion) | copy-start | bytes 3076
  58.9 153.9 %copy-start.31 = (bf16[2,256,1024]{2,1,0:T(8,128)(2,1)S(1)}, bf16[2,256,1024]{2,1,0:T(8,128)(2,1)}, u32[]{:S(2)}) copy-start(bf16[2,256,1024]{2,1,0:T(8,128)(2,1)} %shard_map.441) | copy-start | bytes 3145732
  244.5 1.9 copy-start.45
  245.4 14.6 %copy-start.20 = (bf16[2,2,1024,64]{2,3,1,0:T(8,128)(2,1)}, bf16[2,2,1024,64]{2,3,1,0:T(8,128)(2,1)S(1)}, u32[]{:S(2)}) copy-start(bf16[2,2,1024,64]{2,3,1,0:T(8,128)(2,1)S(1)} %reshape.478) | copy-start | bytes 1572868
  246.4 13.7 %copy-start.22 = (bf16[2,2,1024,64]{2,3,1,0:T(8,128)(2,1)}, bf16[2,2,1024,64]{2,3,1,0:T(8,128)(2,1)S(1)}, u32[]{:S(2)}) copy-start(bf16[2,2,1024,64]{2,3,1,0:T(8,128)(2,1)S(1)} %reshape.479) | copy-start | bytes 1572868
  261.0 7.6 copy-start.36
  287.1 3.8 copy-start.35
  290.8 27.1 %copy-start.4 = (f32[2,128,1024]{2,1,0:T(8,128)}, f32[2,128,1024]{2,1,0:T(8,128)S(1)}, u32[]{:S(2)}) copy-start(f32[2,128,1024]{2,1,0:T(8,128)S(1)} %reshape.483) | copy-start | bytes 3145732
  371.0 1.0 copy-start.6
  390.2 8.2 copy-start.11
  398.4 4.8 copy-start.1
  409.6 3.7 copy-start.5
  409.6 3.7 copy-start.7
  414.0 18.7 %copy-start.10 = (bf16[2,128,1024]{2,1,0:T(8,128)(2,1)}, bf16[2,128,1024]{2,1,0:T(8,128)(2,1)S(1)}, u32[]{:S(2)}) copy-start(bf16[2,128,1024]{2,1,0:T(8,128)(2,1)S(1)} %get-tuple-element.112) | copy-start | bytes 1572868
  414.4 18.5 %copy-start.37 = (bf16[2,2,1024,64]{2,3,1,0:T(8,128)(2,1)S(1)}, bf16[2,2,1024,64]{2,3,1,0:T(8,128)(2,1)}, u32[]{:S(2)}) copy-start(bf16[2,2,1024,64]{2,3,1,0:T(8,128)(2,1)} %copy-done.36) | copy-start | bytes 1572868
  432.9 7.5 copy-start.38
  440.4 8.2 copy-start.23
  448.7 3.2 copy-start
  451.9 1.3 copy-start.21
  459.2 1.3 copy-start.39
  503.5 4.4 copy-start.24
  503.5 7.3 copy-start.3
  503.5 7.3 copy-start.48
  503.5 7.3 copy-start.50
  507.8 4.4 copy-start.54
  507.8 35.5 %copy-start.46 = (f32[32,64]{1,0:T(8,128)S(1)}, f32[32,64]{1,0:T(8,128)}, u32[]{:S(2)}) copy-start(f32[32,64]{1,0:T(8,128)} %get-tuple-element.63) | copy-start | bytes 24580
  507.9 37.2 %copy-start.42 = (bf16[16,32,64]{2,1,0:T(8,128)(2,1)S(1)}, bf16[16,32,64]{2,1,0:T(8,128)(2,1)}, u32[]{:S(2)}) copy-start(bf16[16,32,64]{2,1,0:T(8,128)(2,1)} %get-tuple-element.53) | copy-start | bytes 196612
  510.8 42.1 %copy-start.33 = (bf16[2,256,1024]{2,1,0:T(8,128)(2,1)S(1)}, bf16[2,256,1024]{2,1,0:T(8,128)(2,1)}, u32[]{:S(2)}) copy-start(bf16[2,256,1024]{2,1,0:T(8,128)(2,1)} %shard_map.446) | copy-start | bytes 3145732
  561.0 9.3 %copy-start.19 = (bf16[8,512,256]{1,2,0:T(8,128)(2,1)S(1)}, bf16[8,512,256]{1,2,0:T(8,128)(2,1)}, u32[]{:S(2)}) copy-start(bf16[8,512,256]{1,2,0:T(8,128)(2,1)} %get-tuple-element.110) | copy-start | bytes 6291460
  561.0 9.3 %copy-start.32 = (bf16[2,256,1024]{2,1,0:T(8,128)(2,1)S(1)}, bf16[2,256,1024]{2,1,0:T(8,128)(2,1)}, u32[]{:S(2)}) copy-start(bf16[2,256,1024]{2,1,0:T(8,128)(2,1)} %shard_map.444) | copy-start | bytes 3145732
  575.9 9.4 %copy-start.34 = (bf16[2,256,1024]{2,1,0:T(8,128)(2,1)S(1)}, bf16[2,256,1024]{2,1,0:T(8,128)(2,1)}, u32[]{:S(2)}) copy-start(bf16[2,256,1024]{2,1,0:T(8,128)(2,1)} %shard_map.449) | copy-start | bytes 3145732
  636.1 4.4 copy-start.29
  658.1 225.6 %copy-start.43 = (f32[1280]{0:T(1024)S(1)}, f32[1280]{0:T(1024)}, u32[]{:S(2)}) copy-start(f32[1280]{0:T(1024)} %param.37) | copy-start | bytes 15364
  658.1 225.6 %copy-start.44 = (f32[2,8,128]{2,1,0:T(8,128)S(1)}, f32[2,8,128]{2,1,0:T(8,128)}, u32[]{:S(2)}) copy-start(f32[2,8,128]{2,1,0:T(8,128)} %get-tuple-element.64) | copy-start | bytes 24580
  658.1 225.6 %copy-start.51 = (f32[1280]{0:T(1024)S(1)}, f32[1280]{0:T(1024)}, u32[]{:S(2)}) copy-start(f32[1280]{0:T(1024)} %param.43) | copy-start | bytes 15364
  658.1 225.7 %copy-start.52 = (f32[1280]{0:T(1024)S(1)}, f32[1280]{0:T(1024)}, u32[]{:S(2)}) copy-start(f32[1280]{0:T(1024)} %param.49) | copy-start | bytes 15364
  658.1 226.3 %copy-start.30 = (f32[1000,64]{0,1:T(8,128)S(1)}, f32[1000,64]{0,1:T(8,128)}, u32[]{:S(2)}) copy-start(f32[1000,64]{0,1:T(8,128)} %param.36) | copy-start | bytes 768004
  658.2 226.3 %copy-start.40 = (f32[1000,64]{0,1:T(8,128)S(1)}, f32[1000,64]{0,1:T(8,128)}, u32[]{:S(2)}) copy-start(f32[1000,64]{0,1:T(8,128)} %param.42) | copy-start | bytes 768004
  658.2 226.3 %copy-start.41 = (f32[1000,64]{0,1:T(8,128)S(1)}, f32[1000,64]{0,1:T(8,128)}, u32[]{:S(2)}) copy-start(f32[1000,64]{0,1:T(8,128)} %param.48) | copy-start | bytes 768004
  885.5 8.1 copy-start.12
  885.5 8.1 copy-start.14
  885.5 8.1 copy-start.16
  885.5 8.1 copy-start.25
  885.5 8.1 copy-start.26
  885.5 8.1 copy-start.27
  885.5 8.9 copy-start.28
  894.4 4.1 copy-start.8
  894.4 4.2 copy-start.9
  894.4 5.4 copy-start.17
  894.4 6.0 copy-start.18

commit v2 on v1

--- a/solution.py
+++ b/solution.py
@@ -64,129 +64,19 @@
     )
 
 
-def gather_kernel(s, w, wo, ss, rs, loc, os, orr):
-    x, y, z, c = place()
-    zl = lax.rem(z, 2)
-    up, down = lax.rem(y + 1, 4), lax.rem(y + 3, 4)
-    side = 1 - 2 * c
-    yp, ym = at(x, y + 1, z, c), at(x, y - 1, z, c)
-    zp, zm = at(x, y, z + 1, c), at(x, y, z - 1, c)
-    xp, xm = at(x + 1, y, z, c), at(x - 1, y, z, c)
-    zs = at(x, y, z + side, c)
-    mate = at(x, y, z, 1 - c)
-    greet([yp, ym, zp, zm, xp, xm, mate])
-
-    def quarter(pos):
-        return pl.ds(pl.multiple_of(ROWS_YZ + QUARTER * lax.rem(pos + 4, 4), 16), QUARTER)
-
-    mine = quarter(x)
-    full, first, second = pl.ds(0, ROWS_YZ), pl.ds(0, HALF_YZ), pl.ds(HALF_YZ, HALF_YZ)
-    order = (0, 1, 2, 3)
-    sent = []
-
-    def go(j, k, src, dst, device):
-        cp = remote(src, dst, ss.at[j, k], rs.at[j, k], device)
-        cp.start()
-        sent.append(cp)
-
-    def got(j, k, ref):
-        remote(ref, ref, ss.at[j, k], rs.at[j, k], mate).wait_recv()
-
-    locals_ = []
-    for j in order:
-        go(j, 0, s.at[j, full], w.at[zl, y, j, full], yp)
-        go(j, 1, s.at[j, full], w.at[zl, y, j, full], ym)
-        go(j, 6, s.at[j, mine], w.at[zl, y, j, mine], zs)
-        for i, rows in enumerate((full, mine)):
-            cp = pltpu.make_async_copy(s.at[j, rows], w.at[zl, y, j, rows], loc.at[j, i])
-            cp.start()
-            locals_.append(cp)
-    for cp in locals_:
-        cp.wait()
-    for j in order:
-        got(j, 6, w.at[1 - zl, y, j, mine])
-        go(j, 7, w.at[:, y, j, mine], w.at[:, y, j, mine], yp)
-        go(j, 8, w.at[:, y, j, mine], w.at[:, y, j, mine], ym)
-        got(j, 0, w.at[zl, down, j, full])
-        got(j, 1, w.at[zl, up, j, full])
-        go(j, 2, w.at[zl, down, j, first], w.at[zl, down, j, first], yp)
-        go(j, 3, w.at[zl, up, j, second], w.at[zl, up, j, second], ym)
-    for j in order:
-        got(j, 7, w.at[:, down, j, mine])
-        got(j, 8, w.at[:, up, j, mine])
-        go(j, 9, w.at[0, down, j, mine], w.at[0, down, j, mine], yp)
-        go(j, 10, w.at[1, up, j, mine], w.at[1, up, j, mine], ym)
-        far = lax.rem(y + 2, 4)
-        got(j, 2, w.at[zl, far, j, first])
-        got(j, 3, w.at[zl, far, j, second])
-        go(j, 4, w.at[zl, :, j, first], w.at[zl, :, j, first], zp)
-        go(j, 5, w.at[zl, :, j, second], w.at[zl, :, j, second], zm)
-    for j in order:
-        far = lax.rem(y + 2, 4)
-        got(j, 9, w.at[0, far, j, mine])
-        got(j, 10, w.at[1, far, j, mine])
-        go(j, 11, w.at[:, :, j, mine], w.at[:, :, j, mine], xp)
-        go(j, 12, w.at[:, :, j, mine], w.at[:, :, j, mine], xm)
-    for j in order:
-        left, right = quarter(x - 1), quarter(x + 1)
-        got(j, 11, w.at[:, :, j, left])
-        got(j, 12, w.at[:, :, j, right])
-        go(j, 13, w.at[0, :, j, left], w.at[0, :, j, left], xp)
-        go(j, 14, w.at[1, :, j, right], w.at[1, :, j, right], xm)
-    last = []
-    for j in order:
-        across = quarter(x + 2)
-        got(j, 4, w.at[1 - zl, :, j, first])
-        got(j, 5, w.at[1 - zl, :, j, second])
-        got(j, 13, w.at[0, :, j, across])
-        got(j, 14, w.at[1, :, j, across])
-        if j == 0:
-            for i in range(2):
-                src = w.at[1, 2 + i, 0]
-                dst = wo.at[2 * i + c]
-                cp = remote(src, dst, os.at[i], orr.at[i], mate)
-                cp.start()
-                lc = pltpu.make_async_copy(src, dst, loc.at[i, 2])
-                lc.start()
-                last += [cp, lc]
-    for cp in last:
-        cp.wait()
-    for cp in sent:
-        cp.wait_send()
-
-
-def gather_weights(shard):
-    return pl.pallas_call(
-        gather_kernel,
-        out_shape=(
-            jax.ShapeDtypeStruct((2, 4, 4, 1024, 256), BF16),
-            jax.ShapeDtypeStruct((4, 1024, 256), BF16),
-        ),
-        in_specs=[ANY],
-        out_specs=(ANY, ANY),
-        scratch_shapes=[
-            pltpu.SemaphoreType.DMA((4, 15)),
-            pltpu.SemaphoreType.DMA((4, 15)),
-            pltpu.SemaphoreType.DMA((4, 3)),
-            pltpu.SemaphoreType.DMA((2,)),
-            pltpu.SemaphoreType.DMA((2,)),
-        ],
-        compiler_params=params(0),
-    )(shard)
-
-
 def pair_kernel(n, *refs):
     ins, outs = refs[:n], refs[n : 2 * n]
-    ss, rs, loc = refs[2 * n :]
+    ss, rs = refs[2 * n :]
     x, y, z, c = place()
     mate = at(x, y, z, 1 - c)
     greet([mate])
     cps = []
     for i in range(n):
         cps.append(remote(ins[i], outs[i].at[c], ss.at[i], rs.at[i], mate))
-        cps.append(pltpu.make_async_copy(ins[i], outs[i].at[c], loc.at[i]))
     for cp in cps:
         cp.start()
+    for i in range(n):
+        outs[i][c] = ins[i][...]
     for cp in cps:
         cp.wait()
 
@@ -196,10 +86,10 @@
     return pl.pallas_call(
         functools.partial(pair_kernel, n),
         out_shape=tuple(jax.ShapeDtypeStruct((2,) + a.shape, a.dtype) for a in arrays),
-        in_specs=[ANY] * n,
-        out_specs=(ANY,) * n,
-        scratch_shapes=[pltpu.SemaphoreType.DMA((n,))] * 3,
-        compiler_params=params(cid),
+        in_specs=[VM] * n,
+        out_specs=(VM,) * n,
+        scratch_shapes=[pltpu.SemaphoreType.DMA((n,))] * 2,
+        compiler_params=params(cid, 32 * 2**20),
     )(*arrays)
 
 
@@ -401,33 +291,148 @@
     )(a)
 
 
-def cond_kernel(
-    msg, slots, table, cond_w, msg_all, slots_all, cond_all, emb_out, ada,
-    cond_own, ada_own, s1, r1, s2, r2, s3, r3, s4, r4,
+NT = (((1,), (1,)), ((), ()))
+
+
+def normalize(v):
+    center = v - jnp.mean(v, -1, keepdims=True)
+    spread = jnp.mean(center * center, -1, keepdims=True)
+    return center * lax.rsqrt(spread + NORM_EPS)
+
+
+def ada_row(ada, k, img):
+    return jnp.concatenate([ada[2 * k, img : img + 1, :], ada[2 * k + 1, img : img + 1, :]], axis=1)
+
+
+def column_of(row):
+    return jnp.transpose(jnp.broadcast_to(row, (128, 128)))
+
+
+def forward_kernel(
+    msg, slots, table, cond_w, x_in, s,
+    msg_all, slots_all, cond_all, emb_out, ada, loss_out,
+    w_o, wo_o, h1_o, h2_o, h3_o, hb_o, ot_o, att_o, x1_o, mlp_o, x2_o, f_o, u_o, dl_o,
+    w, wo, h1, h2, h3, src, hb, oh, ot, att, x1, mlp, x2, acc, got_acc, f, u, dl,
+    cond_own, ada_own, bias, qcol, tcol, wcol, stats,
+    gs, gr, gl, os, orr, s1, r1, s2, r2, s3, r3, s4, r4, ps, pr, as_, ar, al, ts, tr, tl, outs_sem,
 ):
+    x, y, z, c = place()
     dp = lax.axis_index("dp")
     sq = lax.axis_index("seq")
-    core = lax.rem(dp, 2)
+    zl = lax.rem(z, 2)
+    up, down, far = lax.rem(y + 1, 4), lax.rem(y + 3, 4), lax.rem(y + 2, 4)
+    yp, ym = at(x, y + 1, z, c), at(x, y - 1, z, c)
+    zp, zm = at(x, y, z + 1, c), at(x, y, z - 1, c)
+    xp, xm = at(x + 1, y, z, c), at(x - 1, y, z, c)
+    zs = at(x, y, z + 1 - 2 * c, c)
+    mate = at(x, y, z, 1 - c)
+    base = dp - c
     row = [(lax.rem(dp + i, 16), sq) for i in range(1, 16)]
     group = group_peers()
-    greet(row + group[1:])
-    first = []
+    greet(row + group[1:] + [at(x, y, z + 2 * zl - 1, c)])
+
+    pending = []
+
+    def keep(k, src_ref, dst_ref):
+        cp = pltpu.make_async_copy(src_ref, dst_ref, outs_sem.at[k])
+        cp.start()
+        pending.append(cp)
+        return cp
+
+    def quarter(pos):
+        return pl.ds(pl.multiple_of(ROWS_YZ + QUARTER * lax.rem(pos + 4, 4), 16), QUARTER)
+
+    mine = quarter(x)
+    full, first, second = pl.ds(0, ROWS_YZ), pl.ds(0, HALF_YZ), pl.ds(HALF_YZ, HALF_YZ)
+    sent = []
+
+    def go(j, k, a, b, device):
+        cp = remote(a, b, gs.at[j, k], gr.at[j, k], device)
+        cp.start()
+        sent.append(cp)
+
+    def got(j, k, ref):
+        remote(ref, ref, gs.at[j, k], gr.at[j, k], mate).wait_recv()
+
+    def stage(kind, j):
+        if kind == "A":
+            go(j, 0, s.at[j, full], w.at[zl, y, j, full], yp)
+            go(j, 1, s.at[j, full], w.at[zl, y, j, full], ym)
+            go(j, 6, s.at[j, mine], w.at[zl, y, j, mine], zs)
+            for i, rows in enumerate((full, mine)):
+                pltpu.make_async_copy(s.at[j, rows], w.at[zl, y, j, rows], gl.at[j, i]).start()
+        if kind == "B":
+            for i, rows in enumerate((full, mine)):
+                pltpu.make_async_copy(s.at[j, rows], w.at[zl, y, j, rows], gl.at[j, i]).wait()
+            got(j, 6, w.at[1 - zl, y, j, mine])
+            go(j, 7, w.at[:, y, j, mine], w.at[:, y, j, mine], yp)
+            go(j, 8, w.at[:, y, j, mine], w.at[:, y, j, mine], ym)
+            got(j, 0, w.at[zl, down, j, full])
+            got(j, 1, w.at[zl, up, j, full])
+            go(j, 2, w.at[zl, down, j, first], w.at[zl, down, j, first], yp)
+            go(j, 3, w.at[zl, up, j, second], w.at[zl, up, j, second], ym)
+        if kind == "C":
+            got(j, 7, w.at[:, down, j, mine])
+            got(j, 8, w.at[:, up, j, mine])
+            go(j, 9, w.at[0, down, j, mine], w.at[0, down, j, mine], yp)
+            go(j, 10, w.at[1, up, j, mine], w.at[1, up, j, mine], ym)
+            got(j, 2, w.at[zl, far, j, first])
+            got(j, 3, w.at[zl, far, j, second])
+            go(j, 4, w.at[zl, :, j, first], w.at[zl, :, j, first], zp)
+            go(j, 5, w.at[zl, :, j, second], w.at[zl, :, j, second], zm)
+        if kind == "D":
+            got(j, 9, w.at[0, far, j, mine])
+            got(j, 10, w.at[1, far, j, mine])
+            go(j, 11, w.at[:, :, j, mine], w.at[:, :, j, mine], xp)
+            go(j, 12, w.at[:, :, j, mine], w.at[:, :, j, mine], xm)
+        if kind == "E":
+            left, right = quarter(x - 1), quarter(x + 1)
+            got(j, 11, w.at[:, :, j, left])
+            got(j, 12, w.at[:, :, j, right])
+            go(j, 13, w.at[0, :, j, left], w.at[0, :, j, left], xp)
+            go(j, 14, w.at[1, :, j, right], w.at[1, :, j, right], xm)
+        if kind == "F":
+            across = quarter(x + 2)
+            got(j, 4, w.at[1 - zl, :, j, first])
+            got(j, 5, w.at[1 - zl, :, j, second])
+            got(j, 13, w.at[0, :, j, across])
+            got(j, 14, w.at[1, :, j, across])
+            keep(j, w.at[:, :, j], w_o.at[:, :, j])
+            if j == 0:
+                for i in range(2):
+                    remote(w.at[1, 2 + i, 0], wo.at[2 * i + c], os.at[i], orr.at[i], mate).start()
+                    pltpu.make_async_copy(w.at[1, 2 + i, 0], wo.at[2 * i + c], gl.at[i, 2]).start()
+
+    wave = [
+        "A0 A1", "B0 A2", "C0 B1 A3", "D0 C1 B2", "E0 D1 C2 B3", "F0 E1 D2 C3", "E2 D3", "E3", "F1", "F2", "F3"
+    ]
+
+    def pump(n=1):
+        for _ in range(n):
+            if wave:
+                for item in wave.pop(0).split():
+                    stage(item[0], int(item[1]))
+
+    pump()
+    firsts = []
     for i, to in enumerate(row):
         cp = remote(msg, msg_all.at[dp], s1.at[i], r1.at[i], to)
         cp.start()
-        first.append(cp)
+        firsts.append(cp)
     msg_all[dp] = msg[...]
-    for cp in first:
+    for cp in firsts:
         cp.wait()
     seen = msg_all[...]
     count = jnp.sum(seen[:, 10, 2:3], axis=0, keepdims=True)
-    slots[7:8, :] = jnp.broadcast_to(count, (1, 128))
-    second = []
+    slots[8:9, :] = jnp.broadcast_to(count, (1, 128))
+    for d in range(16):
+        bias[pl.ds(10 * d, 10), :] = seen[d, 0:10, :]
+    seconds = []
     for i, to in enumerate(group):
-        cp = remote(slots, slots_all.at[sq * 2 + core], s2.at[i], r2.at[i], to)
+        cp = remote(slots, slots_all.at[sq * 2 + c], s2.at[i], r2.at[i], to)
         cp.start()
-        second.append(cp)
-    slots_all[sq * 2 + core] = slots[...]
+        seconds.append(cp)
+    slots_all[sq * 2 + c] = slots[...]
     classes = table.shape[0]
     lane = lax.broadcasted_iota(jnp.int32, (32, classes), 1)
     labels = jnp.concatenate([seen[d, 10:11, i : i + 1] for d in range(16) for i in range(2)], axis=0)
@@ -436,54 +441,312 @@
     emb_out[...] = emb
     cond_own[...] = (emb / (1.0 + jnp.exp(-emb))).astype(BF16)
     cond_all[dp] = cond_own[...]
-    third = []
+    thirds = []
     for i, to in enumerate(row):
         cp = remote(cond_own, cond_all.at[dp], s3.at[i], r3.at[i], to)
         cp.start()
-        third.append(cp)
-    for cp in third:
+        thirds.append(cp)
+    pump()
+    for cp in thirds:
         cp.wait()
-    acc = jnp.zeros((32, 512), F32)
+    total = jnp.zeros((32, 512), F32)
     for d in range(16):
-        acc += jnp.dot(cond_all[d], cond_w[pl.ds(64 * d, 64), :], preferred_element_type=F32)
-    bias = []
-    for i in range(4):
-        at_row = dp * 4 + i
-        bias.append(msg_all[at_row // 10, pl.ds(lax.rem(at_row, 10), 1), :])
-    acc += jnp.concatenate(bias, axis=1)
+        total += jnp.dot(cond_all[d], cond_w[pl.ds(64 * d, 64), :], preferred_element_type=F32)
+    total += jnp.concatenate([bias[pl.ds(dp * 4 + i, 1), :] for i in range(4)], axis=1)
     for d in range(16):
-        ada_own[d] = acc[2 * d : 2 * d + 2]
-    fourth = []
+        ada_own[d] = total[2 * d : 2 * d + 2]
+    fourths = []
     for i in range(15):
         to = lax.rem(dp + 1 + i, 16)
         cp = remote(ada_own.at[to], ada.at[dp], s4.at[i], r4.at[i], (to, sq))
         cp.start()
-        fourth.append(cp)
+        fourths.append(cp)
     ada[dp] = ada_own[dp]
-    for cp in fourth:
+    pump()
+    for cp in fourths:
         cp.wait()
-    for cp in second:
+    for cp in seconds:
         cp.wait()
 
-
-def condition(msg, slots, table, cond_w):
+    owner = lax.rem(sq, 2)
+    for img in range(2):
+        for g in range(8):
+            qcol[img, g] = column_of(slots_all[g * 2 + owner, pl.ds(2 + img, 1), :])
+        for q in range(2):
+            at_rows = pl.ds((q * 2 + img) * 128, 128)
+            tcol[at_rows, :] = column_of(slots_all[sq * 2 + q, pl.ds(4 + img, 1), :])
+            wcol[at_rows, :] = column_of(slots_all[sq * 2 + q, pl.ds(6 + img, 1), :])
+    true_count = jnp.sum(
+        jnp.concatenate([slots_all[2 * g, 8:9, 0:1] for g in range(8)], axis=0), axis=0, keepdims=True
+    )
+
+    def blocks(fn):
+        for img in range(2):
+            def body(i, carry, img=img):
+                fn(img, pl.ds(pl.multiple_of(img * 128 + i * 32, 32), 32))
+                return carry
+            lax.fori_loop(0, 4, body, 0)
+
+    def exchange(k, ref):
+        cp = remote(ref.at[c], ref.at[c], ps.at[k], pr.at[k], mate)
+        cp.start()
+        return cp
+
+    def modulated(img, v, scale, shift):
+        return (normalize(v) * (1.0 + ada_row(ada, scale, img)) + ada_row(ada, shift, img)).astype(BF16)
+
+    def do_h1(img, rows):
+        h1[c, rows, :] = modulated(img, x_in[rows, :].astype(F32), 2, 4)
+
+    blocks(do_h1)
+    cp = exchange(0, h1)
+    pump()
+    cp.wait()
+    keep(4, h1, h1_o)
+    pump(2)
+
+    def bias_row(start):
+        return jnp.concatenate([bias[pl.ds(start, 1), :], bias[pl.ds(start + 1, 1), :]], axis=1)
+
+    tokens = h1[...].reshape(512, 1024)
+    for j in range(6):
+        t, jj = j // 2, j % 2
+        val = jnp.dot(tokens, w[j // 4, j % 4, 0], preferred_element_type=F32)
+        if t != 1:
+            val = val + bias_row(64 + (0 if t == 0 else 8) + (2 * jj + c) * 2)
+        val = val.astype(BF16)
+        for half in range(2):
+            for ip in range(2):
+                src[(jj * 2 + half) * 2 + ip, t] = val[
+                    ip * 256 : ip * 256 + 256, half * 128 : half * 128 + 128
+                ].reshape(2, 128, 128)
+    cps = []
+    for i in range(1, 8):
+        to = lax.rem(sq + i, 8)
+        cp = remote(src.at[to], hb.at[sq], as_.at[i], ar.at[i], (dp, to))
+        cp.start()
+        cps.append(cp)
+    hb[sq] = src[sq]
+    pump(2)
+    for cp in cps:
+        cp.wait()
+    keep(5, hb, hb_o)
+
+    low_lanes = lax.broadcasted_iota(jnp.int32, (256, 128), 1) < 64
+
+    def attend_block(i, carry):
+        img, qb = i // 4, lax.rem(i, 4)
+        q = jnp.concatenate([hb[2 * qb, 0, img], hb[2 * qb + 1, 0, img]], axis=0)
+        k = jnp.concatenate([hb[g, 1, img] for g in range(8)], axis=0)
+        v = jnp.concatenate([hb[g, 2, img] for g in range(8)], axis=0)
+        key = jnp.concatenate([slots_all[g * 2 + owner, pl.ds(img, 1), :] for g in range(8)], axis=1)
+        query = jnp.concatenate([qcol[img, 2 * qb], qcol[img, 2 * qb + 1]], axis=0)[:, 0:1]
+        seen_by = key <= query
+        heads = []
+        for h in range(2):
+            mask = low_lanes if h == 0 else jnp.logical_not(low_lanes)
+            qh = jnp.where(mask, q, jnp.zeros_like(q))
+            sc = lax.dot_general(qh, k, NT, preferred_element_type=F32) * SCORE_SCALE
+            sc = jnp.where(seen_by, sc, -1e30)
+            e = jnp.exp(sc - jnp.max(sc, axis=-1, keepdims=True))
+            p = (e / jnp.sum(e, axis=-1, keepdims=True)).astype(BF16)
+            heads.append(jnp.dot(p, v, preferred_element_type=F32))
+        o = jnp.where(low_lanes, heads[0], heads[1]).astype(BF16)
+        oh[2 * qb, img] = o[:128]
+        oh[2 * qb + 1, img] = o[128:]
+        return carry
+
+    lax.fori_loop(0, 8, attend_block, 0)
+    pair = sq // 2
+    lanes = head_lanes(pair, c)
+
+    def o_copy(i, img):
+        to = lax.rem(sq + i, 8)
+        return remote(
+            oh.at[to, img], ot.at[pl.ds(img * 128, 128), lanes], ts.at[i, img], tr.at[pair, c, img],
+            (base + owner, to),
+        )
+
+    for img in range(2):
+        for i in range(1, 8):
+            o_copy(i, img).start()
+
+        @pl.when(owner == c)
+        def _():
+            ot[pl.ds(img * 128, 128), lanes] = oh[sq, img]
+
+        @pl.when(owner != c)
+        def _():
+            o_copy(0, img).start()
+
+    pump()
+    for img in range(2):
+        for p in range(4):
+            for q in range(2):
+                view = ot.at[pl.ds(img * 128, 128), pl.ds(((p // 2 * 2 + q) * 2 + p % 2) * 128, 128)]
+
+                @pl.when(jnp.logical_or(sq != p * 2 + c, c != q))
+                def _():
+                    remote(view, view, ts.at[0, img], tr.at[p, q, img], mate).wait_recv()
+
+    keep(6, ot, ot_o)
+    for i in range(2):
+        remote(w.at[1, 2 + i, 0], wo.at[2 * i + c], os.at[i], orr.at[i], mate).wait()
+        pltpu.make_async_copy(w.at[1, 2 + i, 0], wo.at[2 * i + c], gl.at[i, 2]).wait()
+    keep(7, wo, wo_o)
+    for k in range(4):
+        cols = pl.ds(256 * k, 256)
+        att[:, cols] = jnp.dot(ot[...], wo[k], preferred_element_type=F32) + bias_row(80 + 2 * k)
+    keep(8, att, att_o)
+
+    def do_h2(img, rows):
+        v = x_in[rows, :].astype(F32) + ada_row(ada, 0, img) * att[rows, :]
+        x1[rows, :] = v
+        h2[c, rows, :] = modulated(img, v, 3, 5)
+
+    blocks(do_h2)
+    cp = exchange(1, h2)
+    keep(9, x1, x1_o)
+    pump(20)
+    cp.wait()
+    keep(10, h2, h2_o)
+
+    def chunk(ref, j, kind):
+        return ref[j // 4, lax.rem(j, 4), kind]
+
+    def do_f(j, carry):
+        val = jnp.dot(h2[...].reshape(512, 1024), chunk(w, j, 1), preferred_element_type=F32)
+        val = val + bias_row(88 + (2 * j + c) * 2)
+        f[j] = val
+        act = jax.nn.gelu(val, approximate=True).astype(BF16)
+        u[j] = act
+        part = lax.dot_general(act, chunk(w, j, 2), NT, preferred_element_type=F32).reshape(2, 256, 1024)
+
+        @pl.when(j == 0)
+        def _():
+            acc[...] = part
+
+        @pl.when(j > 0)
+        def _():
+            acc[...] += part
+
+        return carry
+
+    lax.fori_loop(0, 8, do_f, 0)
+    f_copy = keep(11, f, f_o)
+    keep(12, u, u_o)
+    cp = remote(acc.at[1 - c], got_acc, ps.at[2], pr.at[2], mate)
+    cp.start()
+    b_two = jnp.concatenate([bias[pl.ds(120 + i, 1), :] for i in range(8)], axis=1)
+    cp.wait()
+
+    def do_h3(img, rows):
+        m = acc[c, rows, :] + got_acc[rows, :] + b_two
+        mlp[rows, :] = m
+        v = x1[rows, :] + ada_row(ada, 1, img) * m
+        x2[rows, :] = v
+        h3[c, rows, :] = modulated(img, v, 6, 7)
+
+    blocks(do_h3)
+    cp = exchange(3, h3)
+    keep(13, mlp, mlp_o)
+    keep(14, x2, x2_o)
+    f_copy.wait()
+    pending[:] = [p for p in pending if p is not f_copy]
+    cp.wait()
+    keep(15, h3, h3_o)
+
+    def do_logits(j, top):
+        val = jnp.dot(h3[...].reshape(512, 1024), chunk(w, j, 3), preferred_element_type=F32)
+        val = val + bias_row(128 + (2 * j + c) * 2)
+        f[j] = val
+        return jnp.maximum(top, jnp.max(val, axis=-1, keepdims=True))
+
+    top = lax.fori_loop(0, 8, do_logits, jnp.full((512, 1), -jnp.inf, F32))
+    inner = lax.broadcasted_iota(jnp.int32, (512, 256), 1)
+
+    def target_hit(j):
+        return inner == (tcol[:, 0:1].astype(jnp.int32) - (2 * j + c) * 256)
+
+    def do_mass(j, carry):
+        mass, picked = carry
+        val = f[j]
+        mass = mass + jnp.sum(jnp.exp(val - top), axis=-1, keepdims=True)
+        picked = picked + jnp.sum(jnp.where(target_hit(j), val, 0.0), axis=-1, keepdims=True)
+        return mass, picked
+
+    zero = jnp.zeros((512, 1), F32)
+    mass, picked = lax.fori_loop(0, 8, do_mass, (zero, zero))
+    lane = lax.broadcasted_iota(jnp.int32, (512, 128), 1)
+    stats[c] = jnp.where(lane == 0, top, jnp.where(lane == 1, mass, picked))
+    cp = exchange(4, stats)
+    cp.wait()
+    both = [stats[0], stats[1]]
+    top_all = jnp.maximum(both[0][:, 0:1], both[1][:, 0:1])
+    mass_all = sum(b[:, 1:2] * jnp.exp(b[:, 0:1] - top_all) for b in both)
+    log_total = top_all + jnp.log(mass_all)
+    weight = wcol[:, 0:1]
+    losses = weight * (log_total - (both[0][:, 2:3] + both[1][:, 2:3]))
+    loss_out[...] = jnp.broadcast_to(0.5 * jnp.sum(losses, axis=0, keepdims=True), (8, 128))
+    share = weight / true_count
+
+    def do_dlogits(j, carry):
+        grad = share * (jnp.exp(f[j] - log_total) - jnp.where(target_hit(j), 1.0, 0.0))
+        dl[j] = grad.astype(BF16)
+        return carry
+
+    lax.fori_loop(0, 8, do_dlogits, 0)
+    keep(16, dl, dl_o)
+    for img in range(2):
+        for i in range(1, 8):
+            o_copy(i, img).wait_send()
+
+        @pl.when(owner != c)
+        def _():
+            o_copy(0, img).wait_send()
+
+    for cp in sent:
+        cp.wait_send()
+    for cp in pending:
+        cp.wait()
+
+
+def forward_pass(msg, slots, table, cond_w, x_rows, shard):
     dma = pltpu.SemaphoreType.DMA
+    sd = jax.ShapeDtypeStruct
+    kept = [
+        sd((2, 4, 4, 1024, 256), BF16), sd((4, 1024, 256), BF16),
+        sd((2, 256, 1024), BF16), sd((2, 256, 1024), BF16), sd((2, 256, 1024), BF16),
+        sd((8, 3, 2, 128, 128), BF16), sd((256, 1024), BF16),
+        sd((256, 1024), F32), sd((256, 1024), F32), sd((256, 1024), F32), sd((256, 1024), F32),
+        sd((8, 512, 256), F32), sd((8, 512, 256), BF16), sd((8, 512, 256), BF16),
+    ]
+    vm = pltpu.VMEM
     return pl.pallas_call(
-        cond_kernel,
-        out_shape=(
-            jax.ShapeDtypeStruct((16, 16, 128), F32),
-            jax.ShapeDtypeStruct((16, 8, 128), F32),
-            jax.ShapeDtypeStruct((16, 32, 64), BF16),
-            jax.ShapeDtypeStruct((32, 64), F32),
-            jax.ShapeDtypeStruct((16, 2, 512), F32),
-        ),
-        in_specs=[VM] * 4,
-        out_specs=(VM,) * 5,
-        scratch_shapes=[pltpu.VMEM((32, 64), BF16), pltpu.VMEM((16, 2, 512), F32)]
-        + [dma((15,))] * 8,
-        input_output_aliases={},
-        compiler_params=params(1),
-    )(msg, slots, table, cond_w)
+        forward_kernel,
+        out_shape=[
+            sd((16, 16, 128), F32), sd((16, 16, 128), F32), sd((16, 32, 64), BF16),
+            sd((32, 64), F32), sd((16, 2, 512), F32), sd((8, 128), F32),
+        ] + kept,
+        in_specs=[VM] * 5 + [ANY],
+        out_specs=[VM] * 6 + [ANY] * len(kept),
+        scratch_shapes=[
+            vm((2, 4, 4, 1024, 256), BF16), vm((4, 1024, 256), BF16),
+            vm((2, 256, 1024), BF16), vm((2, 256, 1024), BF16), vm((2, 256, 1024), BF16),
+            vm((8, 3, 2, 128, 128), BF16), vm((8, 3, 2, 128, 128), BF16), vm((8, 2, 128, 128), BF16),
+            vm((256, 1024), BF16),
+            vm((256, 1024), F32), vm((256, 1024), F32), vm((256, 1024), F32), vm((256, 1024), F32),
+            vm((2, 256, 1024), F32), vm((256, 1024), F32),
+            vm((8, 512, 256), F32), vm((8, 512, 256), BF16), vm((8, 512, 256), BF16),
+            vm((32, 64), BF16), vm((16, 2, 512), F32), vm((160, 128), F32),
+            vm((2, 8, 128, 128), F32), vm((512, 128), F32), vm((512, 128), F32), vm((2, 512, 128), F32),
+            dma((4, 15)), dma((4, 15)), dma((4, 3)), dma((2,)), dma((2,)),
+            dma((15,)), dma((15,)), dma((15,)), dma((15,)), dma((15,)), dma((15,)), dma((15,)), dma((15,)),
+            dma((5,)), dma((5,)), dma((8,)), dma((8,)), dma,
+            dma((8, 2)), dma((4, 2, 2)), dma, dma((17,)),
+        ],
+        compiler_params=params(0, 63 * 2**20),
+    )(msg, slots, table, cond_w, x_rows, shard)
 
 
 def small_kernel(
@@ -905,50 +1168,30 @@
 
     count_part = jnp.sum(pad_mask.astype(F32))
     row = jnp.concatenate([labels.astype(F32), count_part[None], jnp.zeros((125,), F32)])
-    msg = jnp.concatenate(
-        [biases.astype(BF16).astype(F32).reshape(10, 128), row[None], jnp.zeros((5, 128), F32)]
-    )
+    rounded = lax.reduce_precision(biases, 8, 7).reshape(10, 128)
+    msg = jnp.concatenate([rounded, row[None], jnp.zeros((5, 128), F32)])
     level = jnp.where(pad_mask > 0, scale_ids, 1000).astype(F32)
     weight_own = (loss_weights * pad_mask).astype(F32)
     slots = jnp.concatenate(
-        [level * 16.0 + scale_ids.astype(F32), targets.astype(F32), weight_own, jnp.zeros((2, 128), F32)]
+        [level, scale_ids.astype(F32), targets.astype(F32), weight_own, jnp.zeros((8, 128), F32)]
     )
-    msg_all, slots_all, cond_all, embedded, ada = condition(
-        msg, slots, class_table.astype(BF16), wb_cond
-    )
-    w, wo = gather_weights(shard)
+    (
+        msg_all, slots_all, cond_all, embedded, ada, loss_tile,
+        w, wo, h1, h2, h3, heads, o, att, x1, mlp, x2, f, u, dlogits,
+    ) = forward_pass(msg, slots, class_table.astype(BF16), wb_cond, x_in.reshape(256, 1024), shard)
     w = w.reshape(8, 4, 1024, 256)
-
-    bias_all = msg_all[:, :10].reshape(20480)
-    b_q, b_v, b_proj, b_fc1, b_fc2, b_head = jnp.split(
-        bias_all[8192:], [1024, 2048, 3072, 7168, 8192]
-    )
-
-    def own_columns(b):
-        return lax.dynamic_index_in_dim(b.reshape(-1, 2, 256), core, 1, keepdims=False)
-
-    slots_all = slots_all.reshape(8, 2, 8, 128)
-    true_count = jnp.sum(slots_all[:, 0, 7, 0])
+    h1, h2, h3 = (h.reshape(512, 1024) for h in (h1, h2, h3))
+    att, x1, mlp, x2 = (a.reshape(2, 128, 1024) for a in (att, x1, mlp, x2))
+    x = x_in.astype(F32)
+    loss_part = loss_tile[0, 0]
+    slots_all = slots_all.reshape(8, 2, 16, 128)
+    true_count = jnp.sum(slots_all[:, 0, 8, 0])
     ada_rows = jnp.transpose(ada, (1, 0, 2)).reshape(2, 1, 8192)
     g_a, g_m, s_a, s_m, t_a, t_m, s_h, t_h = jnp.split(ada_rows, 8, axis=2)
     sq_index = lax.axis_index("seq")
-    pair_slots = lax.dynamic_index_in_dim(slots_all, sq_index, 0, keepdims=False)
-    target_pair = pair_slots[:, 2:4].reshape(512).astype(jnp.int32)
-    weight_pair = pair_slots[:, 4:6].reshape(512)
-    owner = sq_index % 2
-    levels = lax.dynamic_index_in_dim(slots_all, owner, 1, keepdims=False)[:, 0:2]
-    levels = jnp.transpose(levels, (1, 0, 2)).reshape(2, 1024)
-    key_level = jnp.floor(levels / 16.0)
-    query_level = levels - key_level * 16.0
-
-    x = x_in.astype(F32)
-    h1 = modulate(x, s_a, t_a).astype(BF16).reshape(256, 1024)
-    (h1,) = pair_gather(4, h1)
-    h1 = h1.reshape(512, 1024)
-    bias_qkv = jnp.concatenate([own_columns(b_q), jnp.zeros((2, 256), F32), own_columns(b_v)])
-    qkv = (columns(h1, w[:6, 0]) + bias_qkv[:, None, :]).astype(BF16)
-    blocks = qkv.reshape(3, 2, 2, 256, 2, 128).transpose(1, 4, 2, 0, 3, 5).reshape(8, 3, 256, 128)
-    heads = all_to_all(5, blocks)
+    levels = lax.dynamic_index_in_dim(slots_all, sq_index % 2, 1, keepdims=False)
+    key_level = jnp.transpose(levels[:, 0:2], (1, 0, 2)).reshape(2, 1024)
+    query_level = jnp.transpose(levels[:, 2:4], (1, 0, 2)).reshape(2, 1024)
 
     def by_head(block):
         return block.reshape(8, 2, 128, 2, 64).transpose(1, 3, 0, 2, 4).reshape(2, 2, 1024, 64)
@@ -956,47 +1199,11 @@
     def from_head(block):
         return block.reshape(2, 2, 8, 128, 64).transpose(2, 0, 3, 1, 4).reshape(8, 256, 128)
 
-    q, k, v = (by_head(heads[:, i]) for i in range(3))
+    q, k, v = (by_head(heads[:, i].reshape(8, 256, 128)) for i in range(3))
     visible = (key_level[:, None, None, :] <= query_level[:, None, :, None])
     scores = jnp.einsum("ihqd,ihkd->ihqk", q, k, preferred_element_type=F32) * SCORE_SCALE
     probs = jax.nn.softmax(jnp.where(visible, scores, -1e30), axis=-1)
     probs_low = probs.astype(BF16)
-    o = jnp.einsum("ihqk,ihkd->ihqd", probs_low, v, preferred_element_type=F32).astype(BF16)
-    o = to_tokens(6, from_head(o))
-    att = jnp.einsum("td,jdk->tjk", o, wo, preferred_element_type=F32).reshape(256, 1024) + b_proj
-    att = att.reshape(2, 128, 1024)
-    x1 = x + g_a * att
-    h2 = modulate(x1, s_m, t_m).astype(BF16).reshape(256, 1024)
-    (h2,) = pair_gather(7, h2)
-    h2 = h2.reshape(512, 1024)
-    f = columns(h2, w[:, 1]) + own_columns(b_fc1)[:, None, :]
-    u = jax.nn.gelu(f, approximate=True).astype(BF16)
-    mlp = swap_add(8, rows_back(u, w[:, 2]).reshape(2, 256, 1024)) + b_fc2
-    mlp = mlp.reshape(2, 128, 1024)
-    x2 = x1 + g_m * mlp
-    h3 = modulate(x2, s_h, t_h).astype(BF16).reshape(256, 1024)
-    (h3,) = pair_gather(9, h3)
-    h3 = h3.reshape(512, 1024)
-    logits = columns(h3, w[:, 3]) + own_columns(b_head)[:, None, :]
-    top = jnp.max(logits, axis=(0, 2))
-    mass = jnp.sum(jnp.exp(logits - top[None, :, None]), axis=(0, 2))
-    column = (
-        (2 * jnp.arange(8)[:, None] + core) * 256 + jnp.arange(256)[None, :]
-    )
-    target_hit = target_pair[None, :, None] == column[:, None, :]
-    picked = jnp.sum(jnp.where(target_hit, logits, 0.0), axis=(0, 2))
-    stats = jnp.stack([top, mass, picked]).reshape(3, 4, 128)
-    (stats,) = pair_gather(10, stats)
-    stats = stats.reshape(2, 3, 512)
-    top_all = jnp.max(stats[:, 0], axis=0)
-    mass_all = jnp.sum(stats[:, 1] * jnp.exp(stats[:, 0] - top_all[None]), axis=0)
-    log_total = top_all + jnp.log(mass_all)
-    picked_all = jnp.sum(stats[:, 2], axis=0)
-    loss_part = 0.5 * jnp.sum(weight_pair * (log_total - picked_all))
-    dlogits = (
-        (weight_pair / true_count)[None, :, None]
-        * (jnp.exp(logits - log_total[None, :, None]) - target_hit.astype(F32))
-    ).astype(BF16)
 
     grad_head = weight_grad(h3, dlogits)
     db_head = jnp.sum(dlogits.astype(F32), axis=1)

time: 913 us -> 758 us (0.83)
  Pallas kernels: 621 us -> 488 us
  matrix products: 127 us -> 86.9 us
  local copies, waits for them, and re-layouts: 74.9 us -> 102 us
    pallas_call x6 -> x2, Pallas kernels: 104 us -> 4.76 us  [pair_gather(): pl.pallas_call(functools.partial(pair_kernel, n), out_shape=tuple((jax.Sh...]
    pallas_call x2 -> x1, Pallas kernels: 45.9 us -> 24.3 us  [all_to_all(): pl.pallas_call(a2a_kernel, out_shape=jax.ShapeDtypeStruct(a.shape, a.dtyp...]
    dot_general x4 -> x1, matrix products: 28.3 us -> 7.59 us  [columns(): return jnp.einsum('td,jdk->jtk', h, w, preferred_element_type=F32)]
    mul x0 -> x6, local copies, waits for them, and re-layouts: none -> 11.3 us  [the longest x4 7.51 us: modulate(): return layer_norm(values) * (1.0 + scale_row) + shift_row]
    dot_general x2 -> x0, matrix products: 10 us -> none  [the longest x1 7.54 us: local(): jnp.einsum('ihqk,ihkd->ihqd', probs_low, v, preferred_element_type=F32)]
    pallas_call x3 -> x1, Pallas kernels: 193 us -> 183 us  [forward_pass(): pl.pallas_call(forward_kernel, out_shape=[sd((16, 16, 128), F32), sd((16,...]
    dot_general x4 -> x3, matrix products: 18.5 us -> 13.9 us  [rows_back(): return jnp.einsum('jtk,jdk->td', g, w, preferred_element_type=F32)]
where the time goes in v2:
time: 758 us; the launch traced here: 752 us
  Pallas kernels  488 us (64%)
  local copies, waits for them, and re-layouts  102 us (13%)
  matrix products  86.9 us (11%)
  other arithmetic  68.7 us (9%)
    pallas_call x1, Pallas kernels, reduce_grads(): pl.pallas_call(reduce_kernel, out_shape=(jax.ShapeDtypeStruct((4, 1024, 2...  223 us
    pallas_call x1, Pallas kernels, forward_pass(): pl.pallas_call(forward_kernel, out_shape=[sd((16, 16, 128), F32), sd((16,...  183 us
    pallas_call x1, Pallas kernels, small_reduce(): pl.pallas_call(small_kernel, out_shape=(jax.ShapeDtypeStruct((32, 512), F...  32.2 us
    transpose x3, local copies, waits for them, and re-layouts, weight_grad(): return jnp.einsum('td,jtk->jdk', h, g, preferred_element_type=F32)  27.7 us
    pallas_call x1, Pallas kernels, all_to_all(): pl.pallas_call(a2a_kernel, out_shape=jax.ShapeDtypeStruct(a.shape, a.dtyp...  24.3 us
    dot_general x4, matrix products, weight_grad(): return jnp.einsum('td,jtk->jdk', h, g, preferred_element_type=F32)  20.2 us
    convert_element_type x5, other arithmetic, local(): copies = [weight.astype(BF16) for weight in new_weights]  17.9 us

profile of v2, /device:TPU:1, one launch (start us, length us, event | category | flops | bytes accessed | tf_op | source)
XLA Modules:
  0.0 751.9 jit_solution(4426193295939143505)
XLA Ops:
  0.7 1.4 convert_reduce_fusion.7
  6.4 1.2 concatenate.25.slots
  9.4 2.7 convert_element_type.113.cond_w
  12.2 1.5 copy-done.11
  13.8 1.6 pad_maximum_fusion.1.s
  15.4 183.2 %shard_map.439 = (f32[16,16,128]{2,1,0:T(8,128)}, f32[16,16,128]{2,1,0:T(8,128)}, bf16[16,32,64]{2,1,0:T(8,128)(2,1)}, f32[32,64]{1,0:T(8,128)}, f32[16,2,512]{2...) custom-call(f32[16,128]{1,0:T(8,128)} %maximum_maximum_fusion.1.msg,, ...), custom_call_target="tpu_custom_call" | custom-call | tf_op jit(solution)/shard_map/pallas_call | solution.py:725
  199.7 1.4 reduce_sum.309
  201.1 5.2 fusion.25.a
  206.3 2.9 shard_map.440
  211.2 2.0 shard_map.441
  213.2 7.6 %convert_reduce_fusion.1 = (f32[8,256]{1,0:T(8,128)S(1)}, bf16[8,512,256]{2,1,0:T(8,128)(2,1)S(1)}) fusion(f32[8,512,256]{2,1,0:T(8,128)} %get-tuple-element.71, bf16[512,1024,1]{1,0,2:T(8,128)(2,1)S(1)} %bitcast.371, bf16[8,4,1024,256]{3,2,1,0:T(8,128)(2,1)} %bitcast.410), kind=kOutput, calls=%fused_computation.34 | convolution fusion | flops 2170550272 | bytes 11542528 | tf_op jit(solution)/shard_map/td,jdk->jtk/dot_general | solution.py:1137
  220.8 1.3 copy-done.51
  222.1 4.5 fusion.26.a
  226.7 2.9 shard_map.442
  230.0 1.3 fusion.97
  232.2 1.6 multiply_reduce_fusion.4
  234.9 2.7 mul.560
  237.6 2.7 reshape.466
  240.3 1.4 reshape.465
  242.8 2.7 mul.566
  245.5 1.4 reshape.464
  246.9 1.4 reshape.463
  249.4 2.7 mul.561
  252.1 5.7 fusion.49
  257.8 1.5 fusion.31.a
  259.4 12.2 %shard_map.443 = bf16[8,256,128]{2,1,0:T(8,128)(2,1)} custom-call(bf16[256,1024]{1,0:T(8,128)(2,1)} %fusion.31.a), custom_call_target="tpu_custom_call" | custom-call | tf_op jit(solution)/shard_map/pallas_call | solution.py:280
  271.6 1.3 copy.273
  274.4 2.3 broadcast_compare_fusion
  276.7 2.3 fusion.99
  280.1 11.2 %fusion.101 = (f32[2,2,1024]{2,1,0:T(2,128)S(1)}, f32[2,2,1024,1024]{2,3,1,0:T(8,128)}) fusion(pred[2,1024,1024]{1,2,0:T(8,128)(4,1)} %broadcast_compare_fusion, bf16[2,2,1024,64]{2,3,1,0:T(8,128)(2,1)S(1)} %reshape.461, bf16[2,2,1024,64]{2,3,1,0:T(8,128)(2,1)S(1)} %reshape.462), kind=kOutput, calls=%fused_computation.228 | convolution fusion | flops 553649152 | bytes 19939328 | tf_op jit(solution)/shard_map/sub | solution.py:1205
  291.3 8.4 %fusion.28 = bf16[2,2,1024,64]{2,3,1,0:T(8,128)(2,1)S(1)} fusion(bf16[2,2,1024,64]{2,3,1,0:T(8,128)(2,1)S(1)} %copy-done.34, f32[2,2,1024,1024]{2,3,1,0:T(8,128)} %get-tuple-element.176, f32[2,2,1024]{2,1,0:T(2,128)S(1)} %get-tuple-element.175), kind=kOutput, calls=%fused_computation.75 | convolution fusion | flops 545521664 | bytes 17842176 | tf_op jit(solution)/shard_map/ihqk,ihqd->ihkd/dot_general | solution.py:1245
  301.8 1.3 copy.313
  304.1 11.0 %multiply_reduce_fusion = (f32[2,2,1024]{2,1,0:T(2,128)S(1)}, f32[2,2,1024,1024]{2,3,1,0:T(8,128)}) fusion(f32[2,2,1024,1024]{2,3,1,0:T(8,128)} %get-tuple-element.176, f32[2,2,1024]{2,1,0:T(2,128)S(1)} %get-tuple-element.175, bf16[2,2,1024,64]{2,3,1,0:T(8,128)(2,1)S(1)} %copy-done.35, bf16[2,2,1024,64]{2,3,1,0:T(8,128)(2,1)} %reshape.469), kind=kOutput, calls=%fused_computation.2 | convolution fusion | flops 549449728 | bytes 34635776 | tf_op jit(solution)/shard_map/ihqd,ihkd->ihqk/dot_general | solution.py:1240
  315.1 12.2 %multiply_convert_fusion = bf16[2,2,1024,1024]{2,3,1,0:T(8,128)(2,1)S(1)} fusion(f32[2,2,1024,1024]{2,3,1,0:T(8,128)} %get-tuple-element.178, f32[2,2,1024]{2,1,0:T(2,128)S(1)} %get-tuple-element.177, f32[2,2,1024,1024]{2,3,1,0:T(8,128)} %get-tuple-element.176, f32[2,2,1024]{2,1,0:T(2,128)S(1)} %get-tuple-element.175), kind=kLoop, calls=%fused_computation.1 | loop fusion | flops 16777216 | bytes 41975808 | tf_op jit(solution)/shard_map/convert_element_type | solution.py:1242
  327.3 3.2 copy-done.2
  330.5 2.7 fusion.32
  335.2 4.9 fusion.33
  341.4 2.4 pad_maximum_fusion.2.a
  343.8 24.3 %shard_map.444 = bf16[8,3,256,128]{3,2,1,0:T(8,128)(2,1)} custom-call(bf16[8,3,256,128]{3,2,1,0:T(8,128)(2,1)} %pad_maximum_fusion.2.a), custom_call_target="tpu_custom_call" | custom-call | tf_op jit(solution)/shard_map/pallas_call | solution.py:151
  368.1 3.0 copy.287
  371.1 2.6 reshape.474
  373.8 4.2 fusion.27.a
  378.0 3.3 shard_map.445
  383.6 1.5 convert_reduce_fusion.5
  388.4 32.2 %shard_map.446 = (f32[32,512]{1,0:T(8,128)}, f32[2,8,128]{2,1,0:T(8,128)}, f32[32,64]{1,0:T(8,128)}) custom-call(f32[16,24,128]{2,1,0:T(8,128)} %maximum_maximum_fusion.msg, bf16[1024,512]{1,0:T(8,128)(2,1)} %convert_element_type.113.cond_w), custom_call_target="tpu_custom_call" | custom-call | tf_op jit(solution)/shard_map/pallas_call | solution.py:812
  420.6 3.8 multiply_reduce_fusion.1
  424.4 2.7 shard_map.447
  428.1 2.6 reshape.485
  430.7 3.3 constant_dynamic-slice_fusion
  434.0 2.3 copy.292
  438.1 1.8 convolution_bitcast_fusion.3
  439.9 4.3 pad_maximum_fusion
  444.2 9.4 %copy.293 = f32[8,1024,256]{2,1,0:T(8,128)} copy(f32[8,1024,256]{1,2,0:T(8,128)} %pad_maximum_fusion) | data formatting | bytes 16777216 | tf_op jit(solution)/shard_map/concatenate | solution.py:1293
  453.6 7.2 convolution_bitcast_fusion.2
  460.8 9.3 %copy.295 = f32[8,1024,256]{2,1,0:T(8,128)} copy(f32[8,1024,256]{1,2,0:T(8,128)} %convolution_bitcast_fusion.2) | data formatting | bytes 16777216 | tf_op jit(solution)/shard_map/td,jtk->jdk/transpose | solution.py:1145
  470.0 5.6 convolution_bitcast_fusion.1
  475.6 9.3 %copy.297 = f32[8,1024,256]{2,1,0:T(8,128)} copy(f32[8,1024,256]{1,2,0:T(8,128)} %convolution_bitcast_fusion.1) | data formatting | bytes 16777216 | tf_op jit(solution)/shard_map/td,jtk->jdk/transpose | solution.py:1145
  484.9 5.6 convolution_bitcast_fusion
  490.5 9.2 %copy.299 = f32[8,1024,256]{2,1,0:T(8,128)} copy(f32[8,1024,256]{1,2,0:T(8,128)} %convolution_bitcast_fusion) | data formatting | bytes 16777216 | tf_op jit(solution)/shard_map/td,jtk->jdk/transpose | solution.py:1145
  504.8 222.6 %shard_map.448 = (f32[4,1024,256]{2,1,0:T(8,128)}, f32[8,128]{1,0:T(8,128)}) custom-call(f32[2,4,1024,256]{3,2,1,0:T(8,128)} %bitcast.373, f32[2,4,1024,256]{3,2,1,0:T(8,128)} %bitcast.374, f32[2,4,1024,256]{3,2,1,0:T(8,128)} %bitcast.375, f32[2,4,1024,256]{3,2,1,0:T(8,128)} %bitcast.376, f32[8,128]{1,0:T(8,128)} %scatter.4.refs_4_), custom_call_target="tpu_custom_call" | custom-call | tf_op jit(solution)/shard_map/pallas_call | solution.py:1108
  727.3 1.3 reduce_sum.340
  729.4 8.0 %fusion.93 = (bf16[1024,512]{1,0:T(8,128)(2,1)}, f32[1024,512]{1,0:T(8,128)}, f32[1024,512]{1,0:T(8,128)}, f32[1024,512]{1,0:T(8,128)}) fusion(f32[1024,512]{1,0:T(8,128)} %param.32, f32[1024,512]{1,0:T(8,128)} %get-tuple-element.182, f32[]{:T(128)S(6)} %min.3, f32[1024,512]{1,0:T(8,128)} %param.38, f32[1024,512]{1,0:T(8,128)} %param.44), kind=kLoop, calls=%fused_computation.223 | loop fusion | flops 8388608 | bytes 15728644 | tf_op jit(solution)/shard_map/convert_element_type | solution.py:1311
  738.1 4.1 fusion.87
  743.5 4.2 fusion.89
  (205 shorter events, 38.8 us)
Async XLA Ops:
  0.7 11.5 %copy-start.15 = (f32[1024,256]{1,0:T(8,128)S(1)}, f32[1024,256]{1,0:T(8,128)}, u32[]{:S(2)}) copy-start(f32[1024,256]{1,0:T(8,128)} %param.35) | copy-start | bytes 3145732
  0.7 11.5 %copy-start.17 = (f32[1024,256]{1,0:T(8,128)S(1)}, f32[1024,256]{1,0:T(8,128)}, u32[]{:S(2)}) copy-start(f32[1024,256]{1,0:T(8,128)} %param.33) | copy-start | bytes 3145732
  12.1 1.6 copy-start.11
  206.3 2.9 copy-start.43
  206.3 2.9 copy-start.6
  209.6 1.2 copy-start.3
  210.0 1.2 copy-start.9
  220.8 1.3 copy-start.51
  226.7 2.9 copy-start.4
  230.0 1.3 copy-start.7
  230.0 1.9 copy-start.31
  230.0 2.2 copy-start.32
  241.7 3.8 copy-start.5
  248.3 3.8 copy-start.19
  248.3 3.8 copy-start.20
  252.1 5.7 copy-start.47
  271.6 2.8 copy-start.38
  280.1 11.3 %copy-start.34 = (bf16[2,2,1024,64]{2,3,1,0:T(8,128)(2,1)S(1)}, bf16[2,2,1024,64]{2,3,1,0:T(8,128)(2,1)}, u32[]{:S(2)}) copy-start(bf16[2,2,1024,64]{2,3,1,0:T(8,128)(2,1)} %reshape.468) | copy-start | bytes 1572868
  300.8 3.4 copy-start.35
  327.3 3.2 copy-start.2
  340.3 1.2 copy-start.25
  378.0 3.3 copy-start.13
  381.3 1.4 copy-start.8
  382.3 1.3 copy-start.10
  382.7 2.4 copy-start.23
  385.6 38.8 %copy-start.1 = (bf16[256,1024]{1,0:T(8,128)(2,1)S(1)}, bf16[256,1024]{1,0:T(8,128)(2,1)}, u32[]{:S(2)}) copy-start(bf16[256,1024]{1,0:T(8,128)(2,1)} %get-tuple-element.81.refs_0_) | copy-start | bytes 1572868
  427.1 1.0 copy-start
  436.4 1.4 copy-start.26
  436.4 1.7 copy-start.50
  444.2 9.4 %copy-start.49 = (bf16[2,256,1024]{2,1,0:T(8,128)(2,1)S(1)}, bf16[2,256,1024]{2,1,0:T(8,128)(2,1)}, u32[]{:S(2)}) copy-start(bf16[2,256,1024]{2,1,0:T(8,128)(2,1)} %get-tuple-element.84) | copy-start | bytes 3145732
  460.8 9.3 %copy-start.46 = (bf16[8,512,256]{2,1,0:T(8,128)(2,1)S(1)}, bf16[8,512,256]{2,1,0:T(8,128)(2,1)}, u32[]{:S(2)}) copy-start(bf16[8,512,256]{2,1,0:T(8,128)(2,1)} %get-tuple-element.85) | copy-start | bytes 6291460
  475.6 9.3 %copy-start.24 = (bf16[8,512,256]{2,1,0:T(8,128)(2,1)S(1)}, bf16[8,512,256]{2,1,0:T(8,128)(2,1)}, u32[]{:S(2)}) copy-start(bf16[8,512,256]{2,1,0:T(8,128)(2,1)} %get-tuple-element.69) | copy-start | bytes 6291460
  475.6 9.3 %copy-start.48 = (bf16[2,256,1024]{2,1,0:T(8,128)(2,1)S(1)}, bf16[2,256,1024]{2,1,0:T(8,128)(2,1)}, u32[]{:S(2)}) copy-start(bf16[2,256,1024]{2,1,0:T(8,128)(2,1)} %get-tuple-element.86) | copy-start | bytes 3145732
  490.5 10.1 %copy-start.41 = (f32[32,64]{1,0:T(8,128)S(1)}, f32[32,64]{1,0:T(8,128)}, u32[]{:S(2)}) copy-start(f32[32,64]{1,0:T(8,128)} %get-tuple-element.89) | copy-start | bytes 24580
  490.5 10.1 %copy-start.42 = (f32[32,64]{1,0:T(8,128)S(1)}, f32[32,64]{1,0:T(8,128)}, u32[]{:S(2)}) copy-start(f32[32,64]{1,0:T(8,128)} %get-tuple-element.88) | copy-start | bytes 24580
  490.5 12.4 %copy-start.40 = (f32[2,8,128]{2,1,0:T(8,128)S(1)}, f32[2,8,128]{2,1,0:T(8,128)}, u32[]{:S(2)}) copy-start(f32[2,8,128]{2,1,0:T(8,128)} %get-tuple-element.90) | copy-start | bytes 24580
  729.4 8.1 %copy-start.14 = (f32[4,1024,256]{2,1,0:T(8,128)S(1)}, f32[4,1024,256]{2,1,0:T(8,128)}, u32[]{:S(2)}) copy-start(f32[4,1024,256]{2,1,0:T(8,128)} %get-tuple-element.92) | copy-start | bytes 12582916
  729.4 8.1 %copy-start.16 = (f32[1024,256]{1,0:T(8,128)S(1)}, f32[1024,256]{1,0:T(8,128)}, u32[]{:S(2)}) copy-start(f32[1024,256]{1,0:T(8,128)} %param.35) | copy-start | bytes 3145732
  729.4 8.0 %copy-start.18 = (f32[1024,256]{1,0:T(8,128)S(1)}, f32[1024,256]{1,0:T(8,128)}, u32[]{:S(2)}) copy-start(f32[1024,256]{1,0:T(8,128)} %param.33) | copy-start | bytes 3145732
  729.4 8.0 %copy-start.27 = (f32[1024,256]{1,0:T(8,128)S(1)}, f32[1024,256]{1,0:T(8,128)}, u32[]{:S(2)}) copy-start(f32[1024,256]{1,0:T(8,128)} %param.41) | copy-start | bytes 3145732
  729.4 8.0 %copy-start.28 = (f32[1024,256]{1,0:T(8,128)S(1)}, f32[1024,256]{1,0:T(8,128)}, u32[]{:S(2)}) copy-start(f32[1024,256]{1,0:T(8,128)} %param.47) | copy-start | bytes 3145732
  729.4 8.0 %copy-start.29 = (f32[1024,256]{1,0:T(8,128)S(1)}, f32[1024,256]{1,0:T(8,128)}, u32[]{:S(2)}) copy-start(f32[1024,256]{1,0:T(8,128)} %param.45) | copy-start | bytes 3145732
  729.4 8.6 %copy-start.30 = (f32[1024,256]{1,0:T(8,128)S(1)}, f32[1024,256]{1,0:T(8,128)}, u32[]{:S(2)}) copy-start(f32[1024,256]{1,0:T(8,128)} %param.39) | copy-start | bytes 3145732
  738.1 4.1 copy-start.12
  738.1 4.2 copy-start.21
  738.1 5.4 copy-start.22
  743.5 4.2 copy-start.33
  743.5 4.2 copy-start.36
  743.5 4.2 copy-start.37
  743.5 5.3 copy-start.39
  743.5 5.3 copy-start.44
  743.5 5.3 copy-start.45

commit v3 on v2

v3 whole, which is shorter than its diff:
```python
import functools

import jax
import jax.numpy as jnp
from jax import lax
from jax.experimental import pallas as pl
from jax.experimental.pallas import tpu as pltpu
from jax.sharding import PartitionSpec as P

STEP = 5
HIGH = lax.Precision.HIGHEST
NORM_EPS = 1e-06
CLIP = 0.01
LEARN = 0.02
DECAY = 0.1
BETA_ONE = 0.5
BETA_TWO = 0.5
ADAM_EPS = 1e-08
SCORE_SCALE = 0.125
MESH = pl.DeviceIdType.MESH
F32 = jnp.float32
BF16 = jnp.bfloat16
ANY = pl.BlockSpec(memory_space=pl.ANY)
VM = pl.BlockSpec(memory_space=pltpu.VMEM)

ROWS_YZ = 320
HALF_YZ = 160
QUARTER = 48


def place():
    dp = lax.axis_index("dp")
    sq = lax.axis_index("seq")
    core = lax.rem(dp, 2)
    y = lax.rem(dp // 2, 4)
    z = lax.rem(sq, 2) * 2 + dp // 8
    return sq // 2, y, z, core


def at(x, y, z, core):
    x, y, z = lax.rem(x + 4, 4), lax.rem(y + 4, 4), lax.rem(z + 4, 4)
    return (lax.rem(z, 2) * 8 + y * 2 + core, x * 2 + z // 2)


def greet(devices):
    bar = pltpu.get_barrier_semaphore()
    for device in devices:
        pl.semaphore_signal(bar, inc=1, device_id=device, device_id_type=MESH)
    pl.semaphore_wait(bar, len(devices))


def remote(src, dst, send, recv, device):
    return pltpu.make_async_remote_copy(
        src_ref=src, dst_ref=dst, send_sem=send, recv_sem=recv, device_id=device, device_id_type=MESH
    )


def params(collective_id, vmem=None):
    return pltpu.CompilerParams(
        collective_id=collective_id, has_side_effects=True, vmem_limit_bytes=vmem
    )


def group_peers():
    dp = lax.axis_index("dp")
    sq = lax.axis_index("seq")
    core = lax.rem(dp, 2)
    out = [(dp + 1 - 2 * core, sq)]
    for i in range(1, 8):
        for flip in range(2):
            out.append((dp + flip * (1 - 2 * core), lax.rem(sq + i, 8)))
    return out


def head_lanes(pair, core):
    return pl.ds(pl.multiple_of(((pair // 2 * 2 + core) * 2 + lax.rem(pair, 2)) * 128, 128), 128)


NT = (((1,), (1,)), ((), ()))


def normalize(v):
    center = v - jnp.mean(v, -1, keepdims=True)
    spread = jnp.mean(center * center, -1, keepdims=True)
    return center * lax.rsqrt(spread + NORM_EPS)


def ada_row(ada, k, img):
    return jnp.concatenate([ada[2 * k, img : img + 1, :], ada[2 * k + 1, img : img + 1, :]], axis=1)


def column_of(row):
    return jnp.transpose(jnp.broadcast_to(row, (128, 128)))


def forward_kernel(
    msg, slots, table, cond_w, x_in, s,
    msg_all, slots_all, cond_all, emb_out, ada, loss_out,
    w_o, wo_o, h1_o, h2_o, h3_o, hb_o, ot_o, att_o, x1_o, mlp_o, x2_o, f_o, u_o, dl_o,
    w, wo, h1, h2, h3, src, hb, oh, ot, att, x1, mlp, x2, acc, got_acc, f, u, dl,
    cond_own, ada_own, bias, qcol, tcol, wcol, stats,
    gs, gr, gl, os, orr, s1, r1, s2, r2, s3, r3, s4, r4, ps, pr, as_, ar, al, ts, tr, tl, outs_sem,
):
    x, y, z, c = place()
    dp = lax.axis_index("dp")
    sq = lax.axis_index("seq")
    zl = lax.rem(z, 2)
    up, down, far = lax.rem(y + 1, 4), lax.rem(y + 3, 4), lax.rem(y + 2, 4)
    yp, ym = at(x, y + 1, z, c), at(x, y - 1, z, c)
    zp, zm = at(x, y, z + 1, c), at(x, y, z - 1, c)
    xp, xm = at(x + 1, y, z, c), at(x - 1, y, z, c)
    zs = at(x, y, z + 1 - 2 * c, c)
    mate = at(x, y, z, 1 - c)
    base = dp - c
    row = [(lax.rem(dp + i, 16), sq) for i in range(1, 16)]
    group = group_peers()
    greet(row + group[1:] + [at(x, y, z + 2 * zl - 1, c)])

    pending = []

    def keep(k, src_ref, dst_ref):
        cp = pltpu.make_async_copy(src_ref, dst_ref, outs_sem.at[k])
        cp.start()
        pending.append(cp)
        return cp

    def rows_at(j, start, count):
        return pl.ds(512 * (j % 2) + start, count)

    def quarter(j, pos):
        start = 512 * (j % 2) + ROWS_YZ + QUARTER * lax.rem(pos + 4, 4)
        return pl.ds(pl.multiple_of(start, 16), QUARTER)

    sent = []

    def go(j, k, a, b, device):
        cp = remote(a, b, gs.at[j, k], gr.at[j, k], device)
        cp.start()
        sent.append(cp)

    def got(j, k, ref):
        remote(ref, ref, gs.at[j, k], gr.at[j, k], mate).wait_recv()

    def stage(kind, j):
        m = j // 2
        full, first = rows_at(j, 0, ROWS_YZ), rows_at(j, 0, HALF_YZ)
        second, mine = rows_at(j, HALF_YZ, HALF_YZ), quarter(j, x)
        own = []
        if kind in "AB":
            for i, rows in enumerate((full, mine)):
                own.append(pltpu.make_async_copy(s.at[m, rows], w.at[zl, y, m, rows], gl.at[j, i]))
        if kind == "A":
            go(j, 0, s.at[m, full], w.at[zl, y, m, full], yp)
            go(j, 1, s.at[m, full], w.at[zl, y, m, full], ym)
            go(j, 6, s.at[m, mine], w.at[zl, y, m, mine], zs)
            for cp in own:
                cp.start()
        if kind == "B":
            for cp in own:
                cp.wait()
            got(j, 6, w.at[1 - zl, y, m, mine])
            go(j, 7, w.at[:, y, m, mine], w.at[:, y, m, mine], yp)
            go(j, 8, w.at[:, y, m, mine], w.at[:, y, m, mine], ym)
            got(j, 0, w.at[zl, down, m, full])
            got(j, 1, w.at[zl, up, m, full])
            go(j, 2, w.at[zl, down, m, first], w.at[zl, down, m, first], yp)
            go(j, 3, w.at[zl, up, m, second], w.at[zl, up, m, second], ym)
        if kind == "C":
            got(j, 7, w.at[:, down, m, mine])
            got(j, 8, w.at[:, up, m, mine])
            go(j, 9, w.at[0, down, m, mine], w.at[0, down, m, mine], yp)
            go(j, 10, w.at[1, up, m, mine], w.at[1, up, m, mine], ym)
            got(j, 2, w.at[zl, far, m, first])
            got(j, 3, w.at[zl, far, m, second])
            go(j, 4, w.at[zl, :, m, first], w.at[zl, :, m, first], zp)
            go(j, 5, w.at[zl, :, m, second], w.at[zl, :, m, second], zm)
        if kind == "D":
            got(j, 9, w.at[0, far, m, mine])
            got(j, 10, w.at[1, far, m, mine])
            go(j, 11, w.at[:, :, m, mine], w.at[:, :, m, mine], xp)
            go(j, 12, w.at[:, :, m, mine], w.at[:, :, m, mine], xm)
        if kind == "E":
            left, right = quarter(j, x - 1), quarter(j, x + 1)
            got(j, 11, w.at[:, :, m, left])
            got(j, 12, w.at[:, :, m, right])
            go(j, 13, w.at[0, :, m, left], w.at[0, :, m, left], xp)
            go(j, 14, w.at[1, :, m, right], w.at[1, :, m, right], xm)
        if kind == "F":
            across = quarter(j, x + 2)
            got(j, 4, w.at[1 - zl, :, m, first])
            got(j, 5, w.at[1 - zl, :, m, second])
            got(j, 13, w.at[0, :, m, across])
            got(j, 14, w.at[1, :, m, across])
            if j % 2:
                keep(m, w.at[:, :, m], w_o.at[:, :, m])
            if j == 1:
                for i in range(2):
                    remote(w.at[1, 2 + i, 0], wo.at[2 * i + c], os.at[i], orr.at[i], mate).start()
                    pltpu.make_async_copy(w.at[1, 2 + i, 0], wo.at[2 * i + c], gl.at[i, 2]).start()

    wave = [
        ["A0"], ["A1"], ["B0", "A2"], ["B1", "C0", "A3"],
        ["C1", "D0", "B2", "A4"], ["D1", "E0", "C2", "B3", "A5"], ["E1", "F0", "D2", "C3", "B4"], ["F1"],
        ["E2", "D3", "C4", "B5", "A6"],
        ["F2", "E3", "D4", "C5", "B6", "A7"], ["F3", "E4", "D5", "C6", "B7"], ["F4", "E5", "D6", "C7"],
        ["F5", "E6", "D7"], ["F6", "E7"], ["F7"],
    ]

    def pump(n=1):
        for _ in range(n):
            if wave:
                for item in wave.pop(0):
                    stage(item[0], int(item[1]))

    firsts = []
    for i, to in enumerate(row):
        cp = remote(msg, msg_all.at[dp], s1.at[i], r1.at[i], to)
        cp.start()
        firsts.append(cp)
    msg_all[dp] = msg[...]
    pump()
    for cp in firsts:
        cp.wait()
    seen = msg_all[...]
    count = jnp.sum(seen[:, 10, 2:3], axis=0, keepdims=True)
    slots[8:9, :] = jnp.broadcast_to(count, (1, 128))
    for d in range(16):
        bias[pl.ds(10 * d, 10), :] = seen[d, 0:10, :]
    seconds = []
    for i, to in enumerate(group):
        cp = remote(slots, slots_all.at[sq * 2 + c], s2.at[i], r2.at[i], to)
        cp.start()
        seconds.append(cp)
    slots_all[sq * 2 + c] = slots[...]
    classes = table.shape[1]
    lane = lax.broadcasted_iota(jnp.int32, (32, classes), 1)
    labels = jnp.concatenate([seen[d, 10:11, i : i + 1] for d in range(16) for i in range(2)], axis=0)
    hit = jnp.where(lane == labels.astype(jnp.int32), 1.0, 0.0).astype(BF16)
    emb = lax.dot_general(hit, table[...], NT, preferred_element_type=F32)
    emb_out[...] = emb
    cond_own[...] = (emb / (1.0 + jnp.exp(-emb))).astype(BF16)
    cond_all[dp] = cond_own[...]
    thirds = []
    for i, to in enumerate(row):
        cp = remote(cond_own, cond_all.at[dp], s3.at[i], r3.at[i], to)
        cp.start()
        thirds.append(cp)
    pump()
    for cp in thirds:
        cp.wait()
    total = jnp.zeros((32, 512), F32)
    for d in range(16):
        total += jnp.dot(cond_all[d], cond_w[pl.ds(64 * d, 64), :], preferred_element_type=F32)
    total += jnp.concatenate([bias[pl.ds(dp * 4 + i, 1), :] for i in range(4)], axis=1)
    for d in range(16):
        ada_own[d] = total[2 * d : 2 * d + 2]
    fourths = []
    for i in range(15):
        to = lax.rem(dp + 1 + i, 16)
        cp = remote(ada_own.at[to], ada.at[dp], s4.at[i], r4.at[i], (to, sq))
        cp.start()
        fourths.append(cp)
    ada[dp] = ada_own[dp]
    pump()
    for cp in fourths:
        cp.wait()
    for cp in seconds:
        cp.wait()

    owner = lax.rem(sq, 2)
    for img in range(2):
        for g in range(8):
            qcol[img, g] = column_of(slots_all[g * 2 + owner, pl.ds(2 + img, 1), :])
        for q in range(2):
            at_rows = pl.ds((q * 2 + img) * 128, 128)
            tcol[at_rows, :] = column_of(slots_all[sq * 2 + q, pl.ds(4 + img, 1), :])
            wcol[at_rows, :] = column_of(slots_all[sq * 2 + q, pl.ds(6 + img, 1), :])
    true_count = jnp.sum(
        jnp.concatenate([slots_all[2 * g, 8:9, 0:1] for g in range(8)], axis=0), axis=0, keepdims=True
    )

    def blocks(fn):
        for img in range(2):
            def body(i, carry, img=img):
                fn(img, pl.ds(pl.multiple_of(img * 128 + i * 32, 32), 32))
                return carry
            lax.fori_loop(0, 4, body, 0)

    def exchange(k, ref):
        cp = remote(ref.at[c], ref.at[c], ps.at[k], pr.at[k], mate)
        cp.start()
        return cp

    def modulated(img, v, scale, shift):
        return (normalize(v) * (1.0 + ada_row(ada, scale, img)) + ada_row(ada, shift, img)).astype(BF16)

    def do_h1(img, rows):
        h1[c, rows, :] = modulated(img, x_in[rows, :].astype(F32), 2, 4)

    blocks(do_h1)
    cp = exchange(0, h1)
    pump()
    cp.wait()
    keep(4, h1, h1_o)
    pump(4)

    def bias_row(start):
        return jnp.concatenate([bias[pl.ds(start, 1), :], bias[pl.ds(start + 1, 1), :]], axis=1)

    tokens = h1[...].reshape(512, 1024)
    for j in range(6):
        t, jj = j // 2, j % 2
        val = jnp.dot(tokens, w[j // 4, j % 4, 0], preferred_element_type=F32)
        if t != 1:
            val = val + bias_row(64 + (0 if t == 0 else 8) + (2 * jj + c) * 2)
        val = val.astype(BF16)
        for half in range(2):
            for ip in range(2):
                src[(jj * 2 + half) * 2 + ip, t] = val[
                    ip * 256 : ip * 256 + 256, half * 128 : half * 128 + 128
                ].reshape(2, 128, 128)
    cps = []
    for i in range(1, 8):
        to = lax.rem(sq + i, 8)
        cp = remote(src.at[to], hb.at[sq], as_.at[i], ar.at[i], (dp, to))
        cp.start()
        cps.append(cp)
    hb[sq] = src[sq]
    pump()
    for cp in cps:
        cp.wait()
    keep(5, hb, hb_o)

    low_lanes = lax.broadcasted_iota(jnp.int32, (256, 128), 1) < 64

    def attend_block(i, carry):
        img, qb = i // 4, lax.rem(i, 4)
        q = jnp.concatenate([hb[2 * qb, 0, img], hb[2 * qb + 1, 0, img]], axis=0)
        k = jnp.concatenate([hb[g, 1, img] for g in range(8)], axis=0)
        v = jnp.concatenate([hb[g, 2, img] for g in range(8)], axis=0)
        key = jnp.concatenate([slots_all[g * 2 + owner, pl.ds(img, 1), :] for g in range(8)], axis=1)
        query = jnp.concatenate([qcol[img, 2 * qb], qcol[img, 2 * qb + 1]], axis=0)[:, 0:1]
        seen_by = key <= query
        heads = []
        for h in range(2):
            mask = low_lanes if h == 0 else jnp.logical_not(low_lanes)
            qh = jnp.where(mask, q, jnp.zeros_like(q))
            sc = lax.dot_general(qh, k, NT, preferred_element_type=F32) * SCORE_SCALE
            sc = jnp.where(seen_by, sc, -1e30)
            e = jnp.exp(sc - jnp.max(sc, axis=-1, keepdims=True))
            p = (e / jnp.sum(e, axis=-1, keepdims=True)).astype(BF16)
            heads.append(jnp.dot(p, v, preferred_element_type=F32))
        o = jnp.where(low_lanes, heads[0], heads[1]).astype(BF16)
        oh[2 * qb, img] = o[:128]
        oh[2 * qb + 1, img] = o[128:]
        return carry

    for i in range(0, 8, 2):
        lax.fori_loop(i, i + 2, attend_block, 0)
        if i < 6:
            pump()
    pair = sq // 2
    lanes = head_lanes(pair, c)

    def o_copy(i, img):
        to = lax.rem(sq + i, 8)
        return remote(
            oh.at[to, img], ot.at[pl.ds(img * 128, 128), lanes], ts.at[i, img], tr.at[pair, c, img],
            (base + owner, to),
        )

    for img in range(2):
        for i in range(1, 8):
            o_copy(i, img).start()

        @pl.when(owner == c)
        def _():
            ot[pl.ds(img * 128, 128), lanes] = oh[sq, img]

        @pl.when(owner != c)
        def _():
            o_copy(0, img).start()

    pump()
    for img in range(2):
        for p in range(4):
            for q in range(2):
                view = ot.at[pl.ds(img * 128, 128), pl.ds(((p // 2 * 2 + q) * 2 + p % 2) * 128, 128)]

                @pl.when(jnp.logical_or(sq != p * 2 + c, c != q))
                def _():
                    remote(view, view, ts.at[0, img], tr.at[p, q, img], mate).wait_recv()

    keep(6, ot, ot_o)
    for i in range(2):
        remote(w.at[1, 2 + i, 0], wo.at[2 * i + c], os.at[i], orr.at[i], mate).wait()
        pltpu.make_async_copy(w.at[1, 2 + i, 0], wo.at[2 * i + c], gl.at[i, 2]).wait()
    keep(7, wo, wo_o)
    for k in range(4):
        cols = pl.ds(256 * k, 256)
        att[:, cols] = jnp.dot(ot[...], wo[k], preferred_element_type=F32) + bias_row(80 + 2 * k)
    keep(8, att, att_o)

    def do_h2(img, rows):
        v = x_in[rows, :].astype(F32) + ada_row(ada, 0, img) * att[rows, :]
        x1[rows, :] = v
        h2[c, rows, :] = modulated(img, v, 3, 5)

    blocks(do_h2)
    cp = exchange(1, h2)
    keep(9, x1, x1_o)
    cp.wait()
    keep(10, h2, h2_o)
    pump()

    def chunk(ref, j, kind):
        return ref[j // 4, lax.rem(j, 4), kind]

    def do_f(j, carry):
        val = jnp.dot(h2[...].reshape(512, 1024), chunk(w, j, 1), preferred_element_type=F32)
        val = val + bias_row(88 + (2 * j + c) * 2)
        f[j] = val
        act = jax.nn.gelu(val, approximate=True).astype(BF16)
        u[j] = act
        part = lax.dot_general(act, chunk(w, j, 2), NT, preferred_element_type=F32).reshape(2, 256, 1024)

        @pl.when(j == 0)
        def _():
            acc[...] = part

        @pl.when(j > 0)
        def _():
            acc[...] += part

        return carry

    lax.fori_loop(0, 8, do_f, 0)
    f_copy = keep(11, f, f_o)
    keep(12, u, u_o)
    cp = remote(acc.at[1 - c], got_acc, ps.at[2], pr.at[2], mate)
    cp.start()
    pump()
    b_two = jnp.concatenate([bias[pl.ds(120 + i, 1), :] for i in range(8)], axis=1)
    cp.wait()

    def do_h3(img, rows):
        m = acc[c, rows, :] + got_acc[rows, :] + b_two
        mlp[rows, :] = m
        v = x1[rows, :] + ada_row(ada, 1, img) * m
        x2[rows, :] = v
        h3[c, rows, :] = modulated(img, v, 6, 7)

    blocks(do_h3)
    cp = exchange(3, h3)
    keep(13, mlp, mlp_o)
    keep(14, x2, x2_o)
    f_copy.wait()
    pending[:] = [p for p in pending if p is not f_copy]
    cp.wait()
    keep(15, h3, h3_o)

    def do_logits(j, top):
        val = jnp.dot(h3[...].reshape(512, 1024), chunk(w, j, 3), preferred_element_type=F32)
        val = val + bias_row(128 + (2 * j + c) * 2)
        f[j] = val
        return jnp.maximum(top, jnp.max(val, axis=-1, keepdims=True))

    top = lax.fori_loop(0, 8, do_logits, jnp.full((512, 1), -jnp.inf, F32))
    inner = lax.broadcasted_iota(jnp.int32, (512, 256), 1)

    def target_hit(j):
        return inner == (tcol[:, 0:1].astype(jnp.int32) - (2 * j + c) * 256)

    def do_mass(j, carry):
        mass, picked = carry
        val = f[j]
        mass = mass + jnp.sum(jnp.exp(val - top), axis=-1, keepdims=True)
        picked = picked + jnp.sum(jnp.where(target_hit(j), val, 0.0), axis=-1, keepdims=True)
        return mass, picked

    zero = jnp.zeros((512, 1), F32)
    mass, picked = lax.fori_loop(0, 8, do_mass, (zero, zero))
    lane = lax.broadcasted_iota(jnp.int32, (512, 128), 1)
    stats[c] = jnp.where(lane == 0, top, jnp.where(lane == 1, mass, picked))
    cp = exchange(4, stats)
    cp.wait()
    both = [stats[0], stats[1]]
    top_all = jnp.maximum(both[0][:, 0:1], both[1][:, 0:1])
    mass_all = sum(b[:, 1:2] * jnp.exp(b[:, 0:1] - top_all) for b in both)
    log_total = top_all + jnp.log(mass_all)
    weight = wcol[:, 0:1]
    losses = weight * (log_total - (both[0][:, 2:3] + both[1][:, 2:3]))
    loss_out[...] = jnp.broadcast_to(0.5 * jnp.sum(losses, axis=0, keepdims=True), (8, 128))
    share = weight / true_count

    def do_dlogits(j, carry):
        grad = share * (jnp.exp(f[j] - log_total) - jnp.where(target_hit(j), 1.0, 0.0))
        dl[j] = grad.astype(BF16)
        return carry

    lax.fori_loop(0, 8, do_dlogits, 0)
    keep(16, dl, dl_o)
    for img in range(2):
        for i in range(1, 8):
            o_copy(i, img).wait_send()

        @pl.when(owner != c)
        def _():
            o_copy(0, img).wait_send()

    for cp in sent:
        cp.wait_send()
    for cp in pending:
        cp.wait()


def forward_pass(msg, slots, table, cond_w, x_rows, shard):
    dma = pltpu.SemaphoreType.DMA
    sd = jax.ShapeDtypeStruct
    kept = [
        sd((2, 4, 4, 1024, 256), BF16), sd((4, 1024, 256), BF16),
        sd((2, 256, 1024), BF16), sd((2, 256, 1024), BF16), sd((2, 256, 1024), BF16),
        sd((8, 3, 2, 128, 128), BF16), sd((256, 1024), BF16),
        sd((256, 1024), F32), sd((256, 1024), F32), sd((256, 1024), F32), sd((256, 1024), F32),
        sd((8, 512, 256), F32), sd((8, 512, 256), BF16), sd((8, 512, 256), BF16),
    ]
    vm = pltpu.VMEM
    return pl.pallas_call(
        forward_kernel,
        out_shape=[
            sd((16, 16, 128), F32), sd((16, 16, 128), F32), sd((16, 32, 64), BF16),
            sd((32, 64), F32), sd((16, 2, 512), F32), sd((8, 128), F32),
        ] + kept,
        in_specs=[VM] * 5 + [ANY],
        out_specs=[VM] * 6 + [ANY] * len(kept),
        scratch_shapes=[
            vm((2, 4, 4, 1024, 256), BF16), vm((4, 1024, 256), BF16),
            vm((2, 256, 1024), BF16), vm((2, 256, 1024), BF16), vm((2, 256, 1024), BF16),
            vm((8, 3, 2, 128, 128), BF16), vm((8, 3, 2, 128, 128), BF16), vm((8, 2, 128, 128), BF16),
            vm((256, 1024), BF16),
            vm((256, 1024), F32), vm((256, 1024), F32), vm((256, 1024), F32), vm((256, 1024), F32),
            vm((2, 256, 1024), F32), vm((256, 1024), F32),
            vm((8, 512, 256), F32), vm((8, 512, 256), BF16), vm((8, 512, 256), BF16),
            vm((32, 64), BF16), vm((16, 2, 512), F32), vm((160, 128), F32),
            vm((2, 8, 128, 128), F32), vm((512, 128), F32), vm((512, 128), F32), vm((2, 512, 128), F32),
            dma((8, 15)), dma((8, 15)), dma((8, 3)), dma((2,)), dma((2,)),
            dma((15,)), dma((15,)), dma((15,)), dma((15,)), dma((15,)), dma((15,)), dma((15,)), dma((15,)),
            dma((5,)), dma((5,)), dma((8,)), dma((8,)), dma,
            dma((8, 2)), dma((4, 2, 2)), dma, dma((17,)),
        ],
        compiler_params=params(0, 63 * 2**20),
    )(msg, slots, table, cond_w, x_rows, shard)


PART_ROWS = (16, 24, 24)
PART_BASE = (0, 128, 320)
ORDERS = ("xyz", "yzx", "zxy")
SLOTS = 3
JOBS = 8


def block_cut(order, phase, rows):
    axis, later = order[phase], order[phase + 1 :]
    if axis != "z" and "z" in later:
        return ("zl", slice(0, 1), slice(1, 2))
    if "y" in later:
        return ("y", slice(0, 2), slice(2, 4))
    if "x" in later:
        return ("x", slice(0, 2), slice(2, 4))
    cut = (rows // 8 + 1) // 2 * 8
    return ("r", slice(0, cut), slice(cut, rows))


def block_dims(part, phase):
    later = ORDERS[part][phase + 1 :]
    return {
        "zl": 2 if "z" in later else 1,
        "y": 4 if "y" in later else 1,
        "x": 4 if "x" in later else 1,
        "zh": 2 if "z" in later else 1,
        "r": PART_ROWS[part],
    }


def recv_shapes():
    shapes = []
    for p in range(3):
        for ph in range(3):
            name, one, two = block_cut(ORDERS[p], ph, PART_ROWS[p])
            for k in range(4 if ph < 2 else 3):
                d = dict(block_dims(p, ph))
                if ph < 2 and k < 2:
                    cut = (one, two)[k]
                    d[name] = cut.stop - cut.start
                shapes.append((SLOTS, d["zl"], d["y"], d["x"], d["zh"], d["r"], 256))
    return shapes


def backward_kernel(*refs):
    names = [
        "msg_all", "slots_all", "cond_all", "emb", "ada", "loss", "cond_w", "x_in", "w_i", "wo_i",
        "h1_i", "h2_i", "h3_i", "hb_i", "ot_i", "att_i", "x1_i", "mlp_i", "x2_i", "f_i", "u_i", "dl_i",
        "out", "norm", "bias_sum", "gtable", "gcond", "wb", "dl", "u", "fb", "hh", "hT", "oT", "dm",
        "otp", "da", "acc", "got", "xa", "xb", "dx", "hb", "doh", "dov", "dkv", "dsrc", "dr", "dq6",
        "kcol", "dmod", "biasp", "smsg", "sgot", "smine", "sall", "spart", "sback", "gst", "gcs",
        "tile", "tiles",
    ]
    names += ["g%d" % i for i in range(3 * SLOTS)] + ["st0", "st1", "st2"]
    n = len(names)
    r = dict(zip(names, refs[:n]))
    rest = list(refs[n:])
    recv = {}
    for p in range(3):
        for ph in range(3):
            count = 4 if ph < 2 else 3
            recv[p, ph] = rest[:count]
            rest = rest[count:]
    (
        ls, fs, ps, pr, hs, hr, hl, as_, ar, js, jr, gss, grs, ol, credit,
        s1, r1, s2, r2, s3, r3, ns, nr, gl,
    ) = rest
    msg_all, slots_all, ada, biasp, dmod = r["msg_all"], r["slots_all"], r["ada"], r["biasp"], r["dmod"]
    dl, u, hT, oT, acc, got = r["dl"], r["u"], r["hT"], r["oT"], r["acc"], r["got"]
    dx, xa, xb, wb, hh = r["dx"], r["xa"], r["xb"], r["wb"], r["hh"]
    dm, otp, da, tile = r["dm"], r["otp"], r["da"], r["tile"]
    parts = [[r["g%d" % (s * 3 + p)] for p in range(3)] for s in range(SLOTS)]
    stage_out = [r["st0"], r["st1"], r["st2"]]
    out = r["out"]

    x, y, z, c = place()
    dp = lax.axis_index("dp")
    sq = lax.axis_index("seq")
    zl, zh = lax.rem(z, 2), z // 2
    base = dp - c
    owner = lax.rem(sq, 2)
    pair = sq // 2
    mate = at(x, y, z, 1 - c)
    row = [lax.rem(dp + i, 16) for i in range(1, 16)]
    line = [lax.rem(sq + i, 8) for i in range(1, 8)]
    greet([(d, sq) for d in row] + group_peers()[1:] + [at(x, y, z + 2 * zl - 1, c)])
    here = {"x": x, "y": y, "z": z}

    def step(axis, by):
        q = dict(here)
        q[axis] = q[axis] + by
        return at(q["x"], q["y"], q["z"], c)

    def load(k, src, dst):
        cp = pltpu.make_async_copy(src, dst, ls.at[k])
        cp.start()
        return cp

    loads = {
        "h3": load(0, r["h3_i"], hh),
        "dl": load(1, r["dl_i"], dl),
        "w3": load(2, r["w_i"].at[:, :, 3], wb),
        "x2": load(3, r["x2_i"], xa),
        "mlp": load(4, r["mlp_i"], xb),
        "u": load(5, r["u_i"], u),
        "hb": load(6, r["hb_i"], r["hb"]),
        "ot": load(8, r["ot_i"], otp.at[c]),
    }

    def view(ref, p, ph, index, half=None):
        order = ORDERS[p]
        sel = {}
        for i, a in enumerate(order):
            sel[a] = here[a] if i < ph else (lax.rem(index + 4, 4) if i == ph else None)
        idx = {
            "zl": slice(0, 2) if sel["z"] is None else pl.ds(lax.rem(sel["z"], 2), 1),
            "y": slice(0, 4) if sel["y"] is None else pl.ds(sel["y"], 1),
            "x": slice(0, 4) if sel["x"] is None else pl.ds(sel["x"], 1),
            "zh": slice(0, 2) if sel["z"] is None else pl.ds(sel["z"] // 2, 1),
            "r": slice(0, PART_ROWS[p]),
        }
        if half is not None:
            name, one, two = block_cut(order, ph, PART_ROWS[p])
            idx[name] = (one, two)[half]
        return ref.at[idx["zl"], idx["y"], idx["x"], idx["zh"], idx["r"]]

    def add(dst, srcs):
        d0, d1, d2, d3 = dst.shape[:4]

        def body(i, carry):
            a, b = i // d1, lax.rem(i, d1)
            for cc in range(d2):
                for d in range(d3):
                    val = dst[a, b, cc, d]
                    for s in srcs:
                        val = val + s[a, b, cc, d]
                    dst[a, b, cc, d] = val
            return carry

        if d0 * d1 == 1:
            body(0, 0)
        else:
            lax.fori_loop(0, d0 * d1, body, 0)

    neighbours = [step(a, b) for a in "xyz" for b in (1, -1)]
    unsent = []

    def phases(j, slot, again, reused):
        mine = []
        if again:
            pl.semaphore_wait(credit.at[slot], 6)

        def go(p, ph, k, src, dst, device):
            cp = remote(src, dst, js.at[j, p * 3 + ph, k], jr.at[j, p * 3 + ph, k], device)
            cp.start()
            mine.append(cp)

        def arrived(p, ph, k, ref):
            remote(ref, ref, js.at[j, p * 3 + ph, k], jr.at[j, p * 3 + ph, k], mate).wait_recv()

        for ph in range(3):
            info = []
            for p in range(3):
                a = ORDERS[p][ph]
                info.append((p, a, here[a], parts[slot][p], [b.at[slot] for b in recv[p, ph]]))
            if ph == 2:
                for p, a, i, g, bufs in info:
                    for k, by in enumerate((1, -1, 2)):
                        go(p, ph, k, view(g, p, ph, i + by), bufs[k], step(a, by))
                yield
                for p, a, i, g, bufs in info:
                    for k in range(3):
                        arrived(p, ph, k, bufs[k])
                    add(view(g, p, ph, i), bufs)
                break
            for p, a, i, g, bufs in info:
                go(p, ph, 0, view(g, p, ph, i + 2, 0), bufs[0], step(a, 1))
                go(p, ph, 1, view(g, p, ph, i + 2, 1), bufs[1], step(a, -1))
            yield
            for p, a, i, g, bufs in info:
                arrived(p, ph, 0, bufs[0])
                add(view(g, p, ph, i + 1, 0), [bufs[0]])
                go(p, ph, 2, view(g, p, ph, i + 1), bufs[2], step(a, 1))
                arrived(p, ph, 1, bufs[1])
                add(view(g, p, ph, i - 1, 1), [bufs[1]])
                go(p, ph, 3, view(g, p, ph, i - 1), bufs[3], step(a, -1))
            yield
            for p, a, i, g, bufs in info:
                arrived(p, ph, 2, bufs[2])
                arrived(p, ph, 3, bufs[3])
                add(view(g, p, ph, i), [bufs[2], bufs[3]])
        for p in range(3):
            val = parts[slot][p][zl, y, x, zh]
            stage_out[p][j] = val
            square = val * val
            total = tile[...]
            for t in range(PART_ROWS[p] // 8):
                for k in range(2):
                    total = total + square[8 * t : 8 * t + 8, 128 * k : 128 * k + 128]
            tile[...] = total
        for cp in mine:
            cp.wait_send()
        if reused():
            for device in neighbours:
                pl.semaphore_signal(credit.at[slot], inc=1, device_id=device, device_id_type=MESH)

    def tail(j):
        kind, half = JOB_KIND[j // 2], j % 2
        o = out.at[kind]

        def rows_of(p, xi, zi, count):
            n_rows = PART_ROWS[p]
            start = half * 512 + PART_BASE[p] + (lax.rem(xi + 4, 4) * 2 + zi) * n_rows
            return pl.ds(pl.multiple_of(start, 8), count * n_rows)

        def go(p, k, src, rows, device):
            cp = remote(src, o.at[rows], gss.at[j, p, k], grs.at[j, p, k], device)
            cp.start()
            unsent.append(cp)

        def arrived(p, k, rows):
            remote(o.at[rows], o.at[rows], gss.at[j, p, k], grs.at[j, p, k], mate).wait_recv()

        own = []
        for p in range(3):
            rows = rows_of(p, x, zh, 1)
            cp = pltpu.make_async_copy(stage_out[p].at[j], o.at[rows], ol.at[j, p])
            cp.start()
            own.append(cp)
            go(p, 0, stage_out[p].at[j], rows, step("z", 2))
        yield
        for p in range(3):
            own[p].wait()
            arrived(p, 0, rows_of(p, x, 1 - zh, 1))
            both = rows_of(p, x, 0, 2)
            go(p, 1, o.at[both], both, step("x", 1))
            go(p, 2, o.at[both], both, step("x", -1))
        yield
        for p in range(3):
            arrived(p, 1, rows_of(p, x - 1, 0, 2))
            arrived(p, 2, rows_of(p, x + 1, 0, 2))
            left, right = rows_of(p, x - 1, 0, 1), rows_of(p, x + 1, 1, 1)
            go(p, 3, o.at[left], left, step("x", 1))
            go(p, 4, o.at[right], right, step("x", -1))
        yield
        for p in range(3):
            arrived(p, 3, rows_of(p, x + 2, 0, 1))
            arrived(p, 4, rows_of(p, x + 2, 1, 1))

    JOB_KIND = (3, 2, 1, 0)

    def transpose_into(dst, src):
        def body(i, carry):
            cols = pl.ds(pl.multiple_of(i * 128, 128), 128)
            dst[cols, :] = jnp.transpose(src[:, :, cols].reshape(512, 128))
            return carry
        lax.fori_loop(0, 8, body, 0)

    def store_part(slot, a, b, val):
        for p in range(3):
            n_rows = PART_ROWS[p]
            for xi in range(4):
                for zi in range(2):
                    start = PART_BASE[p] + (xi * 2 + zi) * n_rows
                    parts[slot][p][a, b, xi, zi] = val[start : start + n_rows]

    prepared = set()

    def fill(j, slot):
        kind, half = JOB_KIND[j // 2], j % 2
        if kind not in prepared:
            prepared.add(kind)
            if kind == 3:
                transpose_into(hT, hh)
            if kind == 2:
                transpose_into(hT, dm)
            if kind == 1:
                loads["h2"].wait()
                transpose_into(hT, hh)
                loads["h1"] = load(0, r["h1_i"], hh)
            if kind == 0:
                loads["h1"].wait()
                transpose_into(hT, hh)
                transpose_into(oT, otp)
        rows = pl.ds(half * 512, 512)
        right = {3: dl, 2: u, 1: dl}

        def body(i, carry):
            g = right[kind][i] if kind else r["dq6"][i]
            store_part(slot, i // 4, lax.rem(i, 4), jnp.dot(hT[rows, :], g, preferred_element_type=F32))
            return carry

        lax.fori_loop(0, 8 if kind else 6, body, 0)
        if kind == 0:
            for jj in range(2):
                cols = pl.ds(pl.multiple_of((2 * jj + c) * 256, 256), 256)
                g = da[:, :, cols].reshape(512, 256)
                store_part(slot, 1, 2 + jj, jnp.dot(oT[rows, :], g, preferred_element_type=F32))

    queue = list(range(JOBS))
    running = []
    tails = []
    free = list(range(SLOTS))
    ready = {3}
    used = set()

    steps_done = {}

    def launch():
        if not (queue and free and JOB_KIND[queue[0] // 2] in ready):
            return
        if running and steps_done[running[-1][1]] < 1:
            return
        j = queue.pop(0)
        slot = free.pop(0)
        fill(j, slot)
        gen = phases(j, slot, slot in used, lambda: len(queue) > len(free))
        used.add(slot)
        next(gen)
        steps_done[j] = 0
        running.append((gen, j, slot))

    def service(count=1):
        for _ in range(count):
            old = list(tails)
            for entry in list(running):
                gen, j, slot = entry
                try:
                    next(gen)
                    steps_done[j] += 1
                except StopIteration:
                    running[:] = [e for e in running if e is not entry]
                    free.append(slot)
                    t = tail(j)
                    next(t)
                    tails.append(t)
            launch()
            for gen in old:
                try:
                    next(gen)
                except StopIteration:
                    tails.remove(gen)

    tile[...] = jnp.zeros((8, 128), F32)
    biasp[...] = jnp.zeros((160, 128), F32)
    dmod[...] = jnp.zeros((2, 8, 1024), F32)
    loads["h3"].wait()
    loads["dl"].wait()
    launch()
    loads["h2"] = load(0, r["h2_i"], hh)

    def store_bias(start, val):
        for i in range(val.shape[1] // 128):
            biasp[pl.ds(start + i, 1), :] = val[:, 128 * i : 128 * i + 128]

    def blocks(fn):
        for img in range(2):
            def body(i, carry, img=img):
                fn(img, pl.ds(pl.multiple_of(img * 128 + i * 32, 32), 32))
                return carry
            lax.fori_loop(0, 4, body, 0)

    def exchange(k, ref):
        cp = remote(ref.at[c], ref.at[c], ps.at[k], pr.at[k], mate)
        cp.start()
        return cp

    def swap(k):
        cp = remote(acc.at[1 - c], got, ps.at[k], pr.at[k], mate)
        cp.start()
        return cp

    def back_rows(grad, count):
        def body(i, carry):
            for half in range(2):
                part = lax.dot_general(
                    grad[i, 256 * half : 256 * half + 256, :], wb[i // 4, lax.rem(i, 4)], NT,
                    preferred_element_type=F32,
                )

                @pl.when(i == 0)
                def _():
                    acc[half] = part

                @pl.when(i > 0)
                def _():
                    acc[half] += part

            return carry
        lax.fori_loop(0, count, body, 0)

    def norm_back(img, v, scale, shift, dy):
        center = v - jnp.mean(v, -1, keepdims=True)
        inv = lax.rsqrt(jnp.mean(center * center, -1, keepdims=True) + NORM_EPS)
        unit = center * inv
        dmod[img, scale : scale + 1, :] += jnp.sum(dy * unit, axis=0, keepdims=True)
        dmod[img, shift : shift + 1, :] += jnp.sum(dy, axis=0, keepdims=True)
        dn = dy * (1.0 + ada_row(ada, scale, img))
        return inv * (
            dn - jnp.mean(dn, -1, keepdims=True) - unit * jnp.mean(dn * unit, -1, keepdims=True)
        )

    loads["w3"].wait()
    back_rows(dl, 8)
    cp = swap(0)
    w_next = load(2, r["w_i"].at[:, :, 2], wb)

    def head_bias(i, carry):
        store_bias(128 + (2 * i + c) * 2, jnp.sum(dl[i].astype(F32), axis=0, keepdims=True))
        return carry

    lax.fori_loop(0, 8, head_bias, 0)
    service()
    loads["x2"].wait()
    loads["mlp"].wait()
    cp.wait()
    fc2_rows = jnp.zeros((1, 1024), F32)

    def do_x2(img, rows):
        grad = norm_back(img, xa[rows, :], 6, 7, acc[c, rows, :] + got[rows, :])
        dx[rows, :] = grad
        dmod[img, 1:2, :] += jnp.sum(grad * xb[rows, :], axis=0, keepdims=True)
        low = (ada_row(ada, 1, img) * grad).astype(BF16)
        dm[c, rows, :] = low
        r["gst"][0, 0:1, :] += jnp.sum(low.astype(F32), axis=0, keepdims=True)

    r["gst"][0, 0:1, :] = fc2_rows
    blocks(do_x2)
    cp = exchange(1, dm)
    store_bias(120, r["gst"][0, 0:1, :])
    loads["x1"] = load(3, r["x1_i"], xa)
    loads["att"] = load(4, r["att_i"], xb)
    cp.wait()
    loads["u"].wait()
    ready.add(2)
    service()
    w_next.wait()

    fb = r["fb"]

    def f_load(i):
        return pltpu.make_async_copy(r["f_i"].at[i], fb.at[lax.rem(i, 2)], fs.at[lax.rem(i, 2)])

    f_load(0).start()

    def do_df(i, carry):
        @pl.when(i < 7)
        def _():
            f_load(i + 1).start()

        du = jnp.dot(dm[...].reshape(512, 1024), wb[i // 4, lax.rem(i, 4)], preferred_element_type=F32)
        f_load(i).wait()
        v = fb[lax.rem(i, 2)]
        k0 = 0.7978845608028654
        th = jnp.tanh(k0 * (v + 0.044715 * (v * v * v)))
        slope = 0.5 * (1.0 + th) + 0.5 * v * (1.0 - th * th) * (k0 * (1.0 + 3.0 * 0.044715 * (v * v)))
        df = (slope * du).astype(BF16)
        dl[i] = df
        store_bias(88 + (2 * i + c) * 2, jnp.sum(df.astype(F32), axis=0, keepdims=True))
        return carry

    while 1 in queue:
        service()
    lax.fori_loop(0, 8, do_df, 0)
    ready.add(1)
    w_next = load(2, r["w_i"].at[:, :, 1], wb)
    service()
    w_next.wait()
    back_rows(dl, 8)
    cp = swap(2)
    w_next = load(2, r["wo_i"], wb.at[0])
    loads["x1"].wait()
    loads["att"].wait()
    loads["ot"].wait()
    ot_swap = exchange(3, otp)
    service()
    cp.wait()

    def do_x1(img, rows):
        grad = norm_back(img, xa[rows, :], 3, 5, acc[c, rows, :] + got[rows, :]) + dx[rows, :]
        dmod[img, 0:1, :] += jnp.sum(grad * xb[rows, :], axis=0, keepdims=True)
        low = (ada_row(ada, 0, img) * grad).astype(BF16)
        da[c, rows, :] = low
        r["gst"][0, 0:1, :] += jnp.sum(low.astype(F32), axis=0, keepdims=True)

    r["gst"][0, 0:1, :] = fc2_rows
    blocks(do_x1)
    da_swap = exchange(4, da)
    store_bias(80, r["gst"][0, 0:1, :])
    w_next.wait()
    dov, doh, hb = r["dov"], r["doh"], r["hb"]
    for img in range(2):
        rows = pl.ds(128 * img, 128)
        low = jnp.zeros((128, 1024), F32)
        for k in range(4):
            low += lax.dot_general(
                da[c, rows, 256 * k : 256 * k + 256], wb[0, k], NT, preferred_element_type=F32
            )
        dov[img] = low.astype(BF16)
    w_next = load(2, r["w_i"].at[:, :, 0], wb)

    def do_sends(fn):
        for p in range(4):
            for q in range(2):
                src = dov.at[:, :, pl.ds(((p // 2 * 2 + q) * 2 + p % 2) * 128, 128)]
                cp = remote(src, doh.at[sq], hs.at[p, q], hr.at[sq], (base + q, p * 2 + c))

                @pl.when(jnp.logical_not(jnp.logical_and(sq == p * 2 + c, c == q)))
                def _():
                    fn(cp)

    do_sends(lambda cp: cp.start())

    @pl.when(owner == c)
    def _():
        doh[sq] = dov[:, :, head_lanes(pair, c)]

    kcol = r["kcol"]
    for img in range(2):
        for g in range(8):
            kcol[img, g] = column_of(slots_all[g * 2 + owner, pl.ds(img, 1), :])
    service()
    for i in range(8):
        landed = doh.at[i]

        @pl.when(jnp.logical_or(sq != i, owner != c))
        def _():
            remote(landed, landed, hs.at[0, 0], hr.at[i], mate).wait_recv()

    loads["hb"].wait()
    dkv, dsrc, dr, dq6 = r["dkv"], r["dsrc"], r["dr"], r["dq6"]
    low_lanes = lax.broadcasted_iota(jnp.int32, (256, 128), 1) < 64
    low_rows = lax.broadcasted_iota(jnp.int32, (128, 256), 0) < 64

    for img in range(2):
        dkv[...] = jnp.zeros((2, 1024, 128), F32)

        def attend_block(qb, carry, img=img):
            q = jnp.concatenate([hb[2 * qb, 0, img], hb[2 * qb + 1, 0, img]], axis=0)
            k = jnp.concatenate([hb[g, 1, img] for g in range(8)], axis=0)
            v = jnp.concatenate([hb[g, 2, img] for g in range(8)], axis=0)
            do = jnp.concatenate([doh[2 * qb, img], doh[2 * qb + 1, img]], axis=0)
            kT = jnp.transpose(k)
            key = jnp.concatenate([kcol[img, g] for g in range(8)], axis=0)[:, 0:1]
            query = jnp.concatenate(
                [slots_all[(2 * qb + i) * 2 + owner, 2 + img : 3 + img, :] for i in range(2)], axis=1
            )
            seen_by = key <= query
            heads = []
            for h in range(2):
                mask = low_lanes if h == 0 else jnp.logical_not(low_lanes)
                qh = jnp.where(mask, q, jnp.zeros_like(q))
                doh_h = jnp.where(mask, do, jnp.zeros_like(do))
                sc = lax.dot_general(k, qh, NT, preferred_element_type=F32) * SCORE_SCALE
                sc = jnp.where(seen_by, sc, -1e30)
                e = jnp.exp(sc - jnp.max(sc, axis=0, keepdims=True))
                p = e / jnp.sum(e, axis=0, keepdims=True)
                dpr = lax.dot_general(v, doh_h, NT, preferred_element_type=F32)
                inner = jnp.sum(p * dpr, axis=0, keepdims=True)
                ds = (p * (dpr - inner)).astype(BF16)
                dkv[0] += jnp.dot(ds, qh, preferred_element_type=F32)
                dkv[1] += jnp.dot(p.astype(BF16), doh_h, preferred_element_type=F32)
                heads.append(jnp.dot(kT, ds, preferred_element_type=F32))
            dq = jnp.transpose(jnp.where(low_rows, heads[0], heads[1]) * SCORE_SCALE).astype(BF16)
            dsrc[2 * qb, 0, img] = dq[:128]
            dsrc[2 * qb + 1, 0, img] = dq[128:]
            return carry

        lax.fori_loop(0, 4, attend_block, 0)
        for g in range(8):
            dsrc[g, 1, img] = (dkv[0, 128 * g : 128 * g + 128] * SCORE_SCALE).astype(BF16)
            dsrc[g, 2, img] = dkv[1, 128 * g : 128 * g + 128].astype(BF16)
        if img == 0:
            service()
    sends = []
    for i, to in enumerate(line):
        cp = remote(dsrc.at[to], dr.at[sq], as_.at[i], ar.at[i], (dp, to))
        cp.start()
        sends.append(cp)
    dr[sq] = dsrc[sq]
    service(2)
    for cp in sends:
        cp.wait()
    for t in range(3):
        for jj in range(2):
            for half in range(2):
                for ip in range(2):
                    dq6[t * 2 + jj, ip * 256 : ip * 256 + 256, half * 128 : half * 128 + 128] = dr[
                        (jj * 2 + half) * 2 + ip, t
                    ].reshape(256, 128)
    for jj in range(2):
        for start, t in ((64, 0), (72, 2)):
            store_bias(
                start + (2 * jj + c) * 2,
                jnp.sum(dq6[t * 2 + jj].astype(F32), axis=0, keepdims=True),
            )
    w_next.wait()
    back_rows(dq6, 6)
    cp = swap(5)
    ot_swap.wait()
    da_swap.wait()
    ready.add(0)
    service()
    cp.wait()

    def do_x0(img, rows):
        norm_back(img, r["x_in"][rows, :].astype(F32), 2, 4, acc[c, rows, :] + got[rows, :])

    blocks(do_x0)
    do_sends(lambda cp: cp.wait_send())

    smsg, sgot, smine = r["smsg"], r["sgot"], r["smine"]
    sall, spart, sback = r["sall"], r["spart"], r["sback"]
    for k in range(8):
        both = dmod[0, k : k + 1, :] + dmod[1, k : k + 1, :]
        for i in range(8):
            biasp[8 * k + i : 8 * k + i + 1, :] = both[:, 128 * i : 128 * i + 128]
    for d in range(16):
        for img in range(2):
            for i in range(4):
                lo = (d % 2) * 512 + i * 128
                smsg[d, img * 4 + i : img * 4 + i + 1, :] = dmod[img, d // 2 : d // 2 + 1, lo : lo + 128]
        smsg[d, 8:18, :] = biasp[10 * d : 10 * d + 10, :]
        smsg[d, 18:24, :] = jnp.broadcast_to(r["loss"][0:1, :], (6, 128))
    cps = []
    for i, d in enumerate(row):
        cp = remote(smsg.at[d], sgot.at[dp], s1.at[i], r1.at[i], (d, sq))
        cp.start()
        cps.append(cp)
    sgot[dp] = smsg[dp]
    service()
    for cp in cps:
        cp.wait()
    for d in range(16):
        smine[d] = sgot[d, 0:8, :]
    for i in range(2):
        smine[16 + i] = sum(sgot[d, 8 + 8 * i : 16 + 8 * i, :] for d in range(16))
    cps = []
    for i, s in enumerate(line):
        cp = remote(smine, sall.at[sq], s2.at[i], r2.at[i], (dp, s))
        cp.start()
        cps.append(cp)
    sall[sq] = smine[...]
    service()
    for cp in cps:
        cp.wait()
    for k in range(18):
        smine[k] = sum(sall[s, k] for s in range(8))
    r["bias_sum"][0] = smine[16]
    r["bias_sum"][1] = smine[17]
    dada = jnp.concatenate(
        [
            jnp.concatenate([smine[d, 4 * i + k : 4 * i + k + 1, :] for k in range(4)], axis=1)
            for d in range(16)
            for i in range(2)
        ],
        axis=0,
    )

    def dcond_part(d, carry):
        rows = pl.ds(pl.multiple_of(64 * d, 64), 64)
        spart[d] = lax.dot_general(
            dada, r["cond_w"][rows, :].astype(F32), NT, precision=HIGH, preferred_element_type=F32
        )
        return carry

    lax.fori_loop(0, 16, dcond_part, 0)
    cps = []
    for i, d in enumerate(row):
        cp = remote(spart.at[d], sback.at[dp], s3.at[i], r3.at[i], (d, sq))
        cp.start()
        cps.append(cp)
    sback[dp] = spart[dp]
    service()
    squares = jnp.zeros((8, 128), F32)

    def fold(val):
        total = jnp.zeros((8, 128), F32)
        for i in range(val.shape[0] // 8):
            for k in range(val.shape[1] // 128):
                total = total + val[8 * i : 8 * i + 8, 128 * k : 128 * k + 128]
        return total

    gcs = r["gcs"]

    def gcond_copy(d):
        slot = lax.rem(d, 2)
        rows = pl.ds(pl.multiple_of(64 * d, 64), 64)
        return pltpu.make_async_copy(gcs.at[slot], r["gcond"].at[rows], gl.at[slot])

    def gcond_part(d, total):
        @pl.when(d > 1)
        def _():
            gcond_copy(d - 2).wait()

        val = lax.dot_general(
            r["cond_all"][d].astype(F32), dada, (((0,), (0,)), ((), ())),
            precision=HIGH, preferred_element_type=F32,
        )
        gcs[lax.rem(d, 2)] = val
        gcond_copy(d).start()
        return total + fold(val * val)

    squares = squares + lax.fori_loop(0, 16, gcond_part, squares)
    gcond_copy(14).wait()
    gcond_copy(15).wait()
    for cp in cps:
        cp.wait()
    dcond = sum(sback[d] for d in range(16))
    emb = r["emb"][...]
    sig = 1.0 / (1.0 + jnp.exp(-emb))
    demb = dcond * (sig * (1.0 + emb * (1.0 - sig)))
    labels = jnp.concatenate(
        [msg_all[d, 10:11, i : i + 1] for d in range(16) for i in range(2)], axis=0
    ).astype(jnp.int32)
    hit = jnp.where(lax.broadcasted_iota(jnp.int32, (32, 1000), 1) == labels, 1.0, 0.0)
    gtable = jnp.dot(jnp.transpose(demb), hit, precision=HIGH, preferred_element_type=F32)
    r["gtable"][...] = gtable
    table_squares = jnp.sum(jnp.sum(gtable * gtable, axis=1, keepdims=True), axis=0, keepdims=True)
    bias_rows = jnp.concatenate([smine[16], smine[17][0:2]], axis=0)
    bias_squares = jnp.sum(jnp.sum(bias_rows * bias_rows, axis=1, keepdims=True), axis=0, keepdims=True)
    spot = jnp.logical_and(
        lax.broadcasted_iota(jnp.int32, (8, 128), 0) == 0, lax.broadcasted_iota(jnp.int32, (8, 128), 1) == 0
    )
    squares = squares + jnp.where(spot, table_squares + bias_squares, 0.0)
    while queue or running:
        service()
    tile[...] += squares * 0.125
    tiles = r["tiles"]
    cps = []
    for i, d in enumerate(row):
        cp = remote(tile, tiles.at[i], ns.at[i], nr.at[i], (d, sq))
        cp.start()
        cps.append(cp)
    for cp in cps:
        cp.wait()
    tile[...] += sum(tiles[i] for i in range(15))
    cps = []
    for i, d in enumerate(line):
        cp = remote(tile, tiles.at[15 + i], ns.at[15 + i], nr.at[15 + i], (dp, d))
        cp.start()
        cps.append(cp)
    service()
    for cp in cps:
        cp.wait()
    r["norm"][...] = tile[...] + sum(tiles[15 + i] for i in range(7))
    while tails:
        service()
    for cp in unsent:
        cp.wait_send()


def backward_pass(small, kept):
    dma = pltpu.SemaphoreType.DMA
    sd = jax.ShapeDtypeStruct
    vm = pltpu.VMEM
    scratch = [
        vm((2, 4, 1024, 256), BF16),
        vm((8, 512, 256), BF16), vm((8, 512, 256), BF16), vm((2, 512, 256), F32),
        vm((2, 256, 1024), BF16), vm((1024, 512), BF16), vm((1024, 512), BF16),
        vm((2, 256, 1024), BF16), vm((2, 256, 1024), BF16), vm((2, 256, 1024), BF16),
        vm((2, 256, 1024), F32), vm((256, 1024), F32), vm((256, 1024), F32), vm((256, 1024), F32),
        vm((256, 1024), F32),
        vm((8, 3, 2, 128, 128), BF16), vm((8, 2, 128, 128), BF16), vm((2, 128, 1024), BF16),
        vm((2, 1024, 128), F32), vm((8, 3, 2, 128, 128), BF16), vm((8, 3, 2, 128, 128), BF16),
        vm((6, 512, 256), BF16), vm((2, 8, 128, 128), F32), vm((2, 8, 1024), F32), vm((160, 128), F32),
        vm((16, 24, 128), F32), vm((16, 24, 128), F32), vm((18, 8, 128), F32), vm((8, 18, 8, 128), F32),
        vm((16, 32, 64), F32), vm((16, 32, 64), F32), vm((1, 8, 1024), F32),
        vm((2, 64, 512), F32),
        vm((8, 128), F32), vm((22, 8, 128), F32),
    ]
    for _ in range(SLOTS):
        for p in range(3):
            scratch.append(vm((2, 4, 4, 2, PART_ROWS[p], 256), F32))
    for p in range(3):
        scratch.append(vm((JOBS, PART_ROWS[p], 256), F32))
    scratch += [vm(shape, F32) for shape in recv_shapes()]
    scratch += [
        dma((9,)), dma((2,)), dma((6,)), dma((6,)), dma((4, 2)), dma((8,)), dma, dma((7,)), dma((7,)),
        dma((JOBS, 9, 4)), dma((JOBS, 9, 4)), dma((JOBS, 3, 5)), dma((JOBS, 3, 5)), dma((JOBS, 3)),
        pltpu.SemaphoreType.REGULAR((SLOTS,)),
        dma((15,)), dma((15,)), dma((7,)), dma((7,)), dma((15,)), dma((15,)), dma((22,)), dma((22,)),
        dma((2,)),
    ]
    return pl.pallas_call(
        backward_kernel,
        out_shape=[
            sd((4, 1024, 256), F32), sd((8, 128), F32), sd((2, 8, 128), F32),
            sd((64, 1000), F32), sd((1024, 512), F32),
        ],
        in_specs=[VM] * len(small) + [ANY] * len(kept),
        out_specs=[ANY, VM, VM, VM, ANY],
        scratch_shapes=scratch,
        compiler_params=params(1, 64 * 2**20 - 2**17),
    )(*small, *kept)


def adamw(weight, first, second, grad, factor):
    clipped = grad * factor
    first_new = BETA_ONE * first + (1.0 - BETA_ONE) * clipped
    second_new = BETA_TWO * second + (1.0 - BETA_TWO) * clipped * clipped
    first_hat = first_new / (1.0 - BETA_ONE**STEP)
    second_hat = second_new / (1.0 - BETA_TWO**STEP)
    weight_new = weight - LEARN * (first_hat / (jnp.sqrt(second_hat) + ADAM_EPS) + DECAY * weight)
    return (weight_new, first_new, second_new)


def local(
    x_in, scale_ids, pad_mask, loss_weights, targets, labels,
    cond_w, attn_w, mlp_w, head_w, class_table, biases,
    first_cond, first_attn, first_mlp, first_head, first_table, first_bias,
    second_cond, second_attn, second_mlp, second_head, second_table, second_bias,
):
    wb_cond = cond_w.astype(BF16)
    shard = jnp.stack([attn_w, mlp_w[0], mlp_w[1], head_w]).astype(BF16)

    x_rows = x_in.reshape(256, 1024)
    count_part = jnp.sum(pad_mask.astype(F32))
    row = jnp.concatenate([labels.astype(F32), count_part[None], jnp.zeros((125,), F32)])
    rounded = lax.reduce_precision(biases, 8, 7).reshape(10, 128)
    msg = jnp.concatenate([rounded, row[None], jnp.zeros((5, 128), F32)])
    level = jnp.where(pad_mask > 0, scale_ids, 1000).astype(F32)
    weight_own = (loss_weights * pad_mask).astype(F32)
    slots = jnp.concatenate(
        [level, scale_ids.astype(F32), targets.astype(F32), weight_own, jnp.zeros((8, 128), F32)]
    )
    (
        msg_all, slots_all, cond_all, embedded, ada, loss_tile,
        w, wo, h1, h2, h3, heads, o, att, x1, mlp, x2, f, u, dlogits,
    ) = forward_pass(msg, slots, class_table.T.astype(BF16), wb_cond, x_rows, shard)
    true_count = jnp.sum(slots_all.reshape(8, 2, 16, 128)[:, 0, 8, 0])
    summed, squares, bias_sum, grad_table, grad_cond = backward_pass(
        (msg_all, slots_all, cond_all, embedded, ada, loss_tile, wb_cond, x_rows),
        (w, wo, h1, h2, h3, heads, o, att, x1, mlp, x2, f, u, dlogits),
    )
    bias_sum = bias_sum.reshape(16, 128)
    loss_total = bias_sum[10, 0]
    grad_bias = bias_sum[:10].reshape(1280)
    grad_norm = jnp.sqrt(jnp.sum(squares))
    factor = jnp.minimum(1.0, CLIP / grad_norm)
    grads = (grad_cond, summed[0], summed[1:3], summed[3], grad_table, grad_bias)
    weights = (cond_w, attn_w, mlp_w, head_w, class_table.T, biases)
    firsts = (first_cond, first_attn, first_mlp, first_head, first_table.T, first_bias)
    seconds = (second_cond, second_attn, second_mlp, second_head, second_table.T, second_bias)
    results = [
        adamw(weight, first, second, grad, factor)
        for weight, first, second, grad in zip(weights, firsts, seconds, grads)
    ]
    new_weights = [entry[0] for entry in results]
    new_first = [entry[1] for entry in results]
    new_second = [entry[2] for entry in results]
    copies = [weight.astype(BF16) for weight in new_weights]
    for group in (new_weights, new_first, new_second, copies):
        group[4] = group[4].T
    return tuple(new_weights + new_first + new_second + copies + [grad_norm, loss_total, true_count])


def solution(mesh):
    split = (P(None, "dp"), P(None, "dp"), P(None, None, "dp"), P(None, "dp"), P(None, "dp"), P("dp"))
    in_specs = (P("dp", "seq", None),) + (P("dp", "seq"),) * 4 + (P("dp"),) + split * 3
    out_specs = split * 4 + (P(), P(), P())
    return jax.shard_map(local, mesh=mesh, in_specs=in_specs, out_specs=out_specs, check_vma=False)
```

time: 758 us -> 439 us (0.58)
  Pallas kernels: 488 us -> 391 us
  local copies, waits for them, and re-layouts: 102 us -> 6.05 us
  matrix products: 86.9 us -> 0 us
  other arithmetic: 68.7 us -> 31.2 us
    dot_general x16 -> x0, matrix products: 75.7 us -> none  [the longest x4 20.2 us: weight_grad(): return jnp.einsum('td,jtk->jdk', h, g, preferred_element_type=F32)]
    pallas_call x9 -> x1, Pallas kernels: 305 us -> 242 us  [backward_pass(): pl.pallas_call(backward_kernel, out_shape=[sd((4, 1024, 256), F32), sd((8...]
    transpose x9 -> x0, local copies, waits for them, and re-layouts: 34 us -> none  [the longest x3 27.7 us: weight_grad(): return jnp.einsum('td,jtk->jdk', h, g, preferred_element_type=F32)]
    pallas_call x1, Pallas kernels: 183 us -> 149 us  [forward_pass(): pl.pallas_call(forward_kernel, out_shape=[sd((16, 16, 128), F32), sd((16,...]
    convert_element_type x4 -> x1, other arithmetic: 19.7 us -> 0.67 us  [local(): class_table.T.astype(BF16)]
    reshape x17 -> x0, local copies, waits for them, and re-layouts: 16.7 us -> none  [the longest x2 4.11 us: local(): att, x1, mlp, x2 = (a.reshape(2, 128, 1024) for a in (att, x1, mlp, x2))]
    mul x6 -> x0, local copies, waits for them, and re-layouts: 11.3 us -> none  [the longest x4 7.51 us: modulate(): return layer_norm(values) * (1.0 + scale_row) + shift_row]
    sub x1 -> x0, matrix products: 11.2 us -> none  [local(): probs = jax.nn.softmax(jnp.where(visible, scores, -1e+30), axis=-1)]
where the time goes in v3:
time: 439 us; the launch traced here: 432 us
  Pallas kernels  391 us (89%)
  other arithmetic  31.2 us (7%)
  local copies, waits for them, and re-layouts  6.05 us (1%)
    pallas_call x1, Pallas kernels, backward_pass(): pl.pallas_call(backward_kernel, out_shape=[sd((4, 1024, 256), F32), sd((8...  242 us
    pallas_call x1, Pallas kernels, forward_pass(): pl.pallas_call(forward_kernel, out_shape=[sd((16, 16, 128), F32), sd((16,...  149 us
    convert_element_type x4, other arithmetic, local(): copies = [weight.astype(BF16) for weight in new_weights]  17.6 us

profile of v3, /device:TPU:1, one launch (start us, length us, event | category | flops | bytes accessed | tf_op | source)
XLA Modules:
  0.0 431.5 jit_solution(17566844543976413819)
XLA Ops:
  0.7 0.0 copy-start
  0.7 0.9 multiply_convert_fusion
  1.6 0.7 convert_element_type.47
  2.2 1.2 concatenate.11.slots
  3.4 1.6 convert_bitcast_fusion
  5.1 0.0 copy-done
  5.1 0.1 convert.12
  5.2 0.0 copy-start.1
  5.2 1.6 pad_maximum_fusion.s
  6.8 0.8 copy-done.1
  7.6 0.0 copy-start.13
  7.6 0.0 copy-start.14
  7.6 0.0 copy-start.17
  7.6 0.0 copy-start.18
  7.6 1.1 convert_element_type.50.cond_w.refs_6_
  8.7 0.0 copy-done.13
  8.7 0.7 bitcast_convert_fusion.table
  9.4 0.0 copy-done.14
  9.4 0.0 copy-done.17
  9.4 0.6 convert_reduce_fusion
  10.0 0.0 copy-done.18
  10.0 0.7 maximum_bitcast_fusion
  10.7 0.1 pad.5.clone
  10.8 0.7 maximum_maximum_fusion.msg
  11.4 149.2 %shard_map.439 = (f32[16,16,128]{2,1,0:T(8,128)}, f32[16,16,128]{2,1,0:T(8,128)}, bf16[16,32,64]{2,1,0:T(8,128)(2,1)}, f32[32,64]{1,0:T(8,128)}, f32[16,2,512]{2...) custom-call(f32[16,128]{1,0:T(8,128)} %maximum_maximum_fusion.msg, ...), custom_call_target="tpu_custom_call" | custom-call | tf_op jit(solution)/shard_map/pallas_call | solution.py:528
  160.7 0.0 copy-start.15
  160.7 0.0 copy-start.16
  160.7 241.9 %shard_map.440 = (f32[4,1024,256]{2,1,0:T(8,128)}, f32[8,128]{1,0:T(8,128)}, f32[2,8,128]{2,1,0:T(8,128)}, f32[64,1000]{1,0:T(8,128)}, f32[1024,512]{1,0:T(8,128)}) custom-call(f32[16,16,128]{2,1,0:T(8,128)} %get-tuple-element.52.refs_0_, f32[16,16,128]{2,1,0:T(8,128)} %get-tuple-element.53.refs_1_, bf16[16,32,64]{2,1,0:T(8,128)(2,1)} %get-tuple-element.54.refs_2_, ...), custom_call_target="tpu_custom_call" | custom-call | tf_op jit(solution)/shard_map/pallas_call | solution.py:1339
  402.6 1.3 reduce_sum.28
  404.6 0.0 copy-done.15
  404.6 0.0 copy-done.16
  404.6 1.3 fusion.12
  405.9 2.3 convert_bitcast_fusion.2
  408.2 0.0 copy-start.3
  408.2 0.0 copy-start.4
  408.2 0.0 copy-start.5
  408.2 0.0 copy-start.9
  408.3 0.0 copy-start.10
  408.3 0.0 copy-start.11
  408.3 0.0 copy-start.12
  408.3 8.0 %fusion.16 = (bf16[2,1024,256]{2,1,0:T(8,128)(2,1)}, f32[2,1024,256]{2,1,0:T(8,128)}, f32[2,1024,256]{2,1,0:T(8,128)}, f32[2,1024,256]{2,1,0:T(8,128)}) fusion(f32[2,1024,256]{2,1,0:T(8,128)} %param.32, f32[]{:T(128)S(6)} %min_shard_map.3, f32[4,1024,256]{2,1,0:T(8,128)} %get-tuple-element.74, f32[2,1024,256]{2,1,0:T(8,128)} %param.38, f32[2,1024,256]{2,1,0:T(8,128)} %param.44), kind=kLoop, calls=%fused_computation.49 | loop fusion | flops 8388608 | bytes 15728644 | tf_op jit(solution)/shard_map/convert_element_type | solution.py:1406
  416.3 0.0 copy-done.3
  416.3 0.0 copy-done.4
  416.3 0.0 copy-done.5
  416.3 0.0 copy-done.9
  416.3 0.0 copy-done.10
  416.3 0.0 copy-done.11
  416.4 0.8 copy-done.12
  417.1 0.0 copy-start.2
  417.1 0.0 copy-start.6
  417.1 0.0 copy-start.7
  417.1 0.0 copy-start.8
  417.1 4.1 fusion.14
  421.2 0.0 copy-done.2
  421.2 0.1 copy-done.6
  421.3 1.2 copy-done.7
  422.6 0.6 copy-done.8
  423.2 4.2 fusion.20
  427.4 1.2 slice.28
  428.6 1.4 slice_reduce_fusion
  (5 shorter events, 0.0 us)
Async XLA Ops:
  0.7 4.4 %copy-start = (f32[2,1024,256]{2,1,0:T(8,128)S(1)}, f32[2,1024,256]{2,1,0:T(8,128)}, u32[]{:S(2)}) copy-start(f32[2,1024,256]{2,1,0:T(8,128)} %param.32) | copy-start | bytes 6291460
  5.2 2.4 copy-start.1
  7.6 1.1 copy-start.13
  7.6 1.8 copy-start.14
  7.6 1.8 copy-start.17
  7.6 2.4 copy-start.18
  160.7 243.9 %copy-start.15 = (f32[1280]{0:T(1024)S(1)}, f32[1280]{0:T(1024)}, u32[]{:S(2)}) copy-start(f32[1280]{0:T(1024)} %param.41) | copy-start | bytes 15364
  160.7 243.9 %copy-start.16 = (f32[1280]{0:T(1024)S(1)}, f32[1280]{0:T(1024)}, u32[]{:S(2)}) copy-start(f32[1280]{0:T(1024)} %param.47) | copy-start | bytes 15364
  408.2 8.1 %copy-start.3 = (f32[4,1024,256]{2,1,0:T(8,128)S(1)}, f32[4,1024,256]{2,1,0:T(8,128)}, u32[]{:S(2)}) copy-start(f32[4,1024,256]{2,1,0:T(8,128)} %get-tuple-element.74) | copy-start | bytes 12582916
  408.2 8.1 %copy-start.4 = (f32[1024,256]{1,0:T(8,128)S(1)}, f32[1024,256]{1,0:T(8,128)}, u32[]{:S(2)}) copy-start(f32[1024,256]{1,0:T(8,128)} %param.33) | copy-start | bytes 3145732
  408.2 8.1 %copy-start.5 = (f32[1024,256]{1,0:T(8,128)S(1)}, f32[1024,256]{1,0:T(8,128)}, u32[]{:S(2)}) copy-start(f32[1024,256]{1,0:T(8,128)} %param.31) | copy-start | bytes 3145732
  408.2 8.1 %copy-start.9 = (f32[1024,256]{1,0:T(8,128)S(1)}, f32[1024,256]{1,0:T(8,128)}, u32[]{:S(2)}) copy-start(f32[1024,256]{1,0:T(8,128)} %param.39) | copy-start | bytes 3145732
  408.3 8.1 %copy-start.10 = (f32[1024,256]{1,0:T(8,128)S(1)}, f32[1024,256]{1,0:T(8,128)}, u32[]{:S(2)}) copy-start(f32[1024,256]{1,0:T(8,128)} %param.45) | copy-start | bytes 3145732
  408.3 8.1 %copy-start.11 = (f32[1024,256]{1,0:T(8,128)S(1)}, f32[1024,256]{1,0:T(8,128)}, u32[]{:S(2)}) copy-start(f32[1024,256]{1,0:T(8,128)} %param.43) | copy-start | bytes 3145732
  408.3 8.8 %copy-start.12 = (f32[1024,256]{1,0:T(8,128)S(1)}, f32[1024,256]{1,0:T(8,128)}, u32[]{:S(2)}) copy-start(f32[1024,256]{1,0:T(8,128)} %param.37) | copy-start | bytes 3145732
  417.1 4.1 copy-start.2
  417.1 4.2 copy-start.6
  417.1 5.4 %copy-start.7 = (f32[1024,512]{1,0:T(8,128)S(1)}, f32[1024,512]{1,0:T(8,128)}, u32[]{:S(2)}) copy-start(f32[1024,512]{1,0:T(8,128)} %param.42) | copy-start | bytes 6291460
  417.1 6.0 %copy-start.8 = (f32[1024,512]{1,0:T(8,128)S(1)}, f32[1024,512]{1,0:T(8,128)}, u32[]{:S(2)}) copy-start(f32[1024,512]{1,0:T(8,128)} %get-tuple-element.72) | copy-start | bytes 6291460

commit v4 on v3

--- a/solution.py
+++ b/solution.py
@@ -94,8 +94,8 @@
 
 
 def forward_kernel(
-    msg, slots, table, cond_w, x_in, s,
-    msg_all, slots_all, cond_all, emb_out, ada, loss_out,
+    msg, slots, table, cond_w, x_in, attn_in, mlp_in, head_in,
+    msg_all, slots_all, cond_all, emb_out, ada, loss_out, cond_low,
     w_o, wo_o, h1_o, h2_o, h3_o, hb_o, ot_o, att_o, x1_o, mlp_o, x2_o, f_o, u_o, dl_o,
     w, wo, h1, h2, h3, src, hb, oh, ot, att, x1, mlp, x2, acc, got_acc, f, u, dl,
     cond_own, ada_own, bias, qcol, tcol, wcol, stats,
@@ -114,6 +114,12 @@
     base = dp - c
     row = [(lax.rem(dp + i, 16), sq) for i in range(1, 16)]
     group = group_peers()
+    incoming = []
+    for j in range(8):
+        rows = pl.ds(512 * (j % 2), 512)
+        source = (attn_in, mlp_in.at[0], mlp_in.at[1], head_in)[j // 2]
+        incoming.append(pltpu.make_async_copy(source.at[rows], f.at[j], gl.at[j, 0]))
+        incoming[-1].start()
     greet(row + group[1:] + [at(x, y, z + 2 * zl - 1, c)])
 
     pending = []
@@ -145,19 +151,15 @@
         m = j // 2
         full, first = rows_at(j, 0, ROWS_YZ), rows_at(j, 0, HALF_YZ)
         second, mine = rows_at(j, HALF_YZ, HALF_YZ), quarter(j, x)
-        own = []
-        if kind in "AB":
-            for i, rows in enumerate((full, mine)):
-                own.append(pltpu.make_async_copy(s.at[m, rows], w.at[zl, y, m, rows], gl.at[j, i]))
         if kind == "A":
-            go(j, 0, s.at[m, full], w.at[zl, y, m, full], yp)
-            go(j, 1, s.at[m, full], w.at[zl, y, m, full], ym)
-            go(j, 6, s.at[m, mine], w.at[zl, y, m, mine], zs)
-            for cp in own:
-                cp.start()
+            incoming[j].wait()
+            w[zl, y, m, full, :] = f[j, 0:ROWS_YZ, :].astype(BF16)
+            at_rows = pl.ds(pl.multiple_of(ROWS_YZ + QUARTER * x, 16), QUARTER)
+            w[zl, y, m, mine, :] = f[j, at_rows, :].astype(BF16)
+            go(j, 0, w.at[zl, y, m, full], w.at[zl, y, m, full], yp)
+            go(j, 1, w.at[zl, y, m, full], w.at[zl, y, m, full], ym)
+            go(j, 6, w.at[zl, y, m, mine], w.at[zl, y, m, mine], zs)
         if kind == "B":
-            for cp in own:
-                cp.wait()
             got(j, 6, w.at[1 - zl, y, m, mine])
             go(j, 7, w.at[:, y, m, mine], w.at[:, y, m, mine], yp)
             go(j, 8, w.at[:, y, m, mine], w.at[:, y, m, mine], ym)
@@ -199,10 +201,10 @@
                     pltpu.make_async_copy(w.at[1, 2 + i, 0], wo.at[2 * i + c], gl.at[i, 2]).start()
 
     wave = [
-        ["A0"], ["A1"], ["B0", "A2"], ["B1", "C0", "A3"],
-        ["C1", "D0", "B2", "A4"], ["D1", "E0", "C2", "B3", "A5"], ["E1", "F0", "D2", "C3", "B4"], ["F1"],
-        ["E2", "D3", "C4", "B5", "A6"],
-        ["F2", "E3", "D4", "C5", "B6", "A7"], ["F3", "E4", "D5", "C6", "B7"], ["F4", "E5", "D6", "C7"],
+        ["A0", "A1"], ["B0", "B1", "A2"], ["C0", "C1", "B2", "D0", "D1", "A3"],
+        ["E0", "E1", "C2", "B3", "A4"], ["F0", "F1"], ["D2", "C3", "B4", "A5"],
+        ["E2", "D3", "C4", "B5", "A6"], ["F2", "E3", "D4", "C5", "B6", "A7"],
+        ["F3", "E4", "D5", "C6", "B7"], ["F4", "E5", "D6", "C7"],
         ["F5", "E6", "D7"], ["F6", "E7"], ["F7"],
     ]
 
@@ -236,7 +238,7 @@
     lane = lax.broadcasted_iota(jnp.int32, (32, classes), 1)
     labels = jnp.concatenate([seen[d, 10:11, i : i + 1] for d in range(16) for i in range(2)], axis=0)
     hit = jnp.where(lane == labels.astype(jnp.int32), 1.0, 0.0).astype(BF16)
-    emb = lax.dot_general(hit, table[...], NT, preferred_element_type=F32)
+    emb = lax.dot_general(hit, table[...].astype(BF16), NT, preferred_element_type=F32)
     emb_out[...] = emb
     cond_own[...] = (emb / (1.0 + jnp.exp(-emb))).astype(BF16)
     cond_all[dp] = cond_own[...]
@@ -250,7 +252,9 @@
         cp.wait()
     total = jnp.zeros((32, 512), F32)
     for d in range(16):
-        total += jnp.dot(cond_all[d], cond_w[pl.ds(64 * d, 64), :], preferred_element_type=F32)
+        low = cond_w[pl.ds(64 * d, 64), :].astype(BF16)
+        cond_low[pl.ds(64 * d, 64), :] = low
+        total += jnp.dot(cond_all[d], low, preferred_element_type=F32)
     total += jnp.concatenate([bias[pl.ds(dp * 4 + i, 1), :] for i in range(4)], axis=1)
     for d in range(16):
         ada_own[d] = total[2 * d : 2 * d + 2]
@@ -302,7 +306,7 @@
     pump()
     cp.wait()
     keep(4, h1, h1_o)
-    pump(4)
+    pump()
 
     def bias_row(start):
         return jnp.concatenate([bias[pl.ds(start, 1), :], bias[pl.ds(start + 1, 1), :]], axis=1)
@@ -319,17 +323,17 @@
                 src[(jj * 2 + half) * 2 + ip, t] = val[
                     ip * 256 : ip * 256 + 256, half * 128 : half * 128 + 128
                 ].reshape(2, 128, 128)
-    cps = []
-    for i in range(1, 8):
-        to = lax.rem(sq + i, 8)
-        cp = remote(src.at[to], hb.at[sq], as_.at[i], ar.at[i], (dp, to))
-        cp.start()
-        cps.append(cp)
+    cps = [[], []]
+    for img in range(2):
+        for i in range(1, 8):
+            to = lax.rem(sq + i, 8)
+            cp = remote(
+                src.at[to, :, img], hb.at[sq, :, img], as_.at[i, img], ar.at[i, img], (dp, to)
+            )
+            cp.start()
+            cps[img].append(cp)
     hb[sq] = src[sq]
     pump()
-    for cp in cps:
-        cp.wait()
-    keep(5, hb, hb_o)
 
     low_lanes = lax.broadcasted_iota(jnp.int32, (256, 128), 1) < 64
 
@@ -355,10 +359,6 @@
         oh[2 * qb + 1, img] = o[128:]
         return carry
 
-    for i in range(0, 8, 2):
-        lax.fori_loop(i, i + 2, attend_block, 0)
-        if i < 6:
-            pump()
     pair = sq // 2
     lanes = head_lanes(pair, c)
 
@@ -370,6 +370,11 @@
         )
 
     for img in range(2):
+        for cp in cps[img]:
+            cp.wait()
+        lax.fori_loop(4 * img, 4 * img + 2, attend_block, 0)
+        pump()
+        lax.fori_loop(4 * img + 2, 4 * img + 4, attend_block, 0)
         for i in range(1, 8):
             o_copy(i, img).start()
 
@@ -381,7 +386,8 @@
         def _():
             o_copy(0, img).start()
 
-    pump()
+        pump()
+    keep(5, hb, hb_o)
     for img in range(2):
         for p in range(4):
             for q in range(2):
@@ -452,6 +458,7 @@
 
     blocks(do_h3)
     cp = exchange(3, h3)
+    pump()
     keep(13, mlp, mlp_o)
     keep(14, x2, x2_o)
     f_copy.wait()
@@ -491,6 +498,7 @@
     weight = wcol[:, 0:1]
     losses = weight * (log_total - (both[0][:, 2:3] + both[1][:, 2:3]))
     loss_out[...] = jnp.broadcast_to(0.5 * jnp.sum(losses, axis=0, keepdims=True), (8, 128))
+    loss_out[7:8, :] = jnp.broadcast_to(true_count, (1, 128))
     share = weight / true_count
 
     def do_dlogits(j, carry):
@@ -514,7 +522,7 @@
         cp.wait()
 
 
-def forward_pass(msg, slots, table, cond_w, x_rows, shard):
+def forward_pass(msg, slots, table, cond_w, x_rows, matrices):
     dma = pltpu.SemaphoreType.DMA
     sd = jax.ShapeDtypeStruct
     kept = [
@@ -529,10 +537,10 @@
         forward_kernel,
         out_shape=[
             sd((16, 16, 128), F32), sd((16, 16, 128), F32), sd((16, 32, 64), BF16),
-            sd((32, 64), F32), sd((16, 2, 512), F32), sd((8, 128), F32),
+            sd((32, 64), F32), sd((16, 2, 512), F32), sd((8, 128), F32), sd((1024, 512), BF16),
         ] + kept,
-        in_specs=[VM] * 5 + [ANY],
-        out_specs=[VM] * 6 + [ANY] * len(kept),
+        in_specs=[VM] * 5 + [ANY] * 3,
+        out_specs=[VM] * 7 + [ANY] * len(kept),
         scratch_shapes=[
             vm((2, 4, 4, 1024, 256), BF16), vm((4, 1024, 256), BF16),
             vm((2, 256, 1024), BF16), vm((2, 256, 1024), BF16), vm((2, 256, 1024), BF16),
@@ -545,11 +553,11 @@
             vm((2, 8, 128, 128), F32), vm((512, 128), F32), vm((512, 128), F32), vm((2, 512, 128), F32),
             dma((8, 15)), dma((8, 15)), dma((8, 3)), dma((2,)), dma((2,)),
             dma((15,)), dma((15,)), dma((15,)), dma((15,)), dma((15,)), dma((15,)), dma((15,)), dma((15,)),
-            dma((5,)), dma((5,)), dma((8,)), dma((8,)), dma,
+            dma((5,)), dma((5,)), dma((8, 2)), dma((8, 2)), dma,
             dma((8, 2)), dma((4, 2, 2)), dma, dma((17,)),
         ],
         compiler_params=params(0, 63 * 2**20),
-    )(msg, slots, table, cond_w, x_rows, shard)
+    )(msg, slots, table, cond_w, x_rows, *matrices)
 
 
 PART_ROWS = (16, 24, 24)
@@ -820,22 +828,25 @@
 
     prepared = set()
 
+    def prepare(kind):
+        if kind in prepared:
+            return
+        prepared.add(kind)
+        if kind == 3:
+            transpose_into(hT, hh)
+        if kind == 2:
+            transpose_into(hT, dm)
+        if kind == 1:
+            loads["h2"].wait()
+            transpose_into(hT, hh)
+            loads["h1"] = load(0, r["h1_i"], hh)
+        if kind == 0:
+            loads["h1"].wait()
+            transpose_into(hT, hh)
+
     def fill(j, slot):
         kind, half = JOB_KIND[j // 2], j % 2
-        if kind not in prepared:
-            prepared.add(kind)
-            if kind == 3:
-                transpose_into(hT, hh)
-            if kind == 2:
-                transpose_into(hT, dm)
-            if kind == 1:
-                loads["h2"].wait()
-                transpose_into(hT, hh)
-                loads["h1"] = load(0, r["h1_i"], hh)
-            if kind == 0:
-                loads["h1"].wait()
-                transpose_into(hT, hh)
-                transpose_into(oT, otp)
+        prepare(kind)
         rows = pl.ds(half * 512, 512)
         right = {3: dl, 2: u, 1: dl}
 
@@ -1053,17 +1064,20 @@
         dov[img] = low.astype(BF16)
     w_next = load(2, r["w_i"].at[:, :, 0], wb)
 
-    def do_sends(fn):
+    def do_sends(fn, img):
         for p in range(4):
             for q in range(2):
-                src = dov.at[:, :, pl.ds(((p // 2 * 2 + q) * 2 + p % 2) * 128, 128)]
-                cp = remote(src, doh.at[sq], hs.at[p, q], hr.at[sq], (base + q, p * 2 + c))
+                src = dov.at[img, :, pl.ds(((p // 2 * 2 + q) * 2 + p % 2) * 128, 128)]
+                cp = remote(
+                    src, doh.at[sq, img], hs.at[p, q, img], hr.at[sq, img], (base + q, p * 2 + c)
+                )
 
                 @pl.when(jnp.logical_not(jnp.logical_and(sq == p * 2 + c, c == q)))
                 def _():
                     fn(cp)
 
-    do_sends(lambda cp: cp.start())
+    for img in range(2):
+        do_sends(lambda cp: cp.start(), img)
 
     @pl.when(owner == c)
     def _():
@@ -1074,19 +1088,23 @@
         for g in range(8):
             kcol[img, g] = column_of(slots_all[g * 2 + owner, pl.ds(img, 1), :])
     service()
-    for i in range(8):
-        landed = doh.at[i]
-
-        @pl.when(jnp.logical_or(sq != i, owner != c))
-        def _():
-            remote(landed, landed, hs.at[0, 0], hr.at[i], mate).wait_recv()
+    ot_swap.wait()
+    transpose_into(oT, otp)
 
     loads["hb"].wait()
     dkv, dsrc, dr, dq6 = r["dkv"], r["dsrc"], r["dr"], r["dq6"]
     low_lanes = lax.broadcasted_iota(jnp.int32, (256, 128), 1) < 64
     low_rows = lax.broadcasted_iota(jnp.int32, (128, 256), 0) < 64
 
+    sends = []
     for img in range(2):
+        for i in range(8):
+            landed = doh.at[i, img]
+
+            @pl.when(jnp.logical_or(sq != i, owner != c))
+            def _():
+                remote(landed, landed, hs.at[0, 0, img], hr.at[i, img], mate).wait_recv()
+
         dkv[...] = jnp.zeros((2, 1024, 128), F32)
 
         def attend_block(qb, carry, img=img):
@@ -1124,15 +1142,19 @@
         for g in range(8):
             dsrc[g, 1, img] = (dkv[0, 128 * g : 128 * g + 128] * SCORE_SCALE).astype(BF16)
             dsrc[g, 2, img] = dkv[1, 128 * g : 128 * g + 128].astype(BF16)
+        for i, to in enumerate(line):
+            cp = remote(
+                dsrc.at[to, :, img], dr.at[sq, :, img], as_.at[i, img], ar.at[i, img], (dp, to)
+            )
+            cp.start()
+            sends.append(cp)
         if img == 0:
             service()
-    sends = []
-    for i, to in enumerate(line):
-        cp = remote(dsrc.at[to], dr.at[sq], as_.at[i], ar.at[i], (dp, to))
-        cp.start()
-        sends.append(cp)
     dr[sq] = dsrc[sq]
-    service(2)
+    service(1)
+    if queue[0] >= 6:
+        prepare(0)
+    service(1)
     for cp in sends:
         cp.wait()
     for t in range(3):
@@ -1142,6 +1164,7 @@
                     dq6[t * 2 + jj, ip * 256 : ip * 256 + 256, half * 128 : half * 128 + 128] = dr[
                         (jj * 2 + half) * 2 + ip, t
                     ].reshape(256, 128)
+    da_swap.wait()
     for jj in range(2):
         for start, t in ((64, 0), (72, 2)):
             store_bias(
@@ -1151,8 +1174,6 @@
     w_next.wait()
     back_rows(dq6, 6)
     cp = swap(5)
-    ot_swap.wait()
-    da_swap.wait()
     ready.add(0)
     service()
     cp.wait()
@@ -1161,7 +1182,8 @@
         norm_back(img, r["x_in"][rows, :].astype(F32), 2, 4, acc[c, rows, :] + got[rows, :])
 
     blocks(do_x0)
-    do_sends(lambda cp: cp.wait_send())
+    for img in range(2):
+        do_sends(lambda cp: cp.wait_send(), img)
 
     smsg, sgot, smine = r["smsg"], r["sgot"], r["smine"]
     sall, spart, sback = r["sall"], r["spart"], r["sback"]
@@ -1297,7 +1319,9 @@
     service()
     for cp in cps:
         cp.wait()
-    r["norm"][...] = tile[...] + sum(tiles[15 + i] for i in range(7))
+    total = tile[...] + sum(tiles[15 + i] for i in range(7))
+    total = jnp.sum(jnp.sum(total, axis=1, keepdims=True), axis=0, keepdims=True)
+    r["norm"][...] = jnp.broadcast_to(total, (8, 128))
     while tails:
         service()
     for cp in unsent:
@@ -1330,7 +1354,7 @@
         scratch.append(vm((JOBS, PART_ROWS[p], 256), F32))
     scratch += [vm(shape, F32) for shape in recv_shapes()]
     scratch += [
-        dma((9,)), dma((2,)), dma((6,)), dma((6,)), dma((4, 2)), dma((8,)), dma, dma((7,)), dma((7,)),
+        dma((9,)), dma((2,)), dma((6,)), dma((6,)), dma((4, 2, 2)), dma((8, 2)), dma, dma((7, 2)), dma((7, 2)),
         dma((JOBS, 9, 4)), dma((JOBS, 9, 4)), dma((JOBS, 3, 5)), dma((JOBS, 3, 5)), dma((JOBS, 3)),
         pltpu.SemaphoreType.REGULAR((SLOTS,)),
         dma((15,)), dma((15,)), dma((7,)), dma((7,)), dma((15,)), dma((15,)), dma((22,)), dma((22,)),
@@ -1365,8 +1389,6 @@
     first_cond, first_attn, first_mlp, first_head, first_table, first_bias,
     second_cond, second_attn, second_mlp, second_head, second_table, second_bias,
 ):
-    wb_cond = cond_w.astype(BF16)
-    shard = jnp.stack([attn_w, mlp_w[0], mlp_w[1], head_w]).astype(BF16)
 
     x_rows = x_in.reshape(256, 1024)
     count_part = jnp.sum(pad_mask.astype(F32))
@@ -1379,10 +1401,10 @@
         [level, scale_ids.astype(F32), targets.astype(F32), weight_own, jnp.zeros((8, 128), F32)]
     )
     (
-        msg_all, slots_all, cond_all, embedded, ada, loss_tile,
+        msg_all, slots_all, cond_all, embedded, ada, loss_tile, wb_cond,
         w, wo, h1, h2, h3, heads, o, att, x1, mlp, x2, f, u, dlogits,
-    ) = forward_pass(msg, slots, class_table.T.astype(BF16), wb_cond, x_rows, shard)
-    true_count = jnp.sum(slots_all.reshape(8, 2, 16, 128)[:, 0, 8, 0])
+    ) = forward_pass(msg, slots, class_table.T, cond_w, x_rows, (attn_w, mlp_w, head_w))
+    true_count = loss_tile[7, 0]
     summed, squares, bias_sum, grad_table, grad_cond = backward_pass(
         (msg_all, slots_all, cond_all, embedded, ada, loss_tile, wb_cond, x_rows),
         (w, wo, h1, h2, h3, heads, o, att, x1, mlp, x2, f, u, dlogits),
@@ -1390,7 +1412,7 @@
     bias_sum = bias_sum.reshape(16, 128)
     loss_total = bias_sum[10, 0]
     grad_bias = bias_sum[:10].reshape(1280)
-    grad_norm = jnp.sqrt(jnp.sum(squares))
+    grad_norm = jnp.sqrt(squares[0, 0])
     factor = jnp.minimum(1.0, CLIP / grad_norm)
     grads = (grad_cond, summed[0], summed[1:3], summed[3], grad_table, grad_bias)
     weights = (cond_w, attn_w, mlp_w, head_w, class_table.T, biases)

time: 439 us -> 421 us (0.959)
  Pallas kernels: 391 us -> 378 us
  other arithmetic: 31.2 us -> 25.4 us
    pallas_call x1, Pallas kernels: 242 us -> 234 us  [backward_pass(): pl.pallas_call(backward_kernel, out_shape=[sd((4, 1024, 256), F32), sd((8...]
    pallas_call x1, Pallas kernels: 149 us -> 144 us  [forward_pass(): pl.pallas_call(forward_kernel, out_shape=[sd((16, 16, 128), F32), sd((16,...]
where the time goes in v4:
time: 421 us; the launch traced here: 414 us
  Pallas kernels  378 us (90%)
  other arithmetic  25.4 us (6%)
  local copies, waits for them, and re-layouts  7.62 us (2%)
    pallas_call x1, Pallas kernels, backward_pass(): pl.pallas_call(backward_kernel, out_shape=[sd((4, 1024, 256), F32), sd((8...  234 us
    pallas_call x1, Pallas kernels, forward_pass(): pl.pallas_call(forward_kernel, out_shape=[sd((16, 16, 128), F32), sd((16,...  144 us
    convert_element_type x4, other arithmetic, local(): copies = [weight.astype(BF16) for weight in new_weights]  17.6 us

profile of v4, /device:TPU:1, one launch (start us, length us, event | category | flops | bytes accessed | tf_op | source)
XLA Modules:
  0.0 413.9 jit_solution(6673580689233572918)
XLA Ops:
  0.7 0.8 multiply_convert_fusion
  1.4 0.7 convert_element_type.40
  2.1 1.2 concatenate.11.slots
  3.3 0.7 reduce-precision_bitcast_fusion
  4.0 1.3 convert_reduce_fusion
  5.3 0.7 convert_element_type.36
  6.0 0.7 maximum_bitcast_fusion
  6.7 0.1 pad.2.clone
  6.8 0.7 maximum_maximum_fusion.msg
  7.4 143.7 %shard_map.439 = (f32[16,16,128]{2,1,0:T(8,128)}, f32[16,16,128]{2,1,0:T(8,128)}, bf16[16,32,64]{2,1,0:T(8,128)(2,1)}, f32[32,64]{1,0:T(8,128)}, f32[16,2,512]{2...) custom-call(f32[16,128]{1,0:T(8,128)} %maximum_maximum_fusion.msg, ...), custom_call_target="tpu_custom_call" | custom-call | tf_op jit(solution)/shard_map/pallas_call | solution.py:536
  151.2 0.0 copy-start.11
  151.2 0.0 copy-start.12
  151.2 0.0 copy-start.13
  151.2 234.1 %shard_map.440 = (f32[4,1024,256]{2,1,0:T(8,128)}, f32[8,128]{1,0:T(8,128)}, f32[2,8,128]{2,1,0:T(8,128)}, f32[64,1000]{1,0:T(8,128)}, f32[1024,512]{1,0:T(8,128)}) custom-call(f32[16,16,128]{2,1,0:T(8,128)} %get-tuple-element.53.refs_0_, f32[16,16,128]{2,1,0:T(8,128)} %get-tuple-element.54.refs_1_, bf16[16,32,64]{2,1,0:T(8,128)(2,1)} %get-tuple-element.55.refs_2_, ...), custom_call_target="tpu_custom_call" | custom-call | tf_op jit(solution)/shard_map/pallas_call | solution.py:1363
  385.3 1.2 slice.21
  387.2 0.0 copy-done.11
  387.2 0.0 copy-done.12
  387.2 0.0 copy-done.13
  387.2 1.3 fusion.10
  388.6 2.3 convert_bitcast_fusion
  390.9 0.0 copy-start.1
  390.9 0.0 copy-start.2
  390.9 0.0 copy-start.3
  390.9 0.0 copy-start.7
  390.9 0.0 copy-start.8
  390.9 0.0 copy-start.9
  390.9 0.0 copy-start.10
  390.9 8.0 %fusion.14 = (bf16[2,1024,256]{2,1,0:T(8,128)(2,1)}, f32[2,1024,256]{2,1,0:T(8,128)}, f32[2,1024,256]{2,1,0:T(8,128)}, f32[2,1024,256]{2,1,0:T(8,128)}) fusion(f32[2,1024,256]{2,1,0:T(8,128)} %mlp_in.1, f32[]{:T(128)S(6)} %min_shard_map.3, f32[4,1024,256]{2,1,0:T(8,128)} %get-tuple-element.76, f32[2,1024,256]{2,1,0:T(8,128)} %param.38, f32[2,1024,256]{2,1,0:T(8,128)} %param.44), kind=kLoop, calls=%fused_computation.41 | loop fusion | flops 8388608 | bytes 15728644 | tf_op jit(solution)/shard_map/convert_element_type | solution.py:1428
  398.9 0.0 copy-done.1
  398.9 0.0 copy-done.2
  398.9 0.0 copy-done.3
  399.0 0.0 copy-done.7
  399.0 0.0 copy-done.8
  399.0 0.0 copy-done.9
  399.0 0.8 copy-done.10
  399.7 0.0 copy-start
  399.8 0.0 copy-start.4
  399.8 0.0 copy-start.5
  399.8 0.0 copy-start.6
  399.8 4.1 fusion.12
  403.8 0.0 copy-done
  403.8 0.1 copy-done.4
  404.0 1.2 copy-done.5
  405.2 0.6 copy-done.6
  405.8 4.2 %fusion.18 = (bf16[1024,512]{1,0:T(8,128)(2,1)}, f32[1024,512]{1,0:T(8,128)}, f32[1024,512]{1,0:T(8,128)}, f32[1024,512]{1,0:T(8,128)}) fusion(f32[1024,512]{1,0:T(8,128)S(1)} %copy-done, f32[1024,512]{1,0:T(8,128)S(1)} %copy-done.6, f32[]{:T(128)S(6)} %min_shard_map.3, f32[1024,512]{1,0:T(8,128)S(1)} %copy-done.4, f32[1024,512]{1,0:T(8,128)S(1)} %copy-done.5), kind=kLoop, calls=%fused_computation.43 | loop fusion | flops 8388608 | bytes 15728644 | tf_op jit(solution)/shard_map/convert_element_type | solution.py:1428
  410.0 1.2 slice.29
  411.2 1.2 slice.27
  (3 shorter events, 0.0 us)
Async XLA Ops:
  151.2 236.0 %copy-start.11 = (f32[1280]{0:T(1024)S(1)}, f32[1280]{0:T(1024)}, u32[]{:S(2)}) copy-start(f32[1280]{0:T(1024)} %param.35) | copy-start | bytes 15364
  151.2 236.0 %copy-start.12 = (f32[1280]{0:T(1024)S(1)}, f32[1280]{0:T(1024)}, u32[]{:S(2)}) copy-start(f32[1280]{0:T(1024)} %param.41) | copy-start | bytes 15364
  151.2 236.0 %copy-start.13 = (f32[1280]{0:T(1024)S(1)}, f32[1280]{0:T(1024)}, u32[]{:S(2)}) copy-start(f32[1280]{0:T(1024)} %param.47) | copy-start | bytes 15364
  390.9 8.1 %copy-start.1 = (f32[4,1024,256]{2,1,0:T(8,128)S(1)}, f32[4,1024,256]{2,1,0:T(8,128)}, u32[]{:S(2)}) copy-start(f32[4,1024,256]{2,1,0:T(8,128)} %get-tuple-element.76) | copy-start | bytes 12582916
  390.9 8.1 %copy-start.2 = (f32[1024,256]{1,0:T(8,128)S(1)}, f32[1024,256]{1,0:T(8,128)}, u32[]{:S(2)}) copy-start(f32[1024,256]{1,0:T(8,128)} %attn_in.1) | copy-start | bytes 3145732
  390.9 8.1 %copy-start.3 = (f32[1024,256]{1,0:T(8,128)S(1)}, f32[1024,256]{1,0:T(8,128)}, u32[]{:S(2)}) copy-start(f32[1024,256]{1,0:T(8,128)} %head_in.1) | copy-start | bytes 3145732
  390.9 8.1 %copy-start.7 = (f32[1024,256]{1,0:T(8,128)S(1)}, f32[1024,256]{1,0:T(8,128)}, u32[]{:S(2)}) copy-start(f32[1024,256]{1,0:T(8,128)} %param.39) | copy-start | bytes 3145732
  390.9 8.1 %copy-start.8 = (f32[1024,256]{1,0:T(8,128)S(1)}, f32[1024,256]{1,0:T(8,128)}, u32[]{:S(2)}) copy-start(f32[1024,256]{1,0:T(8,128)} %param.45) | copy-start | bytes 3145732
  390.9 8.1 %copy-start.9 = (f32[1024,256]{1,0:T(8,128)S(1)}, f32[1024,256]{1,0:T(8,128)}, u32[]{:S(2)}) copy-start(f32[1024,256]{1,0:T(8,128)} %param.43) | copy-start | bytes 3145732
  390.9 8.8 %copy-start.10 = (f32[1024,256]{1,0:T(8,128)S(1)}, f32[1024,256]{1,0:T(8,128)}, u32[]{:S(2)}) copy-start(f32[1024,256]{1,0:T(8,128)} %param.37) | copy-start | bytes 3145732
  399.7 4.1 copy-start
  399.8 4.2 %copy-start.4 = (f32[1024,512]{1,0:T(8,128)S(1)}, f32[1024,512]{1,0:T(8,128)}, u32[]{:S(2)}) copy-start(f32[1024,512]{1,0:T(8,128)} %param.36) | copy-start | bytes 6291460
  399.8 5.4 %copy-start.5 = (f32[1024,512]{1,0:T(8,128)S(1)}, f32[1024,512]{1,0:T(8,128)}, u32[]{:S(2)}) copy-start(f32[1024,512]{1,0:T(8,128)} %param.42) | copy-start | bytes 6291460
  399.8 6.0 %copy-start.6 = (f32[1024,512]{1,0:T(8,128)S(1)}, f32[1024,512]{1,0:T(8,128)}, u32[]{:S(2)}) copy-start(f32[1024,512]{1,0:T(8,128)} %get-tuple-element.74) | copy-start | bytes 6291460

commit v5 on v4

--- a/solution.py
+++ b/solution.py
@@ -94,10 +94,10 @@
 
 
 def forward_kernel(
-    msg, slots, table, cond_w, x_in, attn_in, mlp_in, head_in,
+    labels_in, bias_in, scale_in, pad_in, weight_in, target_in, table, cond_w, x_in, attn_in, mlp_in, head_in,
     msg_all, slots_all, cond_all, emb_out, ada, loss_out, cond_low,
     w_o, wo_o, h1_o, h2_o, h3_o, hb_o, ot_o, att_o, x1_o, mlp_o, x2_o, f_o, u_o, dl_o,
-    w, wo, h1, h2, h3, src, hb, oh, ot, att, x1, mlp, x2, acc, got_acc, f, u, dl,
+    msg, slots, w, wo, h1, h2, h3, src, hb, oh, ot, att, x1, mlp, x2, acc, got_acc, f, u, dl,
     cond_own, ada_own, bias, qcol, tcol, wcol, stats,
     gs, gr, gl, os, orr, s1, r1, s2, r2, s3, r3, s4, r4, ps, pr, as_, ar, al, ts, tr, tl, outs_sem,
 ):
@@ -120,6 +120,21 @@
         source = (attn_in, mlp_in.at[0], mlp_in.at[1], head_in)[j // 2]
         incoming.append(pltpu.make_async_copy(source.at[rows], f.at[j], gl.at[j, 0]))
         incoming[-1].start()
+    pad = pad_in[...]
+    scale = scale_in[...].astype(F32)
+    slots[...] = jnp.zeros((16, 128), F32)
+    slots[0:2, :] = jnp.where(pad > 0, scale, 1000.0)
+    slots[2:4, :] = scale
+    slots[4:6, :] = target_in[...].astype(F32)
+    slots[6:8, :] = (weight_in[...] * pad).astype(F32)
+    real = jnp.sum(jnp.sum(pad.astype(F32), axis=1, keepdims=True), axis=0, keepdims=True)
+    spot = lax.broadcasted_iota(jnp.int32, (1, 128), 1)
+    label = labels_in[...].astype(F32)
+    msg[...] = jnp.zeros((16, 128), F32)
+    msg[0:10, :] = bias_in[...].astype(BF16).astype(F32)
+    msg[10:11, :] = jnp.where(
+        spot == 0, label[:, 0:1], jnp.where(spot == 1, label[:, 1:2], jnp.where(spot == 2, real, 0.0))
+    )
     greet(row + group[1:] + [at(x, y, z + 2 * zl - 1, c)])
 
     pending = []
@@ -522,7 +537,7 @@
         cp.wait()
 
 
-def forward_pass(msg, slots, table, cond_w, x_rows, matrices):
+def forward_pass(small, matrices):
     dma = pltpu.SemaphoreType.DMA
     sd = jax.ShapeDtypeStruct
     kept = [
@@ -539,9 +554,10 @@
             sd((16, 16, 128), F32), sd((16, 16, 128), F32), sd((16, 32, 64), BF16),
             sd((32, 64), F32), sd((16, 2, 512), F32), sd((8, 128), F32), sd((1024, 512), BF16),
         ] + kept,
-        in_specs=[VM] * 5 + [ANY] * 3,
+        in_specs=[VM] * len(small) + [ANY] * 3,
         out_specs=[VM] * 7 + [ANY] * len(kept),
         scratch_shapes=[
+            vm((16, 128), F32), vm((16, 128), F32),
             vm((2, 4, 4, 1024, 256), BF16), vm((4, 1024, 256), BF16),
             vm((2, 256, 1024), BF16), vm((2, 256, 1024), BF16), vm((2, 256, 1024), BF16),
             vm((8, 3, 2, 128, 128), BF16), vm((8, 3, 2, 128, 128), BF16), vm((8, 2, 128, 128), BF16),
@@ -557,12 +573,12 @@
             dma((8, 2)), dma((4, 2, 2)), dma, dma((17,)),
         ],
         compiler_params=params(0, 63 * 2**20),
-    )(msg, slots, table, cond_w, x_rows, *matrices)
+    )(*small, *matrices)
 
 
 PART_ROWS = (16, 24, 24)
 PART_BASE = (0, 128, 320)
-ORDERS = ("xyz", "yzx", "zxy")
+ORDERS = (("xyz", "yzx", "zxy"), ("xyz", "yxz", "zyx"))
 SLOTS = 3
 JOBS = 8
 
@@ -579,8 +595,8 @@
     return ("r", slice(0, cut), slice(cut, rows))
 
 
-def block_dims(part, phase):
-    later = ORDERS[part][phase + 1 :]
+def block_dims(order, part, phase):
+    later = order[phase + 1 :]
     return {
         "zl": 2 if "z" in later else 1,
         "y": 4 if "y" in later else 1,
@@ -590,17 +606,25 @@
     }
 
 
+def recv_plan():
+    for kind in range(2):
+        for p in range(3):
+            for ph in range(3):
+                if kind == 0 or (p > 0 and ph == 1):
+                    yield kind, p, ph, 4 if ph < 2 else 3
+
+
 def recv_shapes():
     shapes = []
-    for p in range(3):
-        for ph in range(3):
-            name, one, two = block_cut(ORDERS[p], ph, PART_ROWS[p])
-            for k in range(4 if ph < 2 else 3):
-                d = dict(block_dims(p, ph))
-                if ph < 2 and k < 2:
-                    cut = (one, two)[k]
-                    d[name] = cut.stop - cut.start
-                shapes.append((SLOTS, d["zl"], d["y"], d["x"], d["zh"], d["r"], 256))
+    for kind, p, ph, count in recv_plan():
+        order = ORDERS[kind][p]
+        name, one, two = block_cut(order, ph, PART_ROWS[p])
+        for k in range(count):
+            d = dict(block_dims(order, p, ph))
+            if ph < 2 and k < 2:
+                cut = (one, two)[k]
+                d[name] = cut.stop - cut.start
+            shapes.append((SLOTS, d["zl"], d["y"], d["x"], d["zh"], d["r"], 256))
     return shapes
 
 
@@ -618,11 +642,9 @@
     r = dict(zip(names, refs[:n]))
     rest = list(refs[n:])
     recv = {}
-    for p in range(3):
-        for ph in range(3):
-            count = 4 if ph < 2 else 3
-            recv[p, ph] = rest[:count]
-            rest = rest[count:]
+    for kind, p, ph, count in recv_plan():
+        recv[kind, p, ph] = rest[:count]
+        rest = rest[count:]
     (
         ls, fs, ps, pr, hs, hr, hl, as_, ar, js, jr, gss, grs, ol, credit,
         s1, r1, s2, r2, s3, r3, ns, nr, gl,
@@ -669,8 +691,7 @@
         "ot": load(8, r["ot_i"], otp.at[c]),
     }
 
-    def view(ref, p, ph, index, half=None):
-        order = ORDERS[p]
+    def view(ref, order, p, ph, index, half=None):
         sel = {}
         for i, a in enumerate(order):
             sel[a] = here[a] if i < ph else (lax.rem(index + 4, 4) if i == ph else None)
@@ -709,6 +730,7 @@
 
     def phases(j, slot, again, reused):
         mine = []
+        kind = j % 2
         if again:
             pl.semaphore_wait(credit.at[slot], 6)
 
@@ -723,34 +745,37 @@
         for ph in range(3):
             info = []
             for p in range(3):
-                a = ORDERS[p][ph]
-                info.append((p, a, here[a], parts[slot][p], [b.at[slot] for b in recv[p, ph]]))
+                order = ORDERS[kind][p]
+                a = order[ph]
+                buffers = recv.get((kind, p, ph), recv[0, p, ph])
+                bufs = [b.at[slot] for b in buffers]
+                info.append((p, a, here[a], functools.partial(view, parts[slot][p], order, p, ph), bufs))
             if ph == 2:
                 for p, a, i, g, bufs in info:
                     for k, by in enumerate((1, -1, 2)):
-                        go(p, ph, k, view(g, p, ph, i + by), bufs[k], step(a, by))
+                        go(p, ph, k, g(i + by), bufs[k], step(a, by))
                 yield
                 for p, a, i, g, bufs in info:
                     for k in range(3):
                         arrived(p, ph, k, bufs[k])
-                    add(view(g, p, ph, i), bufs)
+                    add(g(i), bufs)
                 break
             for p, a, i, g, bufs in info:
-                go(p, ph, 0, view(g, p, ph, i + 2, 0), bufs[0], step(a, 1))
-                go(p, ph, 1, view(g, p, ph, i + 2, 1), bufs[1], step(a, -1))
+                go(p, ph, 0, g(i + 2, 0), bufs[0], step(a, 1))
+                go(p, ph, 1, g(i + 2, 1), bufs[1], step(a, -1))
             yield
             for p, a, i, g, bufs in info:
                 arrived(p, ph, 0, bufs[0])
-                add(view(g, p, ph, i + 1, 0), [bufs[0]])
-                go(p, ph, 2, view(g, p, ph, i + 1), bufs[2], step(a, 1))
+                add(g(i + 1, 0), [bufs[0]])
+                go(p, ph, 2, g(i + 1), bufs[2], step(a, 1))
                 arrived(p, ph, 1, bufs[1])
-                add(view(g, p, ph, i - 1, 1), [bufs[1]])
-                go(p, ph, 3, view(g, p, ph, i - 1), bufs[3], step(a, -1))
+                add(g(i - 1, 1), [bufs[1]])
+                go(p, ph, 3, g(i - 1), bufs[3], step(a, -1))
             yield
             for p, a, i, g, bufs in info:
                 arrived(p, ph, 2, bufs[2])
                 arrived(p, ph, 3, bufs[3])
-                add(view(g, p, ph, i), [bufs[2], bufs[3]])
+                add(g(i), [bufs[2], bufs[3]])
         for p in range(3):
             val = parts[slot][p][zl, y, x, zh]
             stage_out[p][j] = val
@@ -1391,19 +1416,11 @@
 ):
 
     x_rows = x_in.reshape(256, 1024)
-    count_part = jnp.sum(pad_mask.astype(F32))
-    row = jnp.concatenate([labels.astype(F32), count_part[None], jnp.zeros((125,), F32)])
-    rounded = lax.reduce_precision(biases, 8, 7).reshape(10, 128)
-    msg = jnp.concatenate([rounded, row[None], jnp.zeros((5, 128), F32)])
-    level = jnp.where(pad_mask > 0, scale_ids, 1000).astype(F32)
-    weight_own = (loss_weights * pad_mask).astype(F32)
-    slots = jnp.concatenate(
-        [level, scale_ids.astype(F32), targets.astype(F32), weight_own, jnp.zeros((8, 128), F32)]
-    )
+    small = (labels.reshape(1, 2), biases.reshape(10, 128), scale_ids, pad_mask, loss_weights, targets)
     (
         msg_all, slots_all, cond_all, embedded, ada, loss_tile, wb_cond,
         w, wo, h1, h2, h3, heads, o, att, x1, mlp, x2, f, u, dlogits,
-    ) = forward_pass(msg, slots, class_table.T, cond_w, x_rows, (attn_w, mlp_w, head_w))
+    ) = forward_pass(small + (class_table.T, cond_w, x_rows), (attn_w, mlp_w, head_w))
     true_count = loss_tile[7, 0]
     summed, squares, bias_sum, grad_table, grad_cond = backward_pass(
         (msg_all, slots_all, cond_all, embedded, ada, loss_tile, wb_cond, x_rows),

time: 421 us -> 411 us (0.976)
  other arithmetic: 25.4 us -> 19.9 us
where the time goes in v5:
time: 411 us; the launch traced here: 404 us
  Pallas kernels  374 us (91%)
  other arithmetic  19.9 us (5%)
  local copies, waits for them, and re-layouts  6.35 us (2%)
    pallas_call x1, Pallas kernels, backward_pass(): pl.pallas_call(backward_kernel, out_shape=[sd((4, 1024, 256), F32), sd((8...  230 us
    pallas_call x1, Pallas kernels, forward_pass(): pl.pallas_call(forward_kernel, out_shape=[sd((16, 16, 128), F32), sd((16,...  144 us
    convert_element_type x4, other arithmetic, local(): copies = [weight.astype(BF16) for weight in new_weights]  17.6 us

profile of v5, /device:TPU:1, one launch (start us, length us, event | category | flops | bytes accessed | tf_op | source)
XLA Modules:
  0.0 403.8 jit_solution(17034387467169309024)
XLA Ops:
  0.7 144.4 %shard_map.439 = (f32[16,16,128]{2,1,0:T(8,128)}, f32[16,16,128]{2,1,0:T(8,128)}, bf16[16,32,64]{2,1,0:T(8,128)(2,1)}, f32[32,64]{1,0:T(8,128)}, f32[16,2,512]{2...) custom-call(s32[1,2]{1,0:T(1,128)} %bitcast.56, ...), custom_call_target="tpu_custom_call" | custom-call | tf_op jit(solution)/shard_map/pallas_call | solution.py:551
  145.0 0.0 copy-start.11
  145.0 0.0 copy-start.12
  145.1 0.0 copy-start.13
  145.1 230.1 %shard_map.440 = (f32[4,1024,256]{2,1,0:T(8,128)}, f32[8,128]{1,0:T(8,128)}, f32[2,8,128]{2,1,0:T(8,128)}, f32[64,1000]{1,0:T(8,128)}, f32[1024,512]{1,0:T(8,128)}) custom-call(f32[16,16,128]{2,1,0:T(8,128)} %get-tuple-element.53.refs_0_, f32[16,16,128]{2,1,0:T(8,128)} %get-tuple-element.54.refs_1_, bf16[16,32,64]{2,1,0:T(8,128)(2,1)} %get-tuple-element.55.refs_2_, ...), custom_call_target="tpu_custom_call" | custom-call | tf_op jit(solution)/shard_map/pallas_call | solution.py:1388
  375.2 1.2 slice.21
  377.1 0.0 copy-done.11
  377.1 0.0 copy-done.12
  377.1 0.0 copy-done.13
  377.1 1.3 fusion.9
  378.4 2.3 convert_bitcast_fusion
  380.7 0.0 copy-start.1
  380.7 0.0 copy-start.2
  380.8 0.0 copy-start.3
  380.8 0.0 copy-start.7
  380.8 0.0 copy-start.8
  380.8 0.0 copy-start.9
  380.8 0.0 copy-start.10
  380.8 8.0 %fusion.13 = (bf16[2,1024,256]{2,1,0:T(8,128)(2,1)}, f32[2,1024,256]{2,1,0:T(8,128)}, f32[2,1024,256]{2,1,0:T(8,128)}, f32[2,1024,256]{2,1,0:T(8,128)}) fusion(f32[2,1024,256]{2,1,0:T(8,128)} %mlp_in.1, f32[]{:T(128)S(6)} %min_shard_map.3, f32[4,1024,256]{2,1,0:T(8,128)} %get-tuple-element.76, f32[2,1024,256]{2,1,0:T(8,128)} %param.38, f32[2,1024,256]{2,1,0:T(8,128)} %param.44), kind=kLoop, calls=%fused_computation.34 | loop fusion | flops 8388608 | bytes 15728644 | tf_op jit(solution)/shard_map/convert_element_type | solution.py:1445
  388.8 0.0 copy-done.1
  388.8 0.0 copy-done.2
  388.8 0.0 copy-done.3
  388.8 0.0 copy-done.7
  388.8 0.0 copy-done.8
  388.9 0.0 copy-done.9
  388.9 0.8 copy-done.10
  389.6 0.0 copy-start
  389.6 0.0 copy-start.4
  389.6 0.0 copy-start.5
  389.6 0.0 copy-start.6
  389.6 4.1 %fusion.11 = (bf16[1024,256]{1,0:T(8,128)(2,1)}, f32[1024,256]{1,0:T(8,128)}, f32[1024,256]{1,0:T(8,128)}, f32[1024,256]{1,0:T(8,128)}, bf16[1024,256]{1,0:T(8,1...) fusion(f32[1024,256]{1,0:T(8,128)S(1)} %copy-done.3, f32[]{:T(128)S(6)} %min_shard_map.3, ...), kind=kLoop, calls=%fused_computation.33 | loop fusion | flops 8388608 | bytes 15728644 | tf_op jit(solution)/shard_map/convert_element_type | solution.py:1445
  393.7 0.0 copy-done
  393.7 0.1 copy-done.4
  393.9 1.2 copy-done.5
  395.1 0.6 copy-done.6
  395.7 4.2 %fusion.17 = (bf16[1024,512]{1,0:T(8,128)(2,1)}, f32[1024,512]{1,0:T(8,128)}, f32[1024,512]{1,0:T(8,128)}, f32[1024,512]{1,0:T(8,128)}) fusion(f32[1024,512]{1,0:T(8,128)S(1)} %copy-done, f32[1024,512]{1,0:T(8,128)S(1)} %copy-done.6, f32[]{:T(128)S(6)} %min_shard_map.3, f32[1024,512]{1,0:T(8,128)S(1)} %copy-done.4, f32[1024,512]{1,0:T(8,128)S(1)} %copy-done.5), kind=kLoop, calls=%fused_computation.36 | loop fusion | flops 8388608 | bytes 15728644 | tf_op jit(solution)/shard_map/convert_element_type | solution.py:1445
  399.9 1.2 slice.29
  401.1 1.2 slice.27
Async XLA Ops:
  145.0 232.1 %copy-start.11 = (f32[1280]{0:T(1024)S(1)}, f32[1280]{0:T(1024)}, u32[]{:S(2)}) copy-start(f32[1280]{0:T(1024)} %param.35) | copy-start | bytes 15364
  145.0 232.1 %copy-start.12 = (f32[1280]{0:T(1024)S(1)}, f32[1280]{0:T(1024)}, u32[]{:S(2)}) copy-start(f32[1280]{0:T(1024)} %param.41) | copy-start | bytes 15364
  145.1 232.1 %copy-start.13 = (f32[1280]{0:T(1024)S(1)}, f32[1280]{0:T(1024)}, u32[]{:S(2)}) copy-start(f32[1280]{0:T(1024)} %param.47) | copy-start | bytes 15364
  380.7 8.1 %copy-start.1 = (f32[4,1024,256]{2,1,0:T(8,128)S(1)}, f32[4,1024,256]{2,1,0:T(8,128)}, u32[]{:S(2)}) copy-start(f32[4,1024,256]{2,1,0:T(8,128)} %get-tuple-element.76) | copy-start | bytes 12582916
  380.7 8.1 %copy-start.2 = (f32[1024,256]{1,0:T(8,128)S(1)}, f32[1024,256]{1,0:T(8,128)}, u32[]{:S(2)}) copy-start(f32[1024,256]{1,0:T(8,128)} %attn_in.1) | copy-start | bytes 3145732
  380.8 8.1 %copy-start.3 = (f32[1024,256]{1,0:T(8,128)S(1)}, f32[1024,256]{1,0:T(8,128)}, u32[]{:S(2)}) copy-start(f32[1024,256]{1,0:T(8,128)} %head_in.1) | copy-start | bytes 3145732
  380.8 8.1 %copy-start.7 = (f32[1024,256]{1,0:T(8,128)S(1)}, f32[1024,256]{1,0:T(8,128)}, u32[]{:S(2)}) copy-start(f32[1024,256]{1,0:T(8,128)} %param.39) | copy-start | bytes 3145732
  380.8 8.1 %copy-start.8 = (f32[1024,256]{1,0:T(8,128)S(1)}, f32[1024,256]{1,0:T(8,128)}, u32[]{:S(2)}) copy-start(f32[1024,256]{1,0:T(8,128)} %param.45) | copy-start | bytes 3145732
  380.8 8.1 %copy-start.9 = (f32[1024,256]{1,0:T(8,128)S(1)}, f32[1024,256]{1,0:T(8,128)}, u32[]{:S(2)}) copy-start(f32[1024,256]{1,0:T(8,128)} %param.43) | copy-start | bytes 3145732
  380.8 8.8 %copy-start.10 = (f32[1024,256]{1,0:T(8,128)S(1)}, f32[1024,256]{1,0:T(8,128)}, u32[]{:S(2)}) copy-start(f32[1024,256]{1,0:T(8,128)} %param.37) | copy-start | bytes 3145732
  389.6 4.1 %copy-start = (f32[1024,512]{1,0:T(8,128)S(1)}, f32[1024,512]{1,0:T(8,128)}, u32[]{:S(2)}) copy-start(f32[1024,512]{1,0:T(8,128)} %cond_w.1) | copy-start | bytes 6291460
  389.6 4.2 %copy-start.4 = (f32[1024,512]{1,0:T(8,128)S(1)}, f32[1024,512]{1,0:T(8,128)}, u32[]{:S(2)}) copy-start(f32[1024,512]{1,0:T(8,128)} %param.36) | copy-start | bytes 6291460
  389.6 5.4 %copy-start.5 = (f32[1024,512]{1,0:T(8,128)S(1)}, f32[1024,512]{1,0:T(8,128)}, u32[]{:S(2)}) copy-start(f32[1024,512]{1,0:T(8,128)} %param.42) | copy-start | bytes 6291460
  389.6 6.0 %copy-start.6 = (f32[1024,512]{1,0:T(8,128)S(1)}, f32[1024,512]{1,0:T(8,128)}, u32[]{:S(2)}) copy-start(f32[1024,512]{1,0:T(8,128)} %get-tuple-element.74) | copy-start | bytes 6291460

commit v6 on v5

--- a/solution.py
+++ b/solution.py
@@ -1177,9 +1177,8 @@
             service()
     dr[sq] = dsrc[sq]
     service(1)
-    if queue[0] >= 6:
+    if queue and queue[0] >= 6:
         prepare(0)
-    service(1)
     for cp in sends:
         cp.wait()
     for t in range(3):

time: 411 us -> 412 us (level)
  no operation moved by 1% of the time
where the time goes in v6:
time: 412 us; the launch traced here: 405 us
  Pallas kernels  375 us (91%)
  other arithmetic  19.9 us (5%)
  local copies, waits for them, and re-layouts  6.35 us (2%)
    pallas_call x1, Pallas kernels, backward_pass(): pl.pallas_call(backward_kernel, out_shape=[sd((4, 1024, 256), F32), sd((8...  231 us
    pallas_call x1, Pallas kernels, forward_pass(): pl.pallas_call(forward_kernel, out_shape=[sd((16, 16, 128), F32), sd((16,...  144 us
    convert_element_type x4, other arithmetic, local(): copies = [weight.astype(BF16) for weight in new_weights]  17.6 us

profile of v6, /device:TPU:1, one launch (start us, length us, event | category | flops | bytes accessed | tf_op | source)
XLA Modules:
  0.0 404.5 jit_solution(12162738947057526099)
XLA Ops:
  0.7 144.4 %shard_map.439 = (f32[16,16,128]{2,1,0:T(8,128)}, f32[16,16,128]{2,1,0:T(8,128)}, bf16[16,32,64]{2,1,0:T(8,128)(2,1)}, f32[32,64]{1,0:T(8,128)}, f32[16,2,512]{2...) custom-call(s32[1,2]{1,0:T(1,128)} %bitcast.56, ...), custom_call_target="tpu_custom_call" | custom-call | tf_op jit(solution)/shard_map/pallas_call | solution.py:551
  145.0 0.0 copy-start.11
  145.0 0.0 copy-start.12
  145.1 0.0 copy-start.13
  145.1 230.8 %shard_map.440 = (f32[4,1024,256]{2,1,0:T(8,128)}, f32[8,128]{1,0:T(8,128)}, f32[2,8,128]{2,1,0:T(8,128)}, f32[64,1000]{1,0:T(8,128)}, f32[1024,512]{1,0:T(8,128)}) custom-call(f32[16,16,128]{2,1,0:T(8,128)} %get-tuple-element.53.refs_0_, f32[16,16,128]{2,1,0:T(8,128)} %get-tuple-element.54.refs_1_, bf16[16,32,64]{2,1,0:T(8,128)(2,1)} %get-tuple-element.55.refs_2_, ...), custom_call_target="tpu_custom_call" | custom-call | tf_op jit(solution)/shard_map/pallas_call | solution.py:1387
  375.9 1.2 slice.21
  377.8 0.0 copy-done.11
  377.8 0.0 copy-done.12
  377.8 0.0 copy-done.13
  377.8 1.3 fusion.9
  379.1 2.3 convert_bitcast_fusion
  381.4 0.0 copy-start.1
  381.4 0.0 copy-start.2
  381.4 0.0 copy-start.3
  381.5 0.0 copy-start.7
  381.5 0.0 copy-start.8
  381.5 0.0 copy-start.9
  381.5 0.0 copy-start.10
  381.5 8.0 %fusion.13 = (bf16[2,1024,256]{2,1,0:T(8,128)(2,1)}, f32[2,1024,256]{2,1,0:T(8,128)}, f32[2,1024,256]{2,1,0:T(8,128)}, f32[2,1024,256]{2,1,0:T(8,128)}) fusion(f32[2,1024,256]{2,1,0:T(8,128)} %mlp_in.1, f32[]{:T(128)S(6)} %min_shard_map.3, f32[4,1024,256]{2,1,0:T(8,128)} %get-tuple-element.76, f32[2,1024,256]{2,1,0:T(8,128)} %param.38, f32[2,1024,256]{2,1,0:T(8,128)} %param.44), kind=kLoop, calls=%fused_computation.34 | loop fusion | flops 8388608 | bytes 15728644 | tf_op jit(solution)/shard_map/convert_element_type | solution.py:1444
  389.5 0.0 copy-done.1
  389.5 0.0 copy-done.2
  389.5 0.0 copy-done.3
  389.5 0.0 copy-done.7
  389.5 0.0 copy-done.8
  389.6 0.0 copy-done.9
  389.6 0.8 copy-done.10
  390.3 0.0 copy-start
  390.3 0.0 copy-start.4
  390.3 0.0 copy-start.5
  390.3 0.0 copy-start.6
  390.3 4.1 %fusion.11 = (bf16[1024,256]{1,0:T(8,128)(2,1)}, f32[1024,256]{1,0:T(8,128)}, f32[1024,256]{1,0:T(8,128)}, f32[1024,256]{1,0:T(8,128)}, bf16[1024,256]{1,0:T(8,1...) fusion(f32[1024,256]{1,0:T(8,128)S(1)} %copy-done.3, f32[]{:T(128)S(6)} %min_shard_map.3, ...), kind=kLoop, calls=%fused_computation.33 | loop fusion | flops 8388608 | bytes 15728644 | tf_op jit(solution)/shard_map/convert_element_type | solution.py:1444
  394.4 0.0 copy-done
  394.4 0.1 copy-done.4
  394.5 1.2 copy-done.5
  395.8 0.6 copy-done.6
  396.4 4.2 %fusion.17 = (bf16[1024,512]{1,0:T(8,128)(2,1)}, f32[1024,512]{1,0:T(8,128)}, f32[1024,512]{1,0:T(8,128)}, f32[1024,512]{1,0:T(8,128)}) fusion(f32[1024,512]{1,0:T(8,128)S(1)} %copy-done, f32[1024,512]{1,0:T(8,128)S(1)} %copy-done.6, f32[]{:T(128)S(6)} %min_shard_map.3, f32[1024,512]{1,0:T(8,128)S(1)} %copy-done.4, f32[1024,512]{1,0:T(8,128)S(1)} %copy-done.5), kind=kLoop, calls=%fused_computation.36 | loop fusion | flops 8388608 | bytes 15728644 | tf_op jit(solution)/shard_map/convert_element_type | solution.py:1444
  400.6 1.2 slice.29
  401.8 1.2 slice.27
Async XLA Ops:
  145.0 232.8 %copy-start.11 = (f32[1280]{0:T(1024)S(1)}, f32[1280]{0:T(1024)}, u32[]{:S(2)}) copy-start(f32[1280]{0:T(1024)} %param.35) | copy-start | bytes 15364
  145.0 232.8 %copy-start.12 = (f32[1280]{0:T(1024)S(1)}, f32[1280]{0:T(1024)}, u32[]{:S(2)}) copy-start(f32[1280]{0:T(1024)} %param.41) | copy-start | bytes 15364
  145.1 232.8 %copy-start.13 = (f32[1280]{0:T(1024)S(1)}, f32[1280]{0:T(1024)}, u32[]{:S(2)}) copy-start(f32[1280]{0:T(1024)} %param.47) | copy-start | bytes 15364
  381.4 8.1 %copy-start.1 = (f32[4,1024,256]{2,1,0:T(8,128)S(1)}, f32[4,1024,256]{2,1,0:T(8,128)}, u32[]{:S(2)}) copy-start(f32[4,1024,256]{2,1,0:T(8,128)} %get-tuple-element.76) | copy-start | bytes 12582916
  381.4 8.1 %copy-start.2 = (f32[1024,256]{1,0:T(8,128)S(1)}, f32[1024,256]{1,0:T(8,128)}, u32[]{:S(2)}) copy-start(f32[1024,256]{1,0:T(8,128)} %attn_in.1) | copy-start | bytes 3145732
  381.4 8.1 %copy-start.3 = (f32[1024,256]{1,0:T(8,128)S(1)}, f32[1024,256]{1,0:T(8,128)}, u32[]{:S(2)}) copy-start(f32[1024,256]{1,0:T(8,128)} %head_in.1) | copy-start | bytes 3145732
  381.5 8.1 %copy-start.7 = (f32[1024,256]{1,0:T(8,128)S(1)}, f32[1024,256]{1,0:T(8,128)}, u32[]{:S(2)}) copy-start(f32[1024,256]{1,0:T(8,128)} %param.39) | copy-start | bytes 3145732
  381.5 8.1 %copy-start.8 = (f32[1024,256]{1,0:T(8,128)S(1)}, f32[1024,256]{1,0:T(8,128)}, u32[]{:S(2)}) copy-start(f32[1024,256]{1,0:T(8,128)} %param.45) | copy-start | bytes 3145732
  381.5 8.1 %copy-start.9 = (f32[1024,256]{1,0:T(8,128)S(1)}, f32[1024,256]{1,0:T(8,128)}, u32[]{:S(2)}) copy-start(f32[1024,256]{1,0:T(8,128)} %param.43) | copy-start | bytes 3145732
  381.5 8.8 %copy-start.10 = (f32[1024,256]{1,0:T(8,128)S(1)}, f32[1024,256]{1,0:T(8,128)}, u32[]{:S(2)}) copy-start(f32[1024,256]{1,0:T(8,128)} %param.37) | copy-start | bytes 3145732
  390.3 4.1 %copy-start = (f32[1024,512]{1,0:T(8,128)S(1)}, f32[1024,512]{1,0:T(8,128)}, u32[]{:S(2)}) copy-start(f32[1024,512]{1,0:T(8,128)} %cond_w.1) | copy-start | bytes 6291460
  390.3 4.2 %copy-start.4 = (f32[1024,512]{1,0:T(8,128)S(1)}, f32[1024,512]{1,0:T(8,128)}, u32[]{:S(2)}) copy-start(f32[1024,512]{1,0:T(8,128)} %param.36) | copy-start | bytes 6291460
  390.3 5.4 %copy-start.5 = (f32[1024,512]{1,0:T(8,128)S(1)}, f32[1024,512]{1,0:T(8,128)}, u32[]{:S(2)}) copy-start(f32[1024,512]{1,0:T(8,128)} %param.42) | copy-start | bytes 6291460
  390.3 6.0 %copy-start.6 = (f32[1024,512]{1,0:T(8,128)S(1)}, f32[1024,512]{1,0:T(8,128)}, u32[]{:S(2)}) copy-start(f32[1024,512]{1,0:T(8,128)} %get-tuple-element.74) | copy-start | bytes 6291460
